TPU v7x, 512 devices: a whole 4x4x16 slice. The times are simulated.
512 devices in a mesh: gx: 32 (over z_lo, x), gy: 8 (over y, z_hi), gz: 2 (over core).
Axes of the slice: x: 4, y: 4, z: 16 (z_hi: 2, z_lo: 8; z = z_hi * 8 + z_lo), core: 2. Of those that a mesh axis runs over, the one named last changes fastest.
Arguments:
- velocity_term: float32 [128, 256, 256], P('gx', 'gy', 'gz'), may hold values from 0.05 to 0.2
- model_step: float32 [128, 256, 256], P('gx', 'gy', 'gz'), may hold values from -6 to 6
- background: bfloat16 [4, 128, 256, 256], P(None, 'gx', 'gy', 'gz'), may hold values from -6 to 6
- receivers: int32 [3, 256], replicated, may hold values from 0 to 255, as said below
- checkpoints: int32 [16], replicated, may hold values from 0 to 3, as said below
Outputs:
- image: float32 [128, 256, 256], P('gx', 'gy', 'gz')
- traces: float32 [16, 256], replicated
- column_image: float32 [128, 256], P('gx', 'gy')
- wavefield: float32 [128, 256, 256], P('gx', 'gy', 'gz')
Inputs may be any that keep to these rules, and one draw needn't show every extreme that they name: receivers[0] indexes the first lateral dimension (below 128), receivers[1] the second (below 256), receivers[2] depth (below 256). `checkpoints`: never falling over the time steps, beginning at 0 and ending at 3.
All inputs are finite; a program needn't handle non-finite values.
Results may differ from a plain program's by a relative error of at most 0.0003.
Values sent between devices are 32-bit elements; how exact they have to be, the bound alone decides.
No kernel may reach another device: no remote copies, remote signals or barrier semaphores. Data moves between devices by JAX's collectives and lax.ppermute only.
A program may use at most 64 MiB of HBM per device.

v0:
```python
import jax
import jax.numpy as jnp
from jax import lax
from jax.sharding import Mesh
from jax.sharding import PartitionSpec as P

GX_GY_GZ = ("gx_0", "gx_1", "gy_0", "gy_1", "gz")
GX = ("gx_0", "gx_1")
GY = ("gy_0", "gy_1")


near_coef = 4.0 / 3.0
far_coef = -1.0 / 12.0
center_coef = -2.5


def with_halo(block, sides, width):
    for axis, dim in sides:
        count = lax.axis_size(axis)
        forward = [(i, i + 1) for i in range(count - 1)]
        forward.append((count - 1, 0))
        backward = [(target, source) for source, target in forward]
        low = lax.ppermute(
            lax.slice_in_dim(block, block.shape[dim] - width, None, axis=dim), axis, forward
        )
        high = lax.ppermute(lax.slice_in_dim(block, 0, width, axis=dim), axis, backward)
        block = jnp.concatenate([low, block, high], axis=dim)
    return block


def by_axis(x, axes):
    for axis in axes:
        x = lax.psum(x, axis)
    return x


def gathered_total(x, axis):
    blocks = lax.all_gather(x, axis)
    return blocks.sum(axis=0)


def along(padded, dim):
    count = padded.shape[dim]
    first = lax.slice_in_dim(padded, 3, count - 1, axis=dim) + lax.slice_in_dim(
        padded, 1, count - 3, axis=dim
    )
    second = lax.slice_in_dim(padded, 4, count, axis=dim) + lax.slice_in_dim(
        padded, 0, count - 4, axis=dim
    )
    return near_coef * first + far_coef * second


def valid_laplace(padded):
    center = padded[2:-2, 2:-2, 2:-2]
    total = 3.0 * center_coef * center + along(padded[:, 2:-2, 2:-2], 0)
    return total + along(padded[2:-2, :, 2:-2], 1) + along(padded[2:-2, 2:-2, :], 2)


def depth_keep(size_z, width):
    cells = jnp.arange(size_z + 2 * width, dtype=jnp.int32)
    place = lax.axis_index("gz") * size_z - width + cells
    valid = (place >= 0) & (place < size_z * lax.axis_size("gz"))
    return valid.astype(jnp.float32)[None, None, :]


def deep_pad(stacked, keeper):
    whole = with_halo(stacked, ((GX, 1), (GY, 2), ("gz", 3)), 4)
    return whole * keeper[None]


def fixed_pad(stacked, keeper):
    whole = with_halo(stacked, ((GX, 1), (GY, 2), ("gz", 3)), 4)
    return whole * keeper[None]


def sample_row(samples, field, step, clip_x, clip_y, clip_z, inside):
    values = field[clip_x, clip_y, clip_z] * inside
    return lax.dynamic_update_index_in_dim(samples, values, step, 0)


def on_device(velocity_term, model_step, background, receivers, checkpoints):
    size_x, size_y, size_z = model_step.shape
    steps = checkpoints.shape[0]
    local_x = receivers[0] - lax.axis_index(GX) * size_x
    local_y = receivers[1] - lax.axis_index(GY) * size_y
    local_z = receivers[2] - lax.axis_index("gz") * size_z
    inside = (
        (local_x >= 0)
        & (local_x < size_x)
        & (local_y >= 0)
        & (local_y < size_y)
        & (local_z >= 0)
        & (local_z < size_z)
    )
    inside = inside.astype(jnp.float32)
    clip_x = jnp.clip(local_x, 0, size_x - 1)
    clip_y = jnp.clip(local_y, 0, size_y - 1)
    clip_z = jnp.clip(local_z, 0, size_z - 1)
    zeros = jnp.zeros(model_step.shape, jnp.float32)
    record = jnp.zeros((steps, receivers.shape[1]), jnp.float32)
    keep_four = depth_keep(size_z, 4)
    keep_two = depth_keep(size_z, 2)
    stacked = jnp.concatenate(
        [velocity_term[None], model_step[None], background.astype(jnp.float32)], axis=0
    )
    fixed = fixed_pad(stacked, keep_four)
    vel_four = fixed[0]
    vel_two = vel_four[2:-2, 2:-2, 2:-2]
    model_two = fixed[1, 2:-2, 2:-2, 2:-2]
    back_two = fixed[2:, 2:-2, 2:-2, 2:-2]

    def forward_pair(pair, carry):
        previous, current, samples = carry
        step = 2 * pair
        both = deep_pad(jnp.stack([previous, current]), keep_four)
        prev_two = both[0, 2:-2, 2:-2, 2:-2]
        cur_four = both[1]
        cur_two = cur_four[2:-2, 2:-2, 2:-2]
        accel_two = lax.dynamic_index_in_dim(back_two, checkpoints[step], 0, keepdims=False)
        next_two = (
            2.0 * cur_two - prev_two + vel_two * valid_laplace(cur_four) + model_two * accel_two
        ) * keep_two
        first = next_two[2:-2, 2:-2, 2:-2]
        samples = sample_row(samples, first, step, clip_x, clip_y, clip_z, inside)
        accel = lax.dynamic_index_in_dim(
            background, checkpoints[step + 1], 0, keepdims=False
        ).astype(jnp.float32)
        second = (
            2.0 * first - current + velocity_term * valid_laplace(next_two) + model_step * accel
        )
        samples = sample_row(samples, second, step + 1, clip_x, clip_y, clip_z, inside)
        return (first, second, samples)

    previous, current, record = lax.fori_loop(0, steps // 2, forward_pair, (zeros, zeros, record))
    traces = by_axis(record, GX_GY_GZ)
    total_x = size_x * lax.axis_size(GX)
    total_y = size_y * lax.axis_size(GY)
    outer_x = jnp.mod(receivers[0] - lax.axis_index(GX) * size_x + 2, total_x)
    outer_y = jnp.mod(receivers[1] - lax.axis_index(GY) * size_y + 2, total_y)
    outer_z = local_z + 2
    outer_in = (
        (outer_x < size_x + 4) & (outer_y < size_y + 4) & (outer_z >= 0) & (outer_z < size_z + 4)
    )
    outer_in = outer_in.astype(jnp.float32)
    outer_x = jnp.clip(outer_x, 0, size_x + 3)
    outer_y = jnp.clip(outer_y, 0, size_y + 3)
    outer_z = jnp.clip(outer_z, 0, size_z + 3)

    def adjoint_pair(pair, carry):
        later_two, later, image = carry
        step = steps - 1 - 2 * pair
        both = deep_pad(jnp.stack([later_two, later]), keep_four)
        far_two = both[0, 2:-2, 2:-2, 2:-2]
        near_four = both[1]
        near_two = near_four[2:-2, 2:-2, 2:-2]
        wide = 2.0 * near_two - far_two + valid_laplace(vel_four * near_four)
        inject = lax.dynamic_index_in_dim(traces, step, 0, keepdims=False) * outer_in
        wide = wide.at[outer_x, outer_y, outer_z].add(inject) * keep_two
        first = wide[2:-2, 2:-2, 2:-2]
        second = 2.0 * first - later + valid_laplace(vel_two * wide)
        inject_next = lax.dynamic_index_in_dim(traces, step - 1, 0, keepdims=False) * inside
        second = second.at[clip_x, clip_y, clip_z].add(inject_next)
        accel = lax.dynamic_index_in_dim(background, checkpoints[step], 0, keepdims=False).astype(
            jnp.float32
        )
        accel_next = lax.dynamic_index_in_dim(
            background, checkpoints[step - 1], 0, keepdims=False
        ).astype(jnp.float32)
        image = image + first * accel
        image = image + second * accel_next
        return (first, second, image)

    later_two, later, image = lax.fori_loop(0, steps // 2, adjoint_pair, (zeros, zeros, zeros))
    depth_total = size_z * lax.axis_size("gz")
    column_image = gathered_total(jnp.sum(image, axis=2), "gz") / depth_total
    return (image, traces, column_image, current)


def solution(mesh):
    torus = Mesh(
        mesh.devices.reshape(8, 4, 4, 2, mesh.shape["gz"]), ("gx_0", "gx_1", "gy_0", "gy_1", "gz")
    )
    return jax.shard_map(
        on_device,
        mesh=torus,
        in_specs=(P(GX, GY, "gz"), P(GX, GY, "gz"), P(None, GX, GY, "gz"), P(), P()),
        out_specs=(P(GX, GY, "gz"), P(), P(GX, GY), P(GX, GY, "gz")),
        check_vma=False,
    )
```

profile of v0, /device:TPU:9, one launch (start us, length us, event | category | flops | bytes accessed | tf_op | source)
XLA Modules:
  0.0 1411.3 jit_solution(8465047829303979307)
XLA Ops:
  5.6 13.9 collective-permute-start.13
  28.1 12.1 collective-permute-start.14
  43.6 18.6 %collective-permute-done.14 = f32[6,12,4,128]{3,2,1,0:T(4,128)S(1)} collective-permute-done((f32[6,12,4,128]{3,2,1,0:T(4,128)S(1)}, f32[6,12,4,128]{3,2,1,0:T(4,128)S(1)}, u32[]{:S(2)}, u32[]{:S(2)}) %collective-permute-start.14) | collective-permute-done | bytes 147488 | tf_op jit(solution)/shard_map/ppermute | solution.py:23
  88.3 515.8 %while.42 = (s32[]{:T(128)}, f32[4,32,128]{2,1,0:T(8,128)S(1)}, f32[4,32,128]{2,1,0:T(8,128)S(1)}, f32[16,256]{1,0:T(8,128)}, f32[8,36,132]{2,1,0:T(8,128)S(1)},...) while((s32[]{:T(128)}, f32[4,32,128]{2,1,0:T(8,128)S(1)}, ...), condition=%wide.region_1.2_spmd.clone, body=%wide.region_0.1_spmd.clone.sunk | while | flops 3218765 | bytes 10581052 | solution.py:134
  88.4 10.5 collective-permute-start
  101.5 13.4 collective-permute-done.1
  119.7 9.3 collective-permute-start.3
  135.1 9.4 collective-permute-start.4
  169.6 10.6 collective-permute-done.1
  183.9 10.4 collective-permute-start.3
  231.6 10.6 collective-permute-done.1
  242.2 12.4 collective-permute-start.2
  257.1 11.9 collective-permute-done.3
  300.1 10.6 collective-permute-done.1
  315.1 9.6 collective-permute-start.3
  360.2 10.6 collective-permute-done.1
  423.8 10.6 collective-permute-done.1
  439.6 8.9 collective-permute-start.3
  484.8 10.6 collective-permute-done.1
  495.5 8.7 collective-permute-start.2
  510.1 9.1 collective-permute-done.3
  549.4 10.6 collective-permute-done.1
  565.4 8.7 collective-permute-start.3
  604.1 42.1 %psum.35 = f32[16,256]{1,0:T(8,128)S(1)} all-reduce(f32[16,256]{1,0:T(8,128)} %get-tuple-element.1811), channel_id=1, replica_groups=mesh['gx_0'=8,'gx_1'=4,'gy_0'=4,'gy_1'=2,'gz'=2] {'gx_0'}, use_global_device_ids=true, to_apply=%region_2.3 | all-reduce | flops 4096 | bytes 32768 | tf_op jit(solution)/shard_map/psum | solution.py:33
  646.2 11.4 psum.36
  657.6 10.7 psum.37
  668.3 20.3 %psum.38 = f32[16,256]{1,0:T(8,128)S(1)} all-reduce(f32[16,256]{1,0:T(8,128)S(1)} %psum.37), channel_id=1, replica_groups=mesh['gx_0'=8,'gx_1'=4,'gy_0'=4,'gy_1'=2,'gz'=2] {'gy_1'}, use_global_device_ids=true, to_apply=%region_5.6 | all-reduce | flops 4096 | bytes 32768 | tf_op jit(solution)/shard_map/psum | solution.py:33
  688.6 19.2 %psum.39 = f32[16,256]{1,0:T(8,128)S(1)} all-reduce(f32[16,256]{1,0:T(8,128)S(1)} %psum.38), channel_id=1, replica_groups=mesh['gx_0'=8,'gx_1'=4,'gy_0'=4,'gy_1'=2,'gz'=2] {'gz'}, use_global_device_ids=true, to_apply=%region_6.7 | all-reduce | flops 4096 | bytes 32768 | tf_op jit(solution)/shard_map/psum | solution.py:33
  707.8 698.5 %while.43 = (s32[]{:T(128)}, f32[4,32,128]{2,0,1:T(4,128)S(1)}, f32[4,32,128]{2,1,0:T(8,128)S(1)}, f32[4,32,128]{2,0,1:T(4,128)}, f32[12,40,136]{2,0,1:T(8,128)S...) while((s32[]{:T(128)}, f32[4,32,128]{2,0,1:T(4,128)S(1)}, ...), condition=%wide.region_10.11_spmd.clone, body=%wide.region_7.10_spmd.clone.sunk | while | flops 3232334 | bytes 12275631 | solution.py:173
  714.7 13.4 collective-permute-done.7
  728.1 8.6 collective-permute-start.8
  742.2 9.2 collective-permute-done.9
  765.8 15.4 %scatter_fusion = f32[8,36,132]{2,0,1:T(8,128)S(1)} fusion(f32[8,36,132]{2,0,1:T(8,128)S(1)} %fusion.112, s32[256]{0:T(256)S(1)} %bitcast.151, f32[256]{0:T(256)S(1)} %mul.1064), kind=kCustom, calls=%fused_computation.2.clone.clone.1 | custom fusion | flops 256 | bytes 6144 | tf_op jit(solution)/shard_map/while/body/eval_jaxpr/scatter-add | solution.py:158
  781.9 15.4 %scatter_fusion.1 = f32[4,32,128]{2,1,0:T(8,128)S(1)} fusion(f32[4,32,128]{2,1,0:T(8,128)S(1)} %copy.100, s32[256]{0:T(256)S(1)} %bitcast.150, f32[256]{0:T(256)S(1)} %mul.1065), kind=kCustom, calls=%fused_computation.3.clone.clone.1 | custom fusion | flops 256 | bytes 6144 | tf_op jit(solution)/shard_map/while/body/eval_jaxpr/scatter-add | solution.py:162
  804.6 13.1 collective-permute-done.7
  831.8 8.0 collective-permute-done.9
  854.3 15.4 %scatter_fusion = f32[8,36,132]{2,0,1:T(8,128)S(1)} fusion(f32[8,36,132]{2,0,1:T(8,128)S(1)} %fusion.112, s32[256]{0:T(256)S(1)} %bitcast.151, f32[256]{0:T(256)S(1)} %mul.1064), kind=kCustom, calls=%fused_computation.2.clone.clone.1 | custom fusion | flops 256 | bytes 6144 | tf_op jit(solution)/shard_map/while/body/eval_jaxpr/scatter-add | solution.py:158
  870.4 15.4 %scatter_fusion.1 = f32[4,32,128]{2,1,0:T(8,128)S(1)} fusion(f32[4,32,128]{2,1,0:T(8,128)S(1)} %copy.100, s32[256]{0:T(256)S(1)} %bitcast.150, f32[256]{0:T(256)S(1)} %mul.1065), kind=kCustom, calls=%fused_computation.3.clone.clone.1 | custom fusion | flops 256 | bytes 6144 | tf_op jit(solution)/shard_map/while/body/eval_jaxpr/scatter-add | solution.py:162
  893.1 10.6 collective-permute-done.7
  903.8 8.1 collective-permute-start.8
  917.9 8.7 collective-permute-done.9
  941.6 15.4 %scatter_fusion = f32[8,36,132]{2,0,1:T(8,128)S(1)} fusion(f32[8,36,132]{2,0,1:T(8,128)S(1)} %fusion.112, s32[256]{0:T(256)S(1)} %bitcast.151, f32[256]{0:T(256)S(1)} %mul.1064), kind=kCustom, calls=%fused_computation.2.clone.clone.1 | custom fusion | flops 256 | bytes 6144 | tf_op jit(solution)/shard_map/while/body/eval_jaxpr/scatter-add | solution.py:158
  957.6 15.4 %scatter_fusion.1 = f32[4,32,128]{2,1,0:T(8,128)S(1)} fusion(f32[4,32,128]{2,1,0:T(8,128)S(1)} %copy.100, s32[256]{0:T(256)S(1)} %bitcast.150, f32[256]{0:T(256)S(1)} %mul.1065), kind=kCustom, calls=%fused_computation.3.clone.clone.1 | custom fusion | flops 256 | bytes 6144 | tf_op jit(solution)/shard_map/while/body/eval_jaxpr/scatter-add | solution.py:162
  980.4 10.3 collective-permute-done.7
  990.8 9.7 collective-permute-start.8
  1004.8 10.3 collective-permute-done.9
  1030.0 15.4 %scatter_fusion = f32[8,36,132]{2,0,1:T(8,128)S(1)} fusion(f32[8,36,132]{2,0,1:T(8,128)S(1)} %fusion.112, s32[256]{0:T(256)S(1)} %bitcast.151, f32[256]{0:T(256)S(1)} %mul.1064), kind=kCustom, calls=%fused_computation.2.clone.clone.1 | custom fusion | flops 256 | bytes 6144 | tf_op jit(solution)/shard_map/while/body/eval_jaxpr/scatter-add | solution.py:158
  1046.1 15.4 %scatter_fusion.1 = f32[4,32,128]{2,1,0:T(8,128)S(1)} fusion(f32[4,32,128]{2,1,0:T(8,128)S(1)} %copy.100, s32[256]{0:T(256)S(1)} %bitcast.150, f32[256]{0:T(256)S(1)} %mul.1065), kind=kCustom, calls=%fused_computation.3.clone.clone.1 | custom fusion | flops 256 | bytes 6144 | tf_op jit(solution)/shard_map/while/body/eval_jaxpr/scatter-add | solution.py:162
  1068.9 10.6 collective-permute-done.7
  1084.4 9.1 collective-permute-start.9
  1114.0 15.4 %scatter_fusion = f32[8,36,132]{2,0,1:T(8,128)S(1)} fusion(f32[8,36,132]{2,0,1:T(8,128)S(1)} %fusion.112, s32[256]{0:T(256)S(1)} %bitcast.151, f32[256]{0:T(256)S(1)} %mul.1064), kind=kCustom, calls=%fused_computation.2.clone.clone.1 | custom fusion | flops 256 | bytes 6144 | tf_op jit(solution)/shard_map/while/body/eval_jaxpr/scatter-add | solution.py:158
  1130.0 15.4 %scatter_fusion.1 = f32[4,32,128]{2,1,0:T(8,128)S(1)} fusion(f32[4,32,128]{2,1,0:T(8,128)S(1)} %copy.100, s32[256]{0:T(256)S(1)} %bitcast.150, f32[256]{0:T(256)S(1)} %mul.1065), kind=kCustom, calls=%fused_computation.3.clone.clone.1 | custom fusion | flops 256 | bytes 6144 | tf_op jit(solution)/shard_map/while/body/eval_jaxpr/scatter-add | solution.py:162
  1152.8 12.4 collective-permute-done.7
  1201.7 15.4 %scatter_fusion = f32[8,36,132]{2,0,1:T(8,128)S(1)} fusion(f32[8,36,132]{2,0,1:T(8,128)S(1)} %fusion.112, s32[256]{0:T(256)S(1)} %bitcast.151, f32[256]{0:T(256)S(1)} %mul.1064), kind=kCustom, calls=%fused_computation.2.clone.clone.1 | custom fusion | flops 256 | bytes 6144 | tf_op jit(solution)/shard_map/while/body/eval_jaxpr/scatter-add | solution.py:158
  1217.8 15.4 %scatter_fusion.1 = f32[4,32,128]{2,1,0:T(8,128)S(1)} fusion(f32[4,32,128]{2,1,0:T(8,128)S(1)} %copy.100, s32[256]{0:T(256)S(1)} %bitcast.150, f32[256]{0:T(256)S(1)} %mul.1065), kind=kCustom, calls=%fused_computation.3.clone.clone.1 | custom fusion | flops 256 | bytes 6144 | tf_op jit(solution)/shard_map/while/body/eval_jaxpr/scatter-add | solution.py:162
  1240.6 11.3 collective-permute-done.7
  1257.2 8.6 collective-permute-start.9
  1286.8 15.4 %scatter_fusion = f32[8,36,132]{2,0,1:T(8,128)S(1)} fusion(f32[8,36,132]{2,0,1:T(8,128)S(1)} %fusion.112, s32[256]{0:T(256)S(1)} %bitcast.151, f32[256]{0:T(256)S(1)} %mul.1064), kind=kCustom, calls=%fused_computation.2.clone.clone.1 | custom fusion | flops 256 | bytes 6144 | tf_op jit(solution)/shard_map/while/body/eval_jaxpr/scatter-add | solution.py:158
  1302.9 15.4 %scatter_fusion.1 = f32[4,32,128]{2,1,0:T(8,128)S(1)} fusion(f32[4,32,128]{2,1,0:T(8,128)S(1)} %copy.100, s32[256]{0:T(256)S(1)} %bitcast.150, f32[256]{0:T(256)S(1)} %mul.1065), kind=kCustom, calls=%fused_computation.3.clone.clone.1 | custom fusion | flops 256 | bytes 6144 | tf_op jit(solution)/shard_map/while/body/eval_jaxpr/scatter-add | solution.py:162
  1325.7 10.6 collective-permute-done.7
  1336.3 8.1 collective-permute-start.8
  1350.4 8.7 collective-permute-done.9
  1374.0 15.4 %scatter_fusion = f32[8,36,132]{2,0,1:T(8,128)S(1)} fusion(f32[8,36,132]{2,0,1:T(8,128)S(1)} %fusion.112, s32[256]{0:T(256)S(1)} %bitcast.151, f32[256]{0:T(256)S(1)} %mul.1064), kind=kCustom, calls=%fused_computation.2.clone.clone.1 | custom fusion | flops 256 | bytes 6144 | tf_op jit(solution)/shard_map/while/body/eval_jaxpr/scatter-add | solution.py:158
  1390.1 15.4 %scatter_fusion.1 = f32[4,32,128]{2,1,0:T(8,128)S(1)} fusion(f32[4,32,128]{2,1,0:T(8,128)S(1)} %copy.100, s32[256]{0:T(256)S(1)} %bitcast.150, f32[256]{0:T(256)S(1)} %mul.1065), kind=kCustom, calls=%fused_computation.3.clone.clone.1 | custom fusion | flops 256 | bytes 6144 | tf_op jit(solution)/shard_map/while/body/eval_jaxpr/scatter-add | solution.py:162
  (779 shorter events, 562.0 us)
Async XLA Ops:
  2.5 23.9 %collective-permute-start.12 = (f32[6,4,32,128]{3,2,1,0:T(8,128)S(1)}, f32[6,4,32,128]{3,2,1,0:T(8,128)S(1)}, u32[]{:S(2)}, u32[]{:S(2)}) collective-permute-start(f32[6,4,32,128]{3,2,1,0:T(8,128)S(1)} %pad_maximum_fusion.13), channel_id=1, source_target_pairs={{0,16},{16,32},{32,48},{48,64},{64,80},{80,96},{96,112},{112,128},... | collective-permute-start | bytes 1179656 | tf_op jit(solution)/shard_map/ppermute | solution.py:23
  5.6 21.6 %collective-permute-start.13 = (f32[6,4,32,128]{3,2,1,0:T(8,128)S(1)}, f32[6,4,32,128]{3,2,1,0:T(8,128)S(1)}, u32[]{:S(2)}, u32[]{:S(2)}) collective-permute-start(f32[6,4,32,128]{3,2,1,0:T(8,128)S(1)} %pad_maximum_fusion.13), channel_id=1, source_target_pairs={{16,0},{32,16},{48,32},{64,48},{80,64},{96,80},{112,96},{128,112},... | collective-permute-start | bytes 1179656 | tf_op jit(solution)/shard_map/ppermute | solution.py:26
  28.1 34.1 %collective-permute-start.14 = (f32[6,12,4,128]{3,2,1,0:T(4,128)S(1)}, f32[6,12,4,128]{3,2,1,0:T(4,128)S(1)}, u32[]{:S(2)}, u32[]{:S(2)}) collective-permute-start(f32[6,12,4,128]{3,2,1,0:T(4,128)S(1)} %get-tuple-element.1366), channel_id=1, source_target_pairs={{0,2},{2,4},{4,6},{6,8},{8,10},{10,12},{12,14},{14,0},{1,3},{3,5},... | collective-permute-start | bytes 442376 | tf_op jit(solution)/shard_map/ppermute | solution.py:23
  40.3 25.2 %collective-permute-start.15 = (f32[6,12,4,128]{3,2,1,0:T(4,128)S(1)}, f32[6,12,4,128]{3,2,1,0:T(4,128)S(1)}, u32[]{:S(2)}, u32[]{:S(2)}) collective-permute-start(f32[6,12,4,128]{3,2,1,0:T(4,128)S(1)} %get-tuple-element.1367), channel_id=1, source_target_pairs={{2,0},{4,2},{6,4},{8,6},{10,8},{12,10},{14,12},{0,14},{3,1},{5,3},... | collective-permute-start | bytes 442376 | tf_op jit(solution)/shard_map/ppermute | solution.py:26
  88.4 13.2 collective-permute-start
  98.8 16.1 %collective-permute-start.1 = (f32[2,4,32,128]{3,2,1,0:T(8,128)S(1)}, f32[2,4,32,128]{3,2,1,0:T(8,128)S(1)}, u32[]{:S(2)}, u32[]{:S(2)}) collective-permute-start(f32[2,4,32,128]{3,2,1,0:T(8,128)S(1)} %pad_maximum_fusion.25), channel_id=1, source_target_pairs={{0,16},{16,32},{32,48},{48,64},{64,80},{80,96},{96,112},{112,128},... | collective-permute-start | bytes 393224 | tf_op jit(solution)/shard_map/while/body/eval_jaxpr/ppermute | solution.py:23
  115.0 14.6 %collective-permute-start.2 = (f32[2,12,4,128]{3,2,1,0:T(4,128)S(1)}, f32[2,12,4,128]{3,2,1,0:T(4,128)S(1)}, u32[]{:S(2)}, u32[]{:S(2)}) collective-permute-start(f32[2,12,4,128]{3,2,1,0:T(4,128)S(1)} %get-tuple-element.1597), channel_id=1, source_target_pairs={{2,0},{4,2},{6,4},{8,6},{10,8},{12,10},{14,12},{0,14},{3,1},{5,3},... | collective-permute-start | bytes 147464 | tf_op jit(solution)/shard_map/while/body/eval_jaxpr/ppermute | solution.py:26
  119.7 14.4 %collective-permute-start.3 = (f32[2,12,4,128]{3,2,1,0:T(4,128)S(1)}, f32[2,12,4,128]{3,2,1,0:T(4,128)S(1)}, u32[]{:S(2)}, u32[]{:S(2)}) collective-permute-start(f32[2,12,4,128]{3,2,1,0:T(4,128)S(1)} %get-tuple-element.1598), channel_id=1, source_target_pairs={{0,2},{2,4},{4,6},{6,8},{8,10},{10,12},{12,14},{14,0},{1,3},{3,5},... | collective-permute-start | bytes 147464 | tf_op jit(solution)/shard_map/while/body/eval_jaxpr/ppermute | solution.py:23
  135.1 16.6 %collective-permute-start.4 = (f32[2,12,40,4]{3,2,1,0:T(8,128)S(1)}, f32[2,12,40,4]{3,2,1,0:T(8,128)S(1)}, u32[]{:S(2)}, u32[]{:S(2)}) collective-permute-start(f32[2,12,40,4]{3,2,1,0:T(8,128)S(1)} %get-tuple-element.1599), channel_id=1, source_target_pairs={{1,0},{0,1},{3,2},{2,3},{5,4},{4,5},{7,6},{6,7},{9,8},{8,9},{11,10... | collective-permute-start | bytes 46088 | tf_op jit(solution)/shard_map/while/body/eval_jaxpr/ppermute | solution.py:26
  165.1 15.2 %collective-permute-start.1 = (f32[2,4,32,128]{3,2,1,0:T(8,128)S(1)}, f32[2,4,32,128]{3,2,1,0:T(8,128)S(1)}, u32[]{:S(2)}, u32[]{:S(2)}) collective-permute-start(f32[2,4,32,128]{3,2,1,0:T(8,128)S(1)} %pad_maximum_fusion.25), channel_id=1, source_target_pairs={{0,16},{16,32},{32,48},{48,64},{64,80},{80,96},{96,112},{112,128},... | collective-permute-start | bytes 393224 | tf_op jit(solution)/shard_map/while/body/eval_jaxpr/ppermute | solution.py:23
  180.3 14.6 %collective-permute-start.2 = (f32[2,12,4,128]{3,2,1,0:T(4,128)S(1)}, f32[2,12,4,128]{3,2,1,0:T(4,128)S(1)}, u32[]{:S(2)}, u32[]{:S(2)}) collective-permute-start(f32[2,12,4,128]{3,2,1,0:T(4,128)S(1)} %get-tuple-element.1597), channel_id=1, source_target_pairs={{2,0},{4,2},{6,4},{8,6},{10,8},{12,10},{14,12},{0,14},{3,1},{5,3},... | collective-permute-start | bytes 147464 | tf_op jit(solution)/shard_map/while/body/eval_jaxpr/ppermute | solution.py:26
  183.9 14.9 %collective-permute-start.3 = (f32[2,12,4,128]{3,2,1,0:T(4,128)S(1)}, f32[2,12,4,128]{3,2,1,0:T(4,128)S(1)}, u32[]{:S(2)}, u32[]{:S(2)}) collective-permute-start(f32[2,12,4,128]{3,2,1,0:T(4,128)S(1)} %get-tuple-element.1598), channel_id=1, source_target_pairs={{0,2},{2,4},{4,6},{6,8},{8,10},{10,12},{12,14},{14,0},{1,3},{3,5},... | collective-permute-start | bytes 147464 | tf_op jit(solution)/shard_map/while/body/eval_jaxpr/ppermute | solution.py:23
  199.7 11.4 collective-permute-start.4
  227.4 14.9 %collective-permute-start.1 = (f32[2,4,32,128]{3,2,1,0:T(8,128)S(1)}, f32[2,4,32,128]{3,2,1,0:T(8,128)S(1)}, u32[]{:S(2)}, u32[]{:S(2)}) collective-permute-start(f32[2,4,32,128]{3,2,1,0:T(8,128)S(1)} %pad_maximum_fusion.25), channel_id=1, source_target_pairs={{0,16},{16,32},{32,48},{48,64},{64,80},{80,96},{96,112},{112,128},... | collective-permute-start | bytes 393224 | tf_op jit(solution)/shard_map/while/body/eval_jaxpr/ppermute | solution.py:23
  242.2 14.9 %collective-permute-start.2 = (f32[2,12,4,128]{3,2,1,0:T(4,128)S(1)}, f32[2,12,4,128]{3,2,1,0:T(4,128)S(1)}, u32[]{:S(2)}, u32[]{:S(2)}) collective-permute-start(f32[2,12,4,128]{3,2,1,0:T(4,128)S(1)} %get-tuple-element.1597), channel_id=1, source_target_pairs={{2,0},{4,2},{6,4},{8,6},{10,8},{12,10},{14,12},{0,14},{3,1},{5,3},... | collective-permute-start | bytes 147464 | tf_op jit(solution)/shard_map/while/body/eval_jaxpr/ppermute | solution.py:26
  254.6 14.4 %collective-permute-start.3 = (f32[2,12,4,128]{3,2,1,0:T(4,128)S(1)}, f32[2,12,4,128]{3,2,1,0:T(4,128)S(1)}, u32[]{:S(2)}, u32[]{:S(2)}) collective-permute-start(f32[2,12,4,128]{3,2,1,0:T(4,128)S(1)} %get-tuple-element.1598), channel_id=1, source_target_pairs={{0,2},{2,4},{4,6},{6,8},{8,10},{10,12},{12,14},{14,0},{1,3},{3,5},... | collective-permute-start | bytes 147464 | tf_op jit(solution)/shard_map/while/body/eval_jaxpr/ppermute | solution.py:23
  269.9 12.2 collective-permute-start.4
  295.5 15.2 %collective-permute-start.1 = (f32[2,4,32,128]{3,2,1,0:T(8,128)S(1)}, f32[2,4,32,128]{3,2,1,0:T(8,128)S(1)}, u32[]{:S(2)}, u32[]{:S(2)}) collective-permute-start(f32[2,4,32,128]{3,2,1,0:T(8,128)S(1)} %pad_maximum_fusion.25), channel_id=1, source_target_pairs={{0,16},{16,32},{32,48},{48,64},{64,80},{80,96},{96,112},{112,128},... | collective-permute-start | bytes 393224 | tf_op jit(solution)/shard_map/while/body/eval_jaxpr/ppermute | solution.py:23
  310.7 14.6 %collective-permute-start.2 = (f32[2,12,4,128]{3,2,1,0:T(4,128)S(1)}, f32[2,12,4,128]{3,2,1,0:T(4,128)S(1)}, u32[]{:S(2)}, u32[]{:S(2)}) collective-permute-start(f32[2,12,4,128]{3,2,1,0:T(4,128)S(1)} %get-tuple-element.1597), channel_id=1, source_target_pairs={{2,0},{4,2},{6,4},{8,6},{10,8},{12,10},{14,12},{0,14},{3,1},{5,3},... | collective-permute-start | bytes 147464 | tf_op jit(solution)/shard_map/while/body/eval_jaxpr/ppermute | solution.py:26
  315.1 14.4 %collective-permute-start.3 = (f32[2,12,4,128]{3,2,1,0:T(4,128)S(1)}, f32[2,12,4,128]{3,2,1,0:T(4,128)S(1)}, u32[]{:S(2)}, u32[]{:S(2)}) collective-permute-start(f32[2,12,4,128]{3,2,1,0:T(4,128)S(1)} %get-tuple-element.1598), channel_id=1, source_target_pairs={{0,2},{2,4},{4,6},{6,8},{8,10},{10,12},{12,14},{14,0},{1,3},{3,5},... | collective-permute-start | bytes 147464 | tf_op jit(solution)/shard_map/while/body/eval_jaxpr/ppermute | solution.py:23
  330.4 11.9 collective-permute-start.4
  355.7 15.2 %collective-permute-start.1 = (f32[2,4,32,128]{3,2,1,0:T(8,128)S(1)}, f32[2,4,32,128]{3,2,1,0:T(8,128)S(1)}, u32[]{:S(2)}, u32[]{:S(2)}) collective-permute-start(f32[2,4,32,128]{3,2,1,0:T(8,128)S(1)} %pad_maximum_fusion.25), channel_id=1, source_target_pairs={{0,16},{16,32},{32,48},{48,64},{64,80},{80,96},{96,112},{112,128},... | collective-permute-start | bytes 393224 | tf_op jit(solution)/shard_map/while/body/eval_jaxpr/ppermute | solution.py:23
  370.9 14.6 %collective-permute-start.2 = (f32[2,12,4,128]{3,2,1,0:T(4,128)S(1)}, f32[2,12,4,128]{3,2,1,0:T(4,128)S(1)}, u32[]{:S(2)}, u32[]{:S(2)}) collective-permute-start(f32[2,12,4,128]{3,2,1,0:T(4,128)S(1)} %get-tuple-element.1597), channel_id=1, source_target_pairs={{2,0},{4,2},{6,4},{8,6},{10,8},{12,10},{14,12},{0,14},{3,1},{5,3},... | collective-permute-start | bytes 147464 | tf_op jit(solution)/shard_map/while/body/eval_jaxpr/ppermute | solution.py:26
  378.7 14.4 %collective-permute-start.3 = (f32[2,12,4,128]{3,2,1,0:T(4,128)S(1)}, f32[2,12,4,128]{3,2,1,0:T(4,128)S(1)}, u32[]{:S(2)}, u32[]{:S(2)}) collective-permute-start(f32[2,12,4,128]{3,2,1,0:T(4,128)S(1)} %get-tuple-element.1598), channel_id=1, source_target_pairs={{0,2},{2,4},{4,6},{6,8},{8,10},{10,12},{12,14},{14,0},{1,3},{3,5},... | collective-permute-start | bytes 147464 | tf_op jit(solution)/shard_map/while/body/eval_jaxpr/ppermute | solution.py:23
  394.0 11.9 collective-permute-start.4
  419.3 15.2 %collective-permute-start.1 = (f32[2,4,32,128]{3,2,1,0:T(8,128)S(1)}, f32[2,4,32,128]{3,2,1,0:T(8,128)S(1)}, u32[]{:S(2)}, u32[]{:S(2)}) collective-permute-start(f32[2,4,32,128]{3,2,1,0:T(8,128)S(1)} %pad_maximum_fusion.25), channel_id=1, source_target_pairs={{0,16},{16,32},{32,48},{48,64},{64,80},{80,96},{96,112},{112,128},... | collective-permute-start | bytes 393224 | tf_op jit(solution)/shard_map/while/body/eval_jaxpr/ppermute | solution.py:23
  434.5 14.6 %collective-permute-start.2 = (f32[2,12,4,128]{3,2,1,0:T(4,128)S(1)}, f32[2,12,4,128]{3,2,1,0:T(4,128)S(1)}, u32[]{:S(2)}, u32[]{:S(2)}) collective-permute-start(f32[2,12,4,128]{3,2,1,0:T(4,128)S(1)} %get-tuple-element.1597), channel_id=1, source_target_pairs={{2,0},{4,2},{6,4},{8,6},{10,8},{12,10},{14,12},{0,14},{3,1},{5,3},... | collective-permute-start | bytes 147464 | tf_op jit(solution)/shard_map/while/body/eval_jaxpr/ppermute | solution.py:26
  439.6 14.4 %collective-permute-start.3 = (f32[2,12,4,128]{3,2,1,0:T(4,128)S(1)}, f32[2,12,4,128]{3,2,1,0:T(4,128)S(1)}, u32[]{:S(2)}, u32[]{:S(2)}) collective-permute-start(f32[2,12,4,128]{3,2,1,0:T(4,128)S(1)} %get-tuple-element.1598), channel_id=1, source_target_pairs={{0,2},{2,4},{4,6},{6,8},{8,10},{10,12},{12,14},{14,0},{1,3},{3,5},... | collective-permute-start | bytes 147464 | tf_op jit(solution)/shard_map/while/body/eval_jaxpr/ppermute | solution.py:23
  454.9 12.0 collective-permute-start.4
  480.3 15.2 %collective-permute-start.1 = (f32[2,4,32,128]{3,2,1,0:T(8,128)S(1)}, f32[2,4,32,128]{3,2,1,0:T(8,128)S(1)}, u32[]{:S(2)}, u32[]{:S(2)}) collective-permute-start(f32[2,4,32,128]{3,2,1,0:T(8,128)S(1)} %pad_maximum_fusion.25), channel_id=1, source_target_pairs={{0,16},{16,32},{32,48},{48,64},{64,80},{80,96},{96,112},{112,128},... | collective-permute-start | bytes 393224 | tf_op jit(solution)/shard_map/while/body/eval_jaxpr/ppermute | solution.py:23
  495.5 14.6 %collective-permute-start.2 = (f32[2,12,4,128]{3,2,1,0:T(4,128)S(1)}, f32[2,12,4,128]{3,2,1,0:T(4,128)S(1)}, u32[]{:S(2)}, u32[]{:S(2)}) collective-permute-start(f32[2,12,4,128]{3,2,1,0:T(4,128)S(1)} %get-tuple-element.1597), channel_id=1, source_target_pairs={{2,0},{4,2},{6,4},{8,6},{10,8},{12,10},{14,12},{0,14},{3,1},{5,3},... | collective-permute-start | bytes 147464 | tf_op jit(solution)/shard_map/while/body/eval_jaxpr/ppermute | solution.py:26
  504.2 15.0 %collective-permute-start.3 = (f32[2,12,4,128]{3,2,1,0:T(4,128)S(1)}, f32[2,12,4,128]{3,2,1,0:T(4,128)S(1)}, u32[]{:S(2)}, u32[]{:S(2)}) collective-permute-start(f32[2,12,4,128]{3,2,1,0:T(4,128)S(1)} %get-tuple-element.1598), channel_id=1, source_target_pairs={{0,2},{2,4},{4,6},{6,8},{8,10},{10,12},{12,14},{14,0},{1,3},{3,5},... | collective-permute-start | bytes 147464 | tf_op jit(solution)/shard_map/while/body/eval_jaxpr/ppermute | solution.py:23
  544.9 15.2 %collective-permute-start.1 = (f32[2,4,32,128]{3,2,1,0:T(8,128)S(1)}, f32[2,4,32,128]{3,2,1,0:T(8,128)S(1)}, u32[]{:S(2)}, u32[]{:S(2)}) collective-permute-start(f32[2,4,32,128]{3,2,1,0:T(8,128)S(1)} %pad_maximum_fusion.25), channel_id=1, source_target_pairs={{0,16},{16,32},{32,48},{48,64},{64,80},{80,96},{96,112},{112,128},... | collective-permute-start | bytes 393224 | tf_op jit(solution)/shard_map/while/body/eval_jaxpr/ppermute | solution.py:23
  560.1 14.6 %collective-permute-start.2 = (f32[2,12,4,128]{3,2,1,0:T(4,128)S(1)}, f32[2,12,4,128]{3,2,1,0:T(4,128)S(1)}, u32[]{:S(2)}, u32[]{:S(2)}) collective-permute-start(f32[2,12,4,128]{3,2,1,0:T(4,128)S(1)} %get-tuple-element.1597), channel_id=1, source_target_pairs={{2,0},{4,2},{6,4},{8,6},{10,8},{12,10},{14,12},{0,14},{3,1},{5,3},... | collective-permute-start | bytes 147464 | tf_op jit(solution)/shard_map/while/body/eval_jaxpr/ppermute | solution.py:26
  565.4 14.4 %collective-permute-start.3 = (f32[2,12,4,128]{3,2,1,0:T(4,128)S(1)}, f32[2,12,4,128]{3,2,1,0:T(4,128)S(1)}, u32[]{:S(2)}, u32[]{:S(2)}) collective-permute-start(f32[2,12,4,128]{3,2,1,0:T(4,128)S(1)} %get-tuple-element.1598), channel_id=1, source_target_pairs={{0,2},{2,4},{4,6},{6,8},{8,10},{10,12},{12,14},{14,0},{1,3},{3,5},... | collective-permute-start | bytes 147464 | tf_op jit(solution)/shard_map/while/body/eval_jaxpr/ppermute | solution.py:23
  580.7 11.9 collective-permute-start.4
  710.0 18.1 %collective-permute-start.7 = (f32[2,4,32,128]{3,1,2,0:T(4,128)S(1)}, f32[2,4,32,128]{3,1,2,0:T(4,128)S(1)}, u32[]{:S(2)}, u32[]{:S(2)}) collective-permute-start(f32[2,4,32,128]{3,1,2,0:T(4,128)S(1)} %pad_maximum_fusion.28), channel_id=1, source_target_pairs={{0,16},{16,32},{32,48},{48,64},{64,80},{80,96},{96,112},{112,128},... | collective-permute-start | bytes 393224 | tf_op jit(solution)/shard_map/while/body/eval_jaxpr/ppermute | solution.py:23
  728.1 14.0 collective-permute-start.8
  736.7 14.6 %collective-permute-start.9 = (f32[2,12,4,128]{3,1,2,0:T(8,128)S(1)}, f32[2,12,4,128]{3,1,2,0:T(8,128)S(1)}, u32[]{:S(2)}, u32[]{:S(2)}) collective-permute-start(f32[2,12,4,128]{3,1,2,0:T(8,128)S(1)} %get-tuple-element.1627), channel_id=1, source_target_pairs={{0,2},{2,4},{4,6},{6,8},{8,10},{10,12},{12,14},{14,0},{1,3},{3,5},... | collective-permute-start | bytes 147464 | tf_op jit(solution)/shard_map/while/body/eval_jaxpr/ppermute | solution.py:23
  800.1 17.7 %collective-permute-start.7 = (f32[2,4,32,128]{3,1,2,0:T(4,128)S(1)}, f32[2,4,32,128]{3,1,2,0:T(4,128)S(1)}, u32[]{:S(2)}, u32[]{:S(2)}) collective-permute-start(f32[2,4,32,128]{3,1,2,0:T(4,128)S(1)} %pad_maximum_fusion.28), channel_id=1, source_target_pairs={{0,16},{16,32},{32,48},{48,64},{64,80},{80,96},{96,112},{112,128},... | collective-permute-start | bytes 393224 | tf_op jit(solution)/shard_map/while/body/eval_jaxpr/ppermute | solution.py:23
  817.8 14.0 collective-permute-start.8
  825.2 14.6 %collective-permute-start.9 = (f32[2,12,4,128]{3,1,2,0:T(8,128)S(1)}, f32[2,12,4,128]{3,1,2,0:T(8,128)S(1)}, u32[]{:S(2)}, u32[]{:S(2)}) collective-permute-start(f32[2,12,4,128]{3,1,2,0:T(8,128)S(1)} %get-tuple-element.1627), channel_id=1, source_target_pairs={{0,2},{2,4},{4,6},{6,8},{8,10},{10,12},{12,14},{14,0},{1,3},{3,5},... | collective-permute-start | bytes 147464 | tf_op jit(solution)/shard_map/while/body/eval_jaxpr/ppermute | solution.py:23
  888.6 15.2 %collective-permute-start.7 = (f32[2,4,32,128]{3,1,2,0:T(4,128)S(1)}, f32[2,4,32,128]{3,1,2,0:T(4,128)S(1)}, u32[]{:S(2)}, u32[]{:S(2)}) collective-permute-start(f32[2,4,32,128]{3,1,2,0:T(4,128)S(1)} %pad_maximum_fusion.28), channel_id=1, source_target_pairs={{0,16},{16,32},{32,48},{48,64},{64,80},{80,96},{96,112},{112,128},... | collective-permute-start | bytes 393224 | tf_op jit(solution)/shard_map/while/body/eval_jaxpr/ppermute | solution.py:23
  903.8 14.0 collective-permute-start.8
  911.9 14.6 %collective-permute-start.9 = (f32[2,12,4,128]{3,1,2,0:T(8,128)S(1)}, f32[2,12,4,128]{3,1,2,0:T(8,128)S(1)}, u32[]{:S(2)}, u32[]{:S(2)}) collective-permute-start(f32[2,12,4,128]{3,1,2,0:T(8,128)S(1)} %get-tuple-element.1627), channel_id=1, source_target_pairs={{0,2},{2,4},{4,6},{6,8},{8,10},{10,12},{12,14},{14,0},{1,3},{3,5},... | collective-permute-start | bytes 147464 | tf_op jit(solution)/shard_map/while/body/eval_jaxpr/ppermute | solution.py:23
  927.2 11.4 collective-permute-start.10
  975.8 14.9 %collective-permute-start.7 = (f32[2,4,32,128]{3,1,2,0:T(4,128)S(1)}, f32[2,4,32,128]{3,1,2,0:T(4,128)S(1)}, u32[]{:S(2)}, u32[]{:S(2)}) collective-permute-start(f32[2,4,32,128]{3,1,2,0:T(4,128)S(1)} %pad_maximum_fusion.28), channel_id=1, source_target_pairs={{0,16},{16,32},{32,48},{48,64},{64,80},{80,96},{96,112},{112,128},... | collective-permute-start | bytes 393224 | tf_op jit(solution)/shard_map/while/body/eval_jaxpr/ppermute | solution.py:23
  990.8 14.0 collective-permute-start.8
  1000.4 14.6 %collective-permute-start.9 = (f32[2,12,4,128]{3,1,2,0:T(8,128)S(1)}, f32[2,12,4,128]{3,1,2,0:T(8,128)S(1)}, u32[]{:S(2)}, u32[]{:S(2)}) collective-permute-start(f32[2,12,4,128]{3,1,2,0:T(8,128)S(1)} %get-tuple-element.1627), channel_id=1, source_target_pairs={{0,2},{2,4},{4,6},{6,8},{8,10},{10,12},{12,14},{14,0},{1,3},{3,5},... | collective-permute-start | bytes 147464 | tf_op jit(solution)/shard_map/while/body/eval_jaxpr/ppermute | solution.py:23
  1015.7 11.4 collective-permute-start.10
  1064.3 15.2 %collective-permute-start.7 = (f32[2,4,32,128]{3,1,2,0:T(4,128)S(1)}, f32[2,4,32,128]{3,1,2,0:T(4,128)S(1)}, u32[]{:S(2)}, u32[]{:S(2)}) collective-permute-start(f32[2,4,32,128]{3,1,2,0:T(4,128)S(1)} %pad_maximum_fusion.28), channel_id=1, source_target_pairs={{0,16},{16,32},{32,48},{48,64},{64,80},{80,96},{96,112},{112,128},... | collective-permute-start | bytes 393224 | tf_op jit(solution)/shard_map/while/body/eval_jaxpr/ppermute | solution.py:23
  1079.5 14.0 collective-permute-start.8
  1084.4 14.6 %collective-permute-start.9 = (f32[2,12,4,128]{3,1,2,0:T(8,128)S(1)}, f32[2,12,4,128]{3,1,2,0:T(8,128)S(1)}, u32[]{:S(2)}, u32[]{:S(2)}) collective-permute-start(f32[2,12,4,128]{3,1,2,0:T(8,128)S(1)} %get-tuple-element.1627), channel_id=1, source_target_pairs={{0,2},{2,4},{4,6},{6,8},{8,10},{10,12},{12,14},{14,0},{1,3},{3,5},... | collective-permute-start | bytes 147464 | tf_op jit(solution)/shard_map/while/body/eval_jaxpr/ppermute | solution.py:23
  1099.6 11.4 collective-permute-start.10
  1148.2 17.0 %collective-permute-start.7 = (f32[2,4,32,128]{3,1,2,0:T(4,128)S(1)}, f32[2,4,32,128]{3,1,2,0:T(4,128)S(1)}, u32[]{:S(2)}, u32[]{:S(2)}) collective-permute-start(f32[2,4,32,128]{3,1,2,0:T(4,128)S(1)} %pad_maximum_fusion.28), channel_id=1, source_target_pairs={{0,16},{16,32},{32,48},{48,64},{64,80},{80,96},{96,112},{112,128},... | collective-permute-start | bytes 393224 | tf_op jit(solution)/shard_map/while/body/eval_jaxpr/ppermute | solution.py:23
  1165.3 14.0 collective-permute-start.8
  1172.1 14.6 %collective-permute-start.9 = (f32[2,12,4,128]{3,1,2,0:T(8,128)S(1)}, f32[2,12,4,128]{3,1,2,0:T(8,128)S(1)}, u32[]{:S(2)}, u32[]{:S(2)}) collective-permute-start(f32[2,12,4,128]{3,1,2,0:T(8,128)S(1)} %get-tuple-element.1627), channel_id=1, source_target_pairs={{0,2},{2,4},{4,6},{6,8},{8,10},{10,12},{12,14},{14,0},{1,3},{3,5},... | collective-permute-start | bytes 147464 | tf_op jit(solution)/shard_map/while/body/eval_jaxpr/ppermute | solution.py:23
  1236.9 14.9 %collective-permute-start.7 = (f32[2,4,32,128]{3,1,2,0:T(4,128)S(1)}, f32[2,4,32,128]{3,1,2,0:T(4,128)S(1)}, u32[]{:S(2)}, u32[]{:S(2)}) collective-permute-start(f32[2,4,32,128]{3,1,2,0:T(4,128)S(1)} %pad_maximum_fusion.28), channel_id=1, source_target_pairs={{0,16},{16,32},{32,48},{48,64},{64,80},{80,96},{96,112},{112,128},... | collective-permute-start | bytes 393224 | tf_op jit(solution)/shard_map/while/body/eval_jaxpr/ppermute | solution.py:23
  1251.8 14.0 collective-permute-start.8
  1257.2 14.6 %collective-permute-start.9 = (f32[2,12,4,128]{3,1,2,0:T(8,128)S(1)}, f32[2,12,4,128]{3,1,2,0:T(8,128)S(1)}, u32[]{:S(2)}, u32[]{:S(2)}) collective-permute-start(f32[2,12,4,128]{3,1,2,0:T(8,128)S(1)} %get-tuple-element.1627), channel_id=1, source_target_pairs={{0,2},{2,4},{4,6},{6,8},{8,10},{10,12},{12,14},{14,0},{1,3},{3,5},... | collective-permute-start | bytes 147464 | tf_op jit(solution)/shard_map/while/body/eval_jaxpr/ppermute | solution.py:23
  1272.5 11.4 collective-permute-start.10
  1321.1 15.2 %collective-permute-start.7 = (f32[2,4,32,128]{3,1,2,0:T(4,128)S(1)}, f32[2,4,32,128]{3,1,2,0:T(4,128)S(1)}, u32[]{:S(2)}, u32[]{:S(2)}) collective-permute-start(f32[2,4,32,128]{3,1,2,0:T(4,128)S(1)} %pad_maximum_fusion.28), channel_id=1, source_target_pairs={{0,16},{16,32},{32,48},{48,64},{64,80},{80,96},{96,112},{112,128},... | collective-permute-start | bytes 393224 | tf_op jit(solution)/shard_map/while/body/eval_jaxpr/ppermute | solution.py:23
  1336.3 14.0 collective-permute-start.8
  1344.4 14.6 %collective-permute-start.9 = (f32[2,12,4,128]{3,1,2,0:T(8,128)S(1)}, f32[2,12,4,128]{3,1,2,0:T(8,128)S(1)}, u32[]{:S(2)}, u32[]{:S(2)}) collective-permute-start(f32[2,12,4,128]{3,1,2,0:T(8,128)S(1)} %get-tuple-element.1627), channel_id=1, source_target_pairs={{0,2},{2,4},{4,6},{6,8},{8,10},{10,12},{12,14},{14,0},{1,3},{3,5},... | collective-permute-start | bytes 147464 | tf_op jit(solution)/shard_map/while/body/eval_jaxpr/ppermute | solution.py:23
  (156 other events, 1863.3 us)
where the time goes:
time: 1420 us; the launch traced here: 1410 us
  starting transfers between devices  462 us (33%)
  waiting for transfers between devices  336 us (24%)
  other arithmetic  331 us (23%)
  local copies, waits for them, and re-layouts  109 us (8%)
  blocking collectives  106 us (7%)
  loops' own time  67.2 us (5%)
    ppermute x51, waiting for transfers between devices, with_halo(): lax.ppermute(lax.slice_in_dim(block, block.shape[dim] - width, None, axis...  318 us
    ppermute x51, starting transfers between devices, with_halo(): lax.ppermute(lax.slice_in_dim(block, 0, width, axis=dim), axis, backward)  250 us
    ppermute x51, starting transfers between devices, with_halo(): lax.ppermute(lax.slice_in_dim(block, block.shape[dim] - width, None, axis...  212 us
    scatter-add x8, other arithmetic, adjoint_pair(): wide = wide.at[outer_x, outer_y, outer_z].add(inject) * keep_two  124 us
    scatter-add x8, other arithmetic, adjoint_pair(): second = second.at[clip_x, clip_y, clip_z].add(inject_next)  123 us
    psum x5, blocking collectives, by_axis(): x = lax.psum(x, axis)  104 us
    gather x16, local copies, waits for them, and re-layouts, sample_row(): values = field[clip_x, clip_y, clip_z] * inside  37.9 us
    another operation x1, loops' own time, on_device(): lax.fori_loop(0, steps // 2, forward_pair, (zeros, zeros, record))  33.6 us
  transfers between devices with their start and end apart: 102, of which 53 were waited for; matrix products, arithmetic and copies ran while one was open for 3% of the time, Pallas kernels for 0%

commit v1 on v0

v1 whole, which is shorter than its diff:
```python
import functools

import jax
import jax.numpy as jnp
from jax import lax
from jax.experimental import pallas as pl
from jax.experimental.pallas import tpu as pltpu
from jax.sharding import Mesh
from jax.sharding import PartitionSpec as P

AXES = ("zl", "x", "y", "zh", "c")
SIZES = (8, 4, 4, 2, 2)
B = 8
R = 3 * B
PAD = 8
NT = 16
near_coef = 4.0 / 3.0
far_coef = -1.0 / 12.0
center_coef = -7.5


def linear(x, y, z, c):
    return ((((z % 8) * 4 + x) * 4 + y) * 2 + z // 8) * 2 + c


def table(place):
    out = []
    for x in range(4):
        for y in range(4):
            for z in range(16):
                for c in range(2):
                    out.append((linear(x, y, z, c), linear(*place(x, y, z, c))))
    return sorted(out)


def shifted(dx=0, dy=0, dz=0, dc=0):
    return table(lambda x, y, z, c: ((x + dx) % 4, (y + dy) % 4, (z + dz) % 16, (c + dc) % 2))


def spread(other):
    def place(x, y, z, c):
        zl, zh = z % 8, z // 8
        return (2 * zh + ((x & 1) ^ other), y, 2 * zl + (x >> 1), c)

    return table(place)


def across(x, y, z, c):
    index = (4 * y + x + (1 if c else -1)) % 16
    return (index % 4, index // 4, z, 1 - c)


SWAP = shifted(dc=1)
ACROSS = table(across)
UP = shifted(dz=1)
DOWN = shifted(dz=-1)


def send(value, pairs):
    return lax.ppermute(value, AXES, pairs)


def back(pairs):
    return sorted((target, source) for source, target in pairs)


def lane_ids():
    return lax.broadcasted_iota(jnp.int32, (8, 128), 1)


def laplace_tile(buf, x, row):
    lane = lane_ids()
    here, near, far = [], [], []
    for half in range(2):
        here.append(buf[x, half, row : row + 8, :])
        near.append(
            (buf[x - 1, half, row : row + 8, :] + buf[x + 1, half, row : row + 8, :])
            + (buf[x, half, row - 1 : row + 7, :] + buf[x, half, row + 1 : row + 9, :])
        )
        far.append(
            (buf[x - 2, half, row : row + 8, :] + buf[x + 2, half, row : row + 8, :])
            + (buf[x, half, row - 2 : row + 6, :] + buf[x, half, row + 2 : row + 10, :])
        )
    low, high = here
    up1 = [pltpu.roll(v, 127, 1) for v in here]
    up2 = [pltpu.roll(v, 126, 1) for v in here]
    dn1 = [pltpu.roll(v, 1, 1) for v in here]
    dn2 = [pltpu.roll(v, 2, 1) for v in here]
    near[0] += jnp.where(lane < 127, up1[0], up1[1]) + jnp.where(lane >= 1, dn1[0], 0.0)
    near[1] += jnp.where(lane < 127, up1[1], 0.0) + jnp.where(lane >= 1, dn1[1], dn1[0])
    far[0] += jnp.where(lane < 126, up2[0], up2[1]) + jnp.where(lane >= 2, dn2[0], 0.0)
    far[1] += jnp.where(lane < 126, up2[1], 0.0) + jnp.where(lane >= 2, dn2[1], dn2[0])
    return here, [
        near_coef * near[h] + far_coef * far[h] + center_coef * here[h] for h in range(2)
    ]


def tiles_for(margin):
    return (PAD, PAD + 8, PAD + 16) if margin > 0 else (PAD + 8,)


def assemble(buf, f, mid, inter, intra, core):
    buf[:, :, PAD + 8 : PAD + 16, :] = mid[f]

    @pl.when(core == 0)
    def _():
        buf[:, :, PAD : PAD + 8, :] = inter[f]
        buf[:, :, PAD + 16 : PAD + 24, :] = intra[f]

    @pl.when(core == 1)
    def _():
        buf[:, :, PAD : PAD + 8, :] = intra[f]
        buf[:, :, PAD + 16 : PAD + 24, :] = inter[f]


def own(buf):
    return buf[B : 2 * B, :, PAD + 8 : PAD + 16, :]


def sample(buf, step, place, receivers, mine, counts, traces):
    lane = lax.broadcasted_iota(jnp.int32, (1, 128), 1)
    lanes = lax.broadcasted_iota(jnp.int32, (1, 256), 1)

    def body(i, _):
        r = mine[i]
        x = receivers[0, r] - place[0] + B
        y = receivers[1, r] - place[1] + PAD + 8
        z = receivers[2, r]
        row = buf[x, z // 128, pl.ds(y, 1), :]
        value = jnp.sum(jnp.where(lane == z % 128, row, 0.0))
        traces[step : step + 1, :] = jnp.where(lanes == r, value, traces[step : step + 1, :])
        return 0

    lax.fori_loop(0, counts[0], body, 0)


def forward_steps(steps, a, b, vel, src, place, checkpoints, receivers, mine, counts, traces):
    for done, step in enumerate(steps):
        margin = 2 * (len(steps) - 1 - done)
        ck = checkpoints[step]

        def plane(x, _, a=a, b=b, margin=margin, ck=ck):
            for row in tiles_for(margin):
                here, lap = laplace_tile(b, x, row)
                for half in range(2):
                    at = (x, half, slice(row, row + 8), slice(None))
                    cell = (x, half, slice(row - PAD, row - PAD + 8), slice(None))
                    a[at] = (
                        2.0 * here[half] - a[at] + vel[cell] * lap[half] + src[(ck, *cell)]
                    )
            return 0

        lax.fori_loop(B - margin, 2 * B + margin, plane, 0)
        a, b = b, a
        sample(b, step, place, receivers, mine, counts, traces)
    return a, b


def first_forward(
    place, checkpoints, receivers, mine, counts, mid, inter, intra, vel, src, pair, traces, a, b
):
    core = place[2]
    for f in range(5):
        into = vel if f == 0 else src.at[f - 1]
        into[:, :, 8:16, :] = mid[f]

        @pl.when(core == 0)
        def _():
            into[:, :, 0:8, :] = inter[f]
            into[:, :, 16:24, :] = intra[f]

        @pl.when(core == 1)
        def _():
            into[:, :, 0:8, :] = intra[f]
            into[:, :, 16:24, :] = inter[f]

    traces[...] = jnp.zeros_like(traces)
    a[...] = jnp.zeros_like(a)
    b[:, :, PAD : PAD + R, :] = src[checkpoints[0]]
    sample(b, 0, place, receivers, mine, counts, traces)
    prev, cur = forward_steps(
        range(1, 5), a, b, vel, src, place, checkpoints, receivers, mine, counts, traces
    )
    pair[0] = own(prev)
    pair[1] = own(cur)


def later_forward(
    steps, place, checkpoints, receivers, mine, counts, vel, src, mid, inter, intra, held,
    pair, traces, a, b,
):
    assemble(a, 0, mid, inter, intra, place[2])
    assemble(b, 1, mid, inter, intra, place[2])
    traces[...] = held[...]
    prev, cur = forward_steps(
        steps, a, b, vel, src, place, checkpoints, receivers, mine, counts, traces
    )
    pair[0] = own(prev)
    pair[1] = own(cur)


def inject(buf, step, place, receivers, near, counts, traces):
    lane = lax.broadcasted_iota(jnp.int32, (1, 128), 1)

    def body(i, _):
        r = near[i]
        x = (receivers[0, r] - place[0] + B) & 127
        y = ((receivers[1, r] - place[1] + B) & 255) + PAD
        z = receivers[2, r]
        half = z // 128
        row = buf[x, half, pl.ds(y, 1), :]
        buf[x, half, pl.ds(y, 1), :] = row + jnp.where(lane == z % 128, traces[step, r], 0.0)
        return 0

    lax.fori_loop(0, counts[1], body, 0)


def add_image(image, buf, back_own, ck):
    image[...] += own(buf) * back_own[ck]


def adjoint_steps(
    steps, a, b, w, vel, back_own, place, checkpoints, receivers, near, counts, traces, image
):
    for done, step in enumerate(steps):
        margin = 2 * (len(steps) - 1 - done)

        def scale(x, _, b=b):
            for row in tiles_for(1):
                for half in range(2):
                    at = (x, half, slice(row, row + 8), slice(None))
                    w[at] = b[at] * vel[x, half, row - PAD : row - PAD + 8, :]
            return 0

        lax.fori_loop(B - margin - 2, 2 * B + margin + 2, scale, 0)

        def plane(x, _, a=a, b=b, margin=margin):
            for row in tiles_for(margin):
                _, lap = laplace_tile(w, x, row)
                for half in range(2):
                    at = (x, half, slice(row, row + 8), slice(None))
                    a[at] = 2.0 * b[at] - a[at] + lap[half]
            return 0

        lax.fori_loop(B - margin, 2 * B + margin, plane, 0)
        a, b = b, a
        inject(b, step, place, receivers, near, counts, traces)
        add_image(image, b, back_own, checkpoints[step])
    return a, b


def first_adjoint(
    place, checkpoints, receivers, near, counts, traces, vel, back_own, pair, image, a, b, w
):
    a[...] = jnp.zeros_like(a)
    b[...] = jnp.zeros_like(b)
    image[...] = jnp.zeros_like(image)
    inject(b, NT - 1, place, receivers, near, counts, traces)
    add_image(image, b, back_own, checkpoints[NT - 1])
    later, now = adjoint_steps(
        range(14, 10, -1), a, b, w, vel, back_own, place, checkpoints, receivers, near, counts,
        traces, image,
    )
    pair[0] = own(later)
    pair[1] = own(now)


def later_adjoint(
    steps, place, checkpoints, receivers, near, counts, traces, vel, back_own, mid, inter, intra,
    held, pair, image, a, b, w,
):
    assemble(a, 0, mid, inter, intra, place[2])
    assemble(b, 1, mid, inter, intra, place[2])
    image[...] = held[...]
    later, now = adjoint_steps(
        steps, a, b, w, vel, back_own, place, checkpoints, receivers, near, counts, traces, image
    )
    pair[0] = own(later)
    pair[1] = own(now)


def list_receivers(place, receivers, mine, near, counts):
    counts[0] = 0
    counts[1] = 0

    def body(r, _):
        x = (receivers[0, r] - place[0] + B) & 127
        y = (receivers[1, r] - place[1] + B) & 255

        @pl.when((x < R) & (y < R))
        def _():
            n = counts[1]
            near[n] = r
            counts[1] = n + 1

            @pl.when((x >= B) & (x < 2 * B) & (y >= B) & (y < 2 * B))
            def _():
                m = counts[0]
                mine[m] = r
                counts[0] = m + 1

        return 0

    lax.fori_loop(0, 256, body, 0)


SM = pl.BlockSpec(memory_space=pltpu.SMEM)
VM = pl.BlockSpec(memory_space=pltpu.VMEM)
FIELD = (R, 2, R + 2 * PAD, 128)


def f32(*shape):
    return jax.ShapeDtypeStruct(shape, jnp.float32)


def i32(*shape):
    return jax.ShapeDtypeStruct(shape, jnp.int32)


def call(body, ins, outs, out_specs, fields):
    return pl.pallas_call(
        body,
        in_specs=ins,
        out_specs=out_specs,
        out_shape=outs,
        scratch_shapes=[pltpu.VMEM(FIELD, jnp.float32)] * fields,
        compiler_params=pltpu.CompilerParams(vmem_limit_bytes=48 * 1024 * 1024),
    )


def exchange(block):
    low = send(block, UP)
    high = send(block, DOWN)
    mid = jnp.concatenate([low, block, high], axis=1)
    return mid, send(mid, ACROSS), send(mid, SWAP)


def pick(two, index):
    return jnp.where(index == 0, two[0], two[1])


def ordered(first, second, index, axis):
    return jnp.where(
        index == 0, jnp.stack([first, second], axis), jnp.stack([second, first], axis)
    )


def inward(stacked, core, odd):
    count = stacked.shape[0]
    rows = stacked.reshape(count, 4, 2, 2, 8, 128)
    even, uneven = rows[:, :, :, 0], rows[:, :, :, 1]
    kept = pick((even, uneven), core)
    came = send(pick((uneven, even), core), SWAP)
    whole = ordered(kept, came, core, 3)
    first, second = whole[:, :, 0], whole[:, :, 1]
    got = send(pick((first, second), odd), spread(0))
    other = send(pick((second, first), odd), spread(1))
    return ordered(got, other, odd, 1).reshape(count, 8, 2, 8, 128)


def outward(block, core, odd):
    first, second = block[:4], block[4:]
    got = send(pick((first, second), odd), back(spread(0)))
    other = send(pick((second, first), odd), back(spread(1)))
    whole = ordered(got, other, odd, 1)
    front, rear = whole[:, :, 0], whole[:, :, 1]
    kept = pick((front, rear), core)
    came = send(pick((rear, front), core), SWAP)
    return ordered(kept, came, core, 2).reshape(4, 32, 128)


def merge(*parts):
    total = parts[0]
    for part in parts[1:]:
        total = jnp.where(total == 0.0, part, total)
    return total


def on_device(velocity_term, model_step, background, receivers, checkpoints):
    core = lax.axis_index("c")
    x = lax.axis_index("x")
    y = lax.axis_index("y")
    z = lax.axis_index("zh") * 8 + lax.axis_index("zl")
    odd = x & 1
    place = jnp.stack([B * z, 16 * (4 * y + x) + B * core, core, core]).astype(jnp.int32)
    mine, near, counts = pl.pallas_call(
        list_receivers,
        in_specs=[SM, SM],
        out_specs=[SM, SM, SM],
        out_shape=[i32(256), i32(256), i32(2)],
    )(place, receivers)
    stacked = jnp.concatenate(
        [velocity_term[None], model_step[None], background.astype(jnp.float32)], axis=0
    )
    inner = inward(stacked, core, odd)
    back_own = inner[2:]
    fields = jnp.concatenate([inner[:1], inner[1:2] * back_own], axis=0)
    vel, src, pair, traces = call(
        first_forward,
        [SM] * 5 + [VM] * 3,
        [f32(R, 2, R, 128), f32(4, R, 2, R, 128), f32(2, B, 2, B, 128), f32(NT, 256)],
        [VM] * 4,
        2,
    )(place, checkpoints, receivers, mine, counts, *exchange(fields))
    for steps in (range(5, 9), range(9, 13), range(13, 16)):
        pair, traces = call(
            functools.partial(later_forward, steps),
            [SM] * 5 + [VM] * 6,
            [f32(2, B, 2, B, 128), f32(NT, 256)],
            [VM] * 2,
            2,
        )(place, checkpoints, receivers, mine, counts, vel, src, *exchange(pair), traces)
    wavefield = outward(pair[1], core, odd)
    traces = merge(traces, send(traces, UP), send(traces, DOWN))
    traces = merge(traces, send(traces, ACROSS), send(traces, SWAP))
    local = traces
    traces = merge(traces, send(traces, shifted(dz=3)), send(traces, shifted(dz=-3)))
    traces = merge(traces, send(traces, shifted(dz=8)))
    traces = merge(traces, send(traces, shifted(dx=1)))
    traces = merge(traces, send(traces, shifted(dx=2)))
    traces = merge(traces, send(traces, shifted(dy=1)))
    traces = merge(traces, send(traces, shifted(dy=2)))
    scalars = (place, checkpoints, receivers, near, counts, local)
    pair, image = call(
        first_adjoint,
        [SM] * 6 + [VM] * 2,
        [f32(2, B, 2, B, 128), f32(B, 2, B, 128)],
        [VM] * 2,
        3,
    )(*scalars, vel, back_own)
    for steps in (range(10, 6, -1), range(6, 2, -1), range(2, -1, -1)):
        pair, image = call(
            functools.partial(later_adjoint, steps),
            [SM] * 6 + [VM] * 6,
            [f32(2, B, 2, B, 128), f32(B, 2, B, 128)],
            [VM] * 2,
            3,
        )(*scalars, vel, back_own, *exchange(pair), image)
    image = outward(image, core, odd)
    column_image = lax.psum(jnp.sum(image, axis=2), "c") / 256.0
    return (image, traces, column_image, wavefield)


def solution(mesh):
    torus = Mesh(mesh.devices.reshape(SIZES), AXES)
    across_x, across_y = ("zl", "x"), ("y", "zh")
    return jax.shard_map(
        on_device,
        mesh=torus,
        in_specs=(
            P(across_x, across_y, "c"),
            P(across_x, across_y, "c"),
            P(None, across_x, across_y, "c"),
            P(),
            P(),
        ),
        out_specs=(
            P(across_x, across_y, "c"),
            P(),
            P(across_x, across_y),
            P(across_x, across_y, "c"),
        ),
        check_vma=False,
    )
```

time: 1420 us -> 366 us (0.26)
  the two profiles are of different devices: /device:TPU:9 before, /device:TPU:213 now
where the time goes in v1:
time: 366 us; the launch traced here: 365 us
  starting transfers between devices  185 us (51%)
  waiting for transfers between devices  108 us (30%)
  Pallas kernels  59.5 us (16%)
  other arithmetic  4.08 us (1%)
    ppermute x48, starting transfers between devices, send(): return lax.ppermute(value, AXES, pairs)  185 us
    ppermute x48, waiting for transfers between devices, send(): return lax.ppermute(value, AXES, pairs)  108 us
    pallas_call x3, Pallas kernels, on_device(): call(functools.partial(later_adjoint, steps), [SM] * 6 + [VM] * 6, [f32(2...  21.5 us
    pallas_call x3, Pallas kernels, on_device(): call(functools.partial(later_forward, steps), [SM] * 5 + [VM] * 6, [f32(2...  17 us
    pallas_call x1, Pallas kernels, on_device(): call(first_adjoint, [SM] * 6 + [VM] * 2, [f32(2, B, 2, B, 128), f32(B, 2,...  8.03 us
  transfers between devices with their start and end apart: 48, of which 27 were waited for; matrix products, arithmetic and copies ran while one was open for 1% of the time, Pallas kernels for 8%

profile of v1, /device:TPU:213, one launch (start us, length us, event | category | flops | bytes accessed | tf_op | source)
XLA Modules:
  0.0 364.8 jit_solution(10910583903105825418)
XLA Ops:
  2.5 2.6 collective-permute-start
  6.3 8.3 %collective-permute-start.1 = (f32[6,4,2,8,128]{4,3,2,1,0:T(8,128)S(1)}, f32[6,4,2,8,128]{4,3,2,1,0:T(8,128)S(1)}, u32[]{:S(2)}, u32[]{:S(2)}) collective-permute-start(f32[6,4,2,8,128]{4,3,2,1,0:T(8,128)S(1)} %get-tuple-element.48), channel_id=1, source_target_pairs={{0,0},{1,1},{2,32},{3,33},{4,4},{5,5},{6,36},{7,37},{8,8},{9,9},{1... | collective-permute-start | bytes 589832 | tf_op jit(solution)/shard_map/ppermute | solution.py:60
  14.6 6.3 %collective-permute-start.2 = (f32[6,4,2,8,128]{4,3,2,1,0:T(8,128)S(1)}, f32[6,4,2,8,128]{4,3,2,1,0:T(8,128)S(1)}, u32[]{:S(2)}, u32[]{:S(2)}) collective-permute-start(f32[6,4,2,8,128]{4,3,2,1,0:T(8,128)S(1)} %get-tuple-element.49), channel_id=1, source_target_pairs={{0,16},{1,17},{2,48},{3,49},{4,20},{5,21},{6,52},{7,53},{8,24},{9,... | collective-permute-start | bytes 589832 | tf_op jit(solution)/shard_map/ppermute | solution.py:60
  20.9 24.9 %collective-permute-done.1 = f32[6,4,2,8,128]{4,3,2,1,0:T(8,128)S(1)} collective-permute-done((f32[6,4,2,8,128]{4,3,2,1,0:T(8,128)S(1)}, f32[6,4,2,8,128]{4,3,2,1,0:T(8,128)S(1)}, u32[]{:S(2)}, u32[]{:S(2)}) %collective-permute-start.1) | collective-permute-done | bytes 196640 | tf_op jit(solution)/shard_map/ppermute | solution.py:60
  45.8 4.2 %collective-permute-done.2 = f32[6,4,2,8,128]{4,3,2,1,0:T(8,128)S(1)} collective-permute-done((f32[6,4,2,8,128]{4,3,2,1,0:T(8,128)S(1)}, f32[6,4,2,8,128]{4,3,2,1,0:T(8,128)S(1)}, u32[]{:S(2)}, u32[]{:S(2)}) %collective-permute-start.2) | collective-permute-done | bytes 196640 | tf_op jit(solution)/shard_map/ppermute | solution.py:60
  52.1 3.4 collective-permute-start.3
  55.5 5.4 %collective-permute-done.4 = f32[5,8,2,8,128]{4,3,2,1,0:T(8,128)S(1)} collective-permute-done((f32[5,8,2,8,128]{4,3,2,1,0:T(8,128)S(1)}, f32[5,8,2,8,128]{4,3,2,1,0:T(8,128)S(1)}, u32[]{:S(2)}, u32[]{:S(2)}) %collective-permute-start.4) | collective-permute-done | bytes 327712 | tf_op jit(solution)/shard_map/ppermute | solution.py:60
  62.9 3.2 collective-permute-start.6
  66.2 2.2 collective-permute-start.5
  69.0 6.4 %shard_map.84 = (s32[256]{0:T(256)}, s32[256]{0:T(256)}, s32[2]{0:T(128)}) custom-call(s32[4]{0:T(128)} %pad_add_fusion.place, s32[3,256]{1,0:T(4,128)} %receivers.17), custom_call_target="tpu_custom_call" | custom-call | tf_op jit(solution)/shard_map/pallas_call | solution.py:386
  75.4 6.2 %collective-permute-done.5.inter = f32[5,24,2,8,128]{4,3,2,1,0:T(8,128)S(1)} collective-permute-done((f32[5,24,2,8,128]{4,3,2,1,0:T(8,128)S(1)}, f32[5,24,2,8,128]{4,3,2,1,0:T(8,128)S(1)}, u32[]{:S(2)}, u32[]{:S(2)}) %collective-permute-start.5) | collective-permute-done | bytes 983072 | tf_op jit(solution)/shard_map/ppermute | solution.py:60
  83.6 6.6 %shard_map.85 = (f32[24,2,24,128]{3,2,1,0:T(8,128)S(1)}, f32[4,24,2,24,128]{4,3,2,1,0:T(8,128)S(1)}, f32[2,8,2,8,128]{4,3,2,1,0:T(8,128)S(1)}, f32[16,256]{1,0:T(8,128)S(1)}) custom-call(s32[4]{0:T(128)S(1)} %copy-done.1, s32[16]{0:T(128)S(1)} %copy-done.2, s32[3,256]{1,0:T(4,128)S(1)} %copy-done, s32[256]{0:T(256)S(1)} %copy-done.5, s32[2]{0:T(128)S(1)} %copy-done.3, ...), custom_call_target="tpu_custom_call" | custom-call | tf_op jit(solution)/shard_map/pallas_call | solution.py:398
  90.1 4.0 %collective-permute-start.7 = (f32[2,8,2,8,128]{4,3,2,1,0:T(8,128)S(1)}, f32[2,8,2,8,128]{4,3,2,1,0:T(8,128)S(1)}, u32[]{:S(2)}, u32[]{:S(2)}) collective-permute-start(f32[2,8,2,8,128]{4,3,2,1,0:T(8,128)S(1)} %get-tuple-element.29), channel_id=1, source_target_pairs={{0,64},{1,65},{2,66},{3,67},{4,68},{5,69},{6,70},{7,71},{8,72},{9,... | collective-permute-start | bytes 393224 | tf_op jit(solution)/shard_map/ppermute | solution.py:60
  97.3 4.2 %collective-permute-done.8 = f32[2,8,2,8,128]{4,3,2,1,0:T(8,128)S(1)} collective-permute-done((f32[2,8,2,8,128]{4,3,2,1,0:T(8,128)S(1)}, f32[2,8,2,8,128]{4,3,2,1,0:T(8,128)S(1)}, u32[]{:S(2)}, u32[]{:S(2)}) %collective-permute-start.8) | collective-permute-done | bytes 131104 | tf_op jit(solution)/shard_map/ppermute | solution.py:60
  101.5 2.4 collective-permute-start.10
  103.9 2.5 collective-permute-start.9
  106.4 6.6 %collective-permute-done.9.inter = f32[2,24,2,8,128]{4,3,2,1,0:T(8,128)S(1)} collective-permute-done((f32[2,24,2,8,128]{4,3,2,1,0:T(8,128)S(1)}, f32[2,24,2,8,128]{4,3,2,1,0:T(8,128)S(1)}, u32[]{:S(2)}, u32[]{:S(2)}) %collective-permute-start.9) | collective-permute-done | bytes 393248 | tf_op jit(solution)/shard_map/ppermute | solution.py:60
  113.0 6.3 %shard_map.86 = (f32[2,8,2,8,128]{4,3,2,1,0:T(8,128)S(1)}, f32[16,256]{1,0:T(8,128)S(1)}) custom-call(s32[4]{0:T(128)S(1)} %copy-done.1, s32[16]{0:T(128)S(1)} %copy-done.2, s32[3,256]{1,0:T(4,128)S(1)} %copy-done, s32[256]{0:T(256)S(1)} %copy-done.5, s32[2]{0:T(128)S(1)} %copy-done.3, f32[24,2,24,128]{3,2,1,0:T(8,128)S(1)} %get-tuple-element.27.vel, ...), custom_call_target="tpu_custom_call" | custom-call | tf_op jit(solution)/shard_map/pallas_call | solution.py:406
  119.3 4.9 %collective-permute-start.11 = (f32[2,8,2,8,128]{4,3,2,1,0:T(8,128)S(1)}, f32[2,8,2,8,128]{4,3,2,1,0:T(8,128)S(1)}, u32[]{:S(2)}, u32[]{:S(2)}) collective-permute-start(f32[2,8,2,8,128]{4,3,2,1,0:T(8,128)S(1)} %get-tuple-element.31), channel_id=1, source_target_pairs={{0,64},{1,65},{2,66},{3,67},{4,68},{5,69},{6,70},{7,71},{8,72},{9,... | collective-permute-start | bytes 393224 | tf_op jit(solution)/shard_map/ppermute | solution.py:60
  127.5 3.9 %collective-permute-done.12 = f32[2,8,2,8,128]{4,3,2,1,0:T(8,128)S(1)} collective-permute-done((f32[2,8,2,8,128]{4,3,2,1,0:T(8,128)S(1)}, f32[2,8,2,8,128]{4,3,2,1,0:T(8,128)S(1)}, u32[]{:S(2)}, u32[]{:S(2)}) %collective-permute-start.12) | collective-permute-done | bytes 131104 | tf_op jit(solution)/shard_map/ppermute | solution.py:60
  131.4 2.5 collective-permute-start.14
  134.0 2.7 collective-permute-start.13
  136.7 6.3 %collective-permute-done.13.inter = f32[2,24,2,8,128]{4,3,2,1,0:T(8,128)S(1)} collective-permute-done((f32[2,24,2,8,128]{4,3,2,1,0:T(8,128)S(1)}, f32[2,24,2,8,128]{4,3,2,1,0:T(8,128)S(1)}, u32[]{:S(2)}, u32[]{:S(2)}) %collective-permute-start.13) | collective-permute-done | bytes 393248 | tf_op jit(solution)/shard_map/ppermute | solution.py:60
  143.1 6.3 %shard_map.87 = (f32[2,8,2,8,128]{4,3,2,1,0:T(8,128)S(1)}, f32[16,256]{1,0:T(8,128)S(1)}) custom-call(s32[4]{0:T(128)S(1)} %copy-done.1, s32[16]{0:T(128)S(1)} %copy-done.2, s32[3,256]{1,0:T(4,128)S(1)} %copy-done, s32[256]{0:T(256)S(1)} %copy-done.5, s32[2]{0:T(128)S(1)} %copy-done.3, f32[24,2,24,128]{3,2,1,0:T(8,128)S(1)} %get-tuple-element.27.vel, ...), custom_call_target="tpu_custom_call" | custom-call | tf_op jit(solution)/shard_map/pallas_call | solution.py:406
  149.4 3.6 collective-permute-start.15
  156.3 3.8 %collective-permute-done.16 = f32[2,8,2,8,128]{4,3,2,1,0:T(8,128)S(1)} collective-permute-done((f32[2,8,2,8,128]{4,3,2,1,0:T(8,128)S(1)}, f32[2,8,2,8,128]{4,3,2,1,0:T(8,128)S(1)}, u32[]{:S(2)}, u32[]{:S(2)}) %collective-permute-start.16) | collective-permute-done | bytes 131104 | tf_op jit(solution)/shard_map/ppermute | solution.py:60
  160.1 2.6 collective-permute-start.18
  162.7 4.7 %collective-permute-start.17 = (f32[2,24,2,8,128]{4,3,2,1,0:T(8,128)S(1)}, f32[2,24,2,8,128]{4,3,2,1,0:T(8,128)S(1)}, u32[]{:S(2)}, u32[]{:S(2)}) collective-permute-start(f32[2,24,2,8,128]{4,3,2,1,0:T(8,128)S(1)} %constant_dynamic-update-slice_fusion.6.mid), channel_id=1, source_target_pairs={{0,61},{1,16},{2,63},{3,18},{4,49},{5,20},{6,51},{7,22},{8,53},{9,... | collective-permute-start | bytes 1179656 | tf_op jit(solution)/shard_map/ppermute | solution.py:60
  167.4 5.4 %collective-permute-done.17.inter = f32[2,24,2,8,128]{4,3,2,1,0:T(8,128)S(1)} collective-permute-done((f32[2,24,2,8,128]{4,3,2,1,0:T(8,128)S(1)}, f32[2,24,2,8,128]{4,3,2,1,0:T(8,128)S(1)}, u32[]{:S(2)}, u32[]{:S(2)}) %collective-permute-start.17) | collective-permute-done | bytes 393248 | tf_op jit(solution)/shard_map/ppermute | solution.py:60
  172.9 4.3 %shard_map.88 = (f32[2,8,2,8,128]{4,3,2,1,0:T(8,128)S(1)}, f32[16,256]{1,0:T(8,128)S(1)}) custom-call(s32[4]{0:T(128)S(1)} %copy-done.1, s32[16]{0:T(128)S(1)} %copy-done.2, s32[3,256]{1,0:T(4,128)S(1)} %copy-done, s32[256]{0:T(256)S(1)} %copy-done.5, s32[2]{0:T(128)S(1)} %copy-done.3, f32[24,2,24,128]{3,2,1,0:T(8,128)S(1)} %get-tuple-element.27.vel, ...), custom_call_target="tpu_custom_call" | custom-call | tf_op jit(solution)/shard_map/pallas_call | solution.py:406
  177.1 5.2 %collective-permute-start.19 = (f32[16,256]{1,0:T(8,128)S(1)}, f32[16,256]{1,0:T(8,128)S(1)}, u32[]{:S(2)}, u32[]{:S(2)}) collective-permute-start(f32[16,256]{1,0:T(8,128)S(1)} %get-tuple-element.35), channel_id=1, source_target_pairs={{0,64},{1,65},{2,66},{3,67},{4,68},{5,69},{6,70},{7,71},{8,72},{9,... | collective-permute-start | bytes 49160 | tf_op jit(solution)/shard_map/ppermute | solution.py:60
  184.3 2.8 collective-permute-done.20
  187.2 4.4 %collective-permute-start.21 = (f32[16,256]{1,0:T(8,128)S(1)}, f32[16,256]{1,0:T(8,128)S(1)}, u32[]{:S(2)}, u32[]{:S(2)}) collective-permute-start(f32[16,256]{1,0:T(8,128)S(1)} %compare_select_fusion.9), channel_id=1, source_target_pairs={{0,61},{1,16},{2,63},{3,18},{4,49},{5,20},{6,51},{7,22},{8,53},{9,... | collective-permute-start | bytes 49160 | tf_op jit(solution)/shard_map/ppermute | solution.py:60
  191.6 2.1 collective-permute-start.22
  194.7 8.0 %shard_map.89 = (f32[2,8,2,8,128]{4,3,2,1,0:T(8,128)S(1)}, f32[8,2,8,128]{3,2,1,0:T(8,128)S(1)}) custom-call(s32[4]{0:T(128)S(1)} %copy-done.1, s32[16]{0:T(128)S(1)} %copy-done.2, s32[3,256]{1,0:T(4,128)S(1)} %copy-done, s32[256]{0:T(256)S(1)} %copy-done.4, s32[2]{0:T(128)S(1)} %copy-done.3, f32[16,256]{1,0:T(8,128)S(1)} %compare_select_fusion.7.traces, ...), custom_call_target="tpu_custom_call" | custom-call | tf_op jit(solution)/shard_map/pallas_call | solution.py:424
  202.7 4.2 %collective-permute-start.23 = (f32[2,8,2,8,128]{4,3,2,1,0:T(8,128)S(1)}, f32[2,8,2,8,128]{4,3,2,1,0:T(8,128)S(1)}, u32[]{:S(2)}, u32[]{:S(2)}) collective-permute-start(f32[2,8,2,8,128]{4,3,2,1,0:T(8,128)S(1)} %get-tuple-element.36), channel_id=1, source_target_pairs={{0,64},{1,65},{2,66},{3,67},{4,68},{5,69},{6,70},{7,71},{8,72},{9,... | collective-permute-start | bytes 393224 | tf_op jit(solution)/shard_map/ppermute | solution.py:60
  209.7 3.8 %collective-permute-done.24 = f32[2,8,2,8,128]{4,3,2,1,0:T(8,128)S(1)} collective-permute-done((f32[2,8,2,8,128]{4,3,2,1,0:T(8,128)S(1)}, f32[2,8,2,8,128]{4,3,2,1,0:T(8,128)S(1)}, u32[]{:S(2)}, u32[]{:S(2)}) %collective-permute-start.24) | collective-permute-done | bytes 131104 | tf_op jit(solution)/shard_map/ppermute | solution.py:60
  213.5 3.1 collective-permute-start.26
  216.6 8.2 %collective-permute-start.25 = (f32[2,24,2,8,128]{4,3,2,1,0:T(8,128)S(1)}, f32[2,24,2,8,128]{4,3,2,1,0:T(8,128)S(1)}, u32[]{:S(2)}, u32[]{:S(2)}) collective-permute-start(f32[2,24,2,8,128]{4,3,2,1,0:T(8,128)S(1)} %constant_dynamic-update-slice_fusion.9.mid), channel_id=1, source_target_pairs={{0,61},{1,16},{2,63},{3,18},{4,49},{5,20},{6,51},{7,22},{8,53},{9,... | collective-permute-start | bytes 1179656 | tf_op jit(solution)/shard_map/ppermute | solution.py:60
  224.8 9.1 %collective-permute-start.45 = (f32[4,2,8,128]{3,2,0,1:T(8,128)S(1)}, f32[4,2,8,128]{3,2,0,1:T(8,128)S(1)}, u32[]{:S(2)}, u32[]{:S(2)}) collective-permute-start(f32[4,2,8,128]{3,2,0,1:T(8,128)S(1)} %get-tuple-element.52), channel_id=1, source_target_pairs={{0,0},{1,1},{2,256},{3,257},{4,4},{5,5},{6,260},{7,261},{8,8},{9,9... | collective-permute-start | bytes 98312 | tf_op jit(solution)/shard_map/ppermute | solution.py:60
  233.9 2.4 collective-permute-start.46
  239.7 4.9 %collective-permute-start.39 = (f32[16,256]{1,0:T(8,128)S(1)}, f32[16,256]{1,0:T(8,128)S(1)}, u32[]{:S(2)}, u32[]{:S(2)}) collective-permute-start(f32[16,256]{1,0:T(8,128)S(1)} %compare_select_fusion.7.traces), channel_id=1, source_target_pairs={{0,322},{1,323},{2,320},{3,321},{4,326},{5,327},{6,324},{7,325},{8... | collective-permute-start | bytes 49160 | tf_op jit(solution)/shard_map/ppermute | solution.py:60
  244.6 2.7 collective-permute-done.46
  247.4 7.8 %shard_map.90 = (f32[2,8,2,8,128]{4,3,2,1,0:T(8,128)S(1)}, f32[8,2,8,128]{3,2,1,0:T(8,128)S(1)}) custom-call(s32[4]{0:T(128)S(1)} %copy-done.1, s32[16]{0:T(128)S(1)} %copy-done.2, s32[3,256]{1,0:T(4,128)S(1)} %copy-done, s32[256]{0:T(256)S(1)} %copy-done.4, s32[2]{0:T(128)S(1)} %copy-done.3, f32[16,256]{1,0:T(8,128)S(1)} %compare_select_fusion.7.traces, ...), custom_call_target="tpu_custom_call" | custom-call | tf_op jit(solution)/shard_map/pallas_call | solution.py:432
  257.1 5.1 %collective-permute-start.40 = (f32[16,256]{1,0:T(8,128)S(1)}, f32[16,256]{1,0:T(8,128)S(1)}, u32[]{:S(2)}, u32[]{:S(2)}) collective-permute-start(f32[16,256]{1,0:T(8,128)S(1)} %compare_select_fusion.5), channel_id=1, source_target_pairs={{0,2},{1,3},{2,0},{3,1},{4,6},{5,7},{6,4},{7,5},{8,10},{9,11},{10,... | collective-permute-start | bytes 49160 | tf_op jit(solution)/shard_map/ppermute | solution.py:60
  262.3 3.4 collective-permute-start.28
  265.7 2.5 collective-permute-done.28
  268.2 5.6 %collective-permute-start.30 = (f32[2,24,2,8,128]{4,3,2,1,0:T(8,128)S(1)}, f32[2,24,2,8,128]{4,3,2,1,0:T(8,128)S(1)}, u32[]{:S(2)}, u32[]{:S(2)}) collective-permute-start(f32[2,24,2,8,128]{4,3,2,1,0:T(8,128)S(1)} %constant_dynamic-update-slice_fusion.12.mid), channel_id=1, source_target_pairs={{0,1},{1,0},{2,3},{3,2},{4,5},{5,4},{6,7},{7,6},{8,9},{9,8},{10,11... | collective-permute-start | bytes 1179656 | tf_op jit(solution)/shard_map/ppermute | solution.py:60
  273.9 3.1 collective-permute-start.29
  277.0 8.7 %collective-permute-start.41 = (f32[16,256]{1,0:T(8,128)S(1)}, f32[16,256]{1,0:T(8,128)S(1)}, u32[]{:S(2)}, u32[]{:S(2)}) collective-permute-start(f32[16,256]{1,0:T(8,128)S(1)} %compare_select_fusion.4), channel_id=1, source_target_pairs={{0,16},{1,17},{2,18},{3,19},{4,20},{5,21},{6,22},{7,23},{8,24},{9,... | collective-permute-start | bytes 49160 | tf_op jit(solution)/shard_map/ppermute | solution.py:60
  287.7 7.8 %shard_map.91 = (f32[2,8,2,8,128]{4,3,2,1,0:T(8,128)S(1)}, f32[8,2,8,128]{3,2,1,0:T(8,128)S(1)}) custom-call(s32[4]{0:T(128)S(1)} %copy-done.1, s32[16]{0:T(128)S(1)} %copy-done.2, s32[3,256]{1,0:T(4,128)S(1)} %copy-done, s32[256]{0:T(256)S(1)} %copy-done.4, s32[2]{0:T(128)S(1)} %copy-done.3, f32[16,256]{1,0:T(8,128)S(1)} %compare_select_fusion.7.traces, ...), custom_call_target="tpu_custom_call" | custom-call | tf_op jit(solution)/shard_map/pallas_call | solution.py:432
  295.5 2.3 collective-permute-start.31
  297.8 3.3 collective-permute-start.42
  301.0 3.0 collective-permute-start.32
  304.1 2.6 collective-permute-done.32
  306.8 5.5 %collective-permute-start.34 = (f32[2,24,2,8,128]{4,3,2,1,0:T(8,128)S(1)}, f32[2,24,2,8,128]{4,3,2,1,0:T(8,128)S(1)}, u32[]{:S(2)}, u32[]{:S(2)}) collective-permute-start(f32[2,24,2,8,128]{4,3,2,1,0:T(8,128)S(1)} %constant_dynamic-update-slice_fusion.15.mid), channel_id=1, source_target_pairs={{0,1},{1,0},{2,3},{3,2},{4,5},{5,4},{6,7},{7,6},{8,9},{9,8},{10,11... | collective-permute-start | bytes 1179656 | tf_op jit(solution)/shard_map/ppermute | solution.py:60
  314.3 3.4 collective-permute-start.43
  319.2 7.3 %collective-permute-start.44 = (f32[16,256]{1,0:T(8,128)S(1)}, f32[16,256]{1,0:T(8,128)S(1)}, u32[]{:S(2)}, u32[]{:S(2)}) collective-permute-start(f32[16,256]{1,0:T(8,128)S(1)} %compare_select_fusion.1), channel_id=1, source_target_pairs={{0,8},{1,9},{2,10},{3,11},{4,12},{5,13},{6,14},{7,15},{8,0},{9,1},... | collective-permute-start | bytes 49160 | tf_op jit(solution)/shard_map/ppermute | solution.py:60
  326.5 6.0 %shard_map.92 = (f32[2,8,2,8,128]{4,3,2,1,0:T(8,128)}, f32[8,2,8,128]{3,2,1,0:T(8,128)S(1)}) custom-call(s32[4]{0:T(128)S(1)} %copy-done.1, s32[16]{0:T(128)S(1)} %copy-done.2, s32[3,256]{1,0:T(4,128)S(1)} %copy-done, s32[256]{0:T(256)S(1)} %copy-done.4, s32[2]{0:T(128)S(1)} %copy-done.3, f32[16,256]{1,0:T(8,128)S(1)} %compare_select_fusion.7.traces, ...), custom_call_target="tpu_custom_call" | custom-call | tf_op jit(solution)/shard_map/pallas_call | solution.py:432
  332.5 10.1 %collective-permute-start.35 = (f32[4,2,8,128]{3,2,1,0:T(8,128)S(1)}, f32[4,2,8,128]{3,2,1,0:T(8,128)S(1)}, u32[]{:S(2)}, u32[]{:S(2)}) collective-permute-start(f32[4,2,8,128]{3,2,1,0:T(8,128)S(1)} %get-tuple-element.56), channel_id=1, source_target_pairs={{0,0},{1,1},{2,256},{3,257},{4,4},{5,5},{6,260},{7,261},{8,8},{9,9... | collective-permute-start | bytes 98312 | tf_op jit(solution)/shard_map/ppermute | solution.py:60
  345.1 2.3 collective-permute-done.35
  347.5 8.5 %collective-permute-done.36 = f32[4,2,8,128]{3,2,1,0:T(8,128)S(1)} collective-permute-done((f32[4,2,8,128]{3,2,1,0:T(8,128)S(1)}, f32[4,2,8,128]{3,2,1,0:T(8,128)S(1)}, u32[]{:S(2)}, u32[]{:S(2)}) %collective-permute-start.36) | collective-permute-done | bytes 32800 | tf_op jit(solution)/shard_map/ppermute | solution.py:60
  356.0 4.1 %collective-permute-start.37 = (f32[4,2,8,128]{3,2,0,1:T(8,128)S(1)}, f32[4,2,8,128]{3,2,0,1:T(8,128)S(1)}, u32[]{:S(2)}, u32[]{:S(2)}) collective-permute-start(f32[4,2,8,128]{3,2,0,1:T(8,128)S(1)} %select_bitcast_fusion.6), channel_id=1, source_target_pairs={{0,1},{1,0},{2,3},{3,2},{4,5},{5,4},{6,7},{7,6},{8,9},{9,8},{10,11... | collective-permute-start | bytes 98312 | tf_op jit(solution)/shard_map/ppermute | solution.py:60
  361.1 2.5 psum.7
  (108 shorter events, 40.7 us)
Async XLA Ops:
  2.5 3.6 collective-permute-start
  6.3 39.5 %collective-permute-start.1 = (f32[6,4,2,8,128]{4,3,2,1,0:T(8,128)S(1)}, f32[6,4,2,8,128]{4,3,2,1,0:T(8,128)S(1)}, u32[]{:S(2)}, u32[]{:S(2)}) collective-permute-start(f32[6,4,2,8,128]{4,3,2,1,0:T(8,128)S(1)} %get-tuple-element.48), channel_id=1, source_target_pairs={{0,0},{1,1},{2,32},{3,33},{4,4},{5,5},{6,36},{7,37},{8,8},{9,9},{1... | collective-permute-start | bytes 589832 | tf_op jit(solution)/shard_map/ppermute | solution.py:60
  14.6 35.5 %collective-permute-start.2 = (f32[6,4,2,8,128]{4,3,2,1,0:T(8,128)S(1)}, f32[6,4,2,8,128]{4,3,2,1,0:T(8,128)S(1)}, u32[]{:S(2)}, u32[]{:S(2)}) collective-permute-start(f32[6,4,2,8,128]{4,3,2,1,0:T(8,128)S(1)} %get-tuple-element.49), channel_id=1, source_target_pairs={{0,16},{1,17},{2,48},{3,49},{4,20},{5,21},{6,52},{7,53},{8,24},{9,... | collective-permute-start | bytes 589832 | tf_op jit(solution)/shard_map/ppermute | solution.py:60
  50.0 31.5 %copy-start = (s32[3,256]{1,0:T(4,128)S(1)}, s32[3,256]{1,0:T(4,128)}, u32[]{:S(2)}) copy-start(s32[3,256]{1,0:T(4,128)} %receivers.17) | copy-start | bytes 9220
  50.1 31.5 %copy-start.2 = (s32[16]{0:T(128)S(1)}, s32[16]{0:T(128)}, u32[]{:S(2)}) copy-start(s32[16]{0:T(128)} %checkpoints.15) | copy-start | bytes 196
  50.2 10.7 %collective-permute-start.4 = (f32[5,8,2,8,128]{4,3,2,1,0:T(8,128)S(1)}, f32[5,8,2,8,128]{4,3,2,1,0:T(8,128)S(1)}, u32[]{:S(2)}, u32[]{:S(2)}) collective-permute-start(f32[5,8,2,8,128]{4,3,2,1,0:T(8,128)S(1)} %pad_maximum_fusion.2), channel_id=1, source_target_pairs={{0,450},{1,451},{2,448},{3,449},{4,454},{5,455},{6,452},{7,453},{8... | collective-permute-start | bytes 983048 | tf_op jit(solution)/shard_map/ppermute | solution.py:60
  52.1 10.7 %collective-permute-start.3 = (f32[5,8,2,8,128]{4,3,2,1,0:T(8,128)S(1)}, f32[5,8,2,8,128]{4,3,2,1,0:T(8,128)S(1)}, u32[]{:S(2)}, u32[]{:S(2)}) collective-permute-start(f32[5,8,2,8,128]{4,3,2,1,0:T(8,128)S(1)} %pad_maximum_fusion.2), channel_id=1, source_target_pairs={{0,64},{1,65},{2,66},{3,67},{4,68},{5,69},{6,70},{7,71},{8,72},{9,... | collective-permute-start | bytes 983048 | tf_op jit(solution)/shard_map/ppermute | solution.py:60
  62.9 12.5 %collective-permute-start.6 = (f32[5,24,2,8,128]{4,3,2,1,0:T(8,128)S(1)}, f32[5,24,2,8,128]{4,3,2,1,0:T(8,128)S(1)}, u32[]{:S(2)}, u32[]{:S(2)}) collective-permute-start(f32[5,24,2,8,128]{4,3,2,1,0:T(8,128)S(1)} %pad_maximum_fusion.mid), channel_id=1, source_target_pairs={{0,1},{1,0},{2,3},{3,2},{4,5},{5,4},{6,7},{7,6},{8,9},{9,8},{10,11... | collective-permute-start | bytes 2949128 | tf_op jit(solution)/shard_map/ppermute | solution.py:60
  66.2 15.4 %collective-permute-start.5 = (f32[5,24,2,8,128]{4,3,2,1,0:T(8,128)S(1)}, f32[5,24,2,8,128]{4,3,2,1,0:T(8,128)S(1)}, u32[]{:S(2)}, u32[]{:S(2)}) collective-permute-start(f32[5,24,2,8,128]{4,3,2,1,0:T(8,128)S(1)} %pad_maximum_fusion.mid), channel_id=1, source_target_pairs={{0,61},{1,16},{2,63},{3,18},{4,49},{5,20},{6,51},{7,22},{8,53},{9,... | collective-permute-start | bytes 2949128 | tf_op jit(solution)/shard_map/ppermute | solution.py:60
  81.6 0.7 copy-start.1
  82.2 0.7 copy-start.3
  82.9 0.7 copy-start.5
  90.1 7.2 %collective-permute-start.7 = (f32[2,8,2,8,128]{4,3,2,1,0:T(8,128)S(1)}, f32[2,8,2,8,128]{4,3,2,1,0:T(8,128)S(1)}, u32[]{:S(2)}, u32[]{:S(2)}) collective-permute-start(f32[2,8,2,8,128]{4,3,2,1,0:T(8,128)S(1)} %get-tuple-element.29), channel_id=1, source_target_pairs={{0,64},{1,65},{2,66},{3,67},{4,68},{5,69},{6,70},{7,71},{8,72},{9,... | collective-permute-start | bytes 393224 | tf_op jit(solution)/shard_map/ppermute | solution.py:60
  94.2 7.3 %collective-permute-start.8 = (f32[2,8,2,8,128]{4,3,2,1,0:T(8,128)S(1)}, f32[2,8,2,8,128]{4,3,2,1,0:T(8,128)S(1)}, u32[]{:S(2)}, u32[]{:S(2)}) collective-permute-start(f32[2,8,2,8,128]{4,3,2,1,0:T(8,128)S(1)} %get-tuple-element.29), channel_id=1, source_target_pairs={{0,450},{1,451},{2,448},{3,449},{4,454},{5,455},{6,452},{7,453},{8... | collective-permute-start | bytes 393224 | tf_op jit(solution)/shard_map/ppermute | solution.py:60
  101.5 4.9 %collective-permute-start.10 = (f32[2,24,2,8,128]{4,3,2,1,0:T(8,128)S(1)}, f32[2,24,2,8,128]{4,3,2,1,0:T(8,128)S(1)}, u32[]{:S(2)}, u32[]{:S(2)}) collective-permute-start(f32[2,24,2,8,128]{4,3,2,1,0:T(8,128)S(1)} %constant_dynamic-update-slice_fusion.mid), channel_id=1, source_target_pairs={{0,1},{1,0},{2,3},{3,2},{4,5},{5,4},{6,7},{7,6},{8,9},{9,8},{10,11... | collective-permute-start | bytes 1179656 | tf_op jit(solution)/shard_map/ppermute | solution.py:60
  103.9 9.1 %collective-permute-start.9 = (f32[2,24,2,8,128]{4,3,2,1,0:T(8,128)S(1)}, f32[2,24,2,8,128]{4,3,2,1,0:T(8,128)S(1)}, u32[]{:S(2)}, u32[]{:S(2)}) collective-permute-start(f32[2,24,2,8,128]{4,3,2,1,0:T(8,128)S(1)} %constant_dynamic-update-slice_fusion.mid), channel_id=1, source_target_pairs={{0,61},{1,16},{2,63},{3,18},{4,49},{5,20},{6,51},{7,22},{8,53},{9,... | collective-permute-start | bytes 1179656 | tf_op jit(solution)/shard_map/ppermute | solution.py:60
  119.3 8.2 %collective-permute-start.11 = (f32[2,8,2,8,128]{4,3,2,1,0:T(8,128)S(1)}, f32[2,8,2,8,128]{4,3,2,1,0:T(8,128)S(1)}, u32[]{:S(2)}, u32[]{:S(2)}) collective-permute-start(f32[2,8,2,8,128]{4,3,2,1,0:T(8,128)S(1)} %get-tuple-element.31), channel_id=1, source_target_pairs={{0,64},{1,65},{2,66},{3,67},{4,68},{5,69},{6,70},{7,71},{8,72},{9,... | collective-permute-start | bytes 393224 | tf_op jit(solution)/shard_map/ppermute | solution.py:60
  124.2 7.2 %collective-permute-start.12 = (f32[2,8,2,8,128]{4,3,2,1,0:T(8,128)S(1)}, f32[2,8,2,8,128]{4,3,2,1,0:T(8,128)S(1)}, u32[]{:S(2)}, u32[]{:S(2)}) collective-permute-start(f32[2,8,2,8,128]{4,3,2,1,0:T(8,128)S(1)} %get-tuple-element.31), channel_id=1, source_target_pairs={{0,450},{1,451},{2,448},{3,449},{4,454},{5,455},{6,452},{7,453},{8... | collective-permute-start | bytes 393224 | tf_op jit(solution)/shard_map/ppermute | solution.py:60
  131.4 5.3 %collective-permute-start.14 = (f32[2,24,2,8,128]{4,3,2,1,0:T(8,128)S(1)}, f32[2,24,2,8,128]{4,3,2,1,0:T(8,128)S(1)}, u32[]{:S(2)}, u32[]{:S(2)}) collective-permute-start(f32[2,24,2,8,128]{4,3,2,1,0:T(8,128)S(1)} %constant_dynamic-update-slice_fusion.3.mid), channel_id=1, source_target_pairs={{0,1},{1,0},{2,3},{3,2},{4,5},{5,4},{6,7},{7,6},{8,9},{9,8},{10,11... | collective-permute-start | bytes 1179656 | tf_op jit(solution)/shard_map/ppermute | solution.py:60
  134.0 9.1 %collective-permute-start.13 = (f32[2,24,2,8,128]{4,3,2,1,0:T(8,128)S(1)}, f32[2,24,2,8,128]{4,3,2,1,0:T(8,128)S(1)}, u32[]{:S(2)}, u32[]{:S(2)}) collective-permute-start(f32[2,24,2,8,128]{4,3,2,1,0:T(8,128)S(1)} %constant_dynamic-update-slice_fusion.3.mid), channel_id=1, source_target_pairs={{0,61},{1,16},{2,63},{3,18},{4,49},{5,20},{6,51},{7,22},{8,53},{9,... | collective-permute-start | bytes 1179656 | tf_op jit(solution)/shard_map/ppermute | solution.py:60
  149.4 6.8 %collective-permute-start.15 = (f32[2,8,2,8,128]{4,3,2,1,0:T(8,128)S(1)}, f32[2,8,2,8,128]{4,3,2,1,0:T(8,128)S(1)}, u32[]{:S(2)}, u32[]{:S(2)}) collective-permute-start(f32[2,8,2,8,128]{4,3,2,1,0:T(8,128)S(1)} %get-tuple-element.33), channel_id=1, source_target_pairs={{0,64},{1,65},{2,66},{3,67},{4,68},{5,69},{6,70},{7,71},{8,72},{9,... | collective-permute-start | bytes 393224 | tf_op jit(solution)/shard_map/ppermute | solution.py:60
  153.0 7.1 %collective-permute-start.16 = (f32[2,8,2,8,128]{4,3,2,1,0:T(8,128)S(1)}, f32[2,8,2,8,128]{4,3,2,1,0:T(8,128)S(1)}, u32[]{:S(2)}, u32[]{:S(2)}) collective-permute-start(f32[2,8,2,8,128]{4,3,2,1,0:T(8,128)S(1)} %get-tuple-element.33), channel_id=1, source_target_pairs={{0,450},{1,451},{2,448},{3,449},{4,454},{5,455},{6,452},{7,453},{8... | collective-permute-start | bytes 393224 | tf_op jit(solution)/shard_map/ppermute | solution.py:60
  156.2 38.4 %copy-start.4 = (s32[256]{0:T(256)S(1)}, s32[256]{0:T(256)}, u32[]{:S(2)}) copy-start(s32[256]{0:T(256)} %get-tuple-element.24.near) | copy-start | bytes 3076
  160.1 7.4 %collective-permute-start.18 = (f32[2,24,2,8,128]{4,3,2,1,0:T(8,128)S(1)}, f32[2,24,2,8,128]{4,3,2,1,0:T(8,128)S(1)}, u32[]{:S(2)}, u32[]{:S(2)}) collective-permute-start(f32[2,24,2,8,128]{4,3,2,1,0:T(8,128)S(1)} %constant_dynamic-update-slice_fusion.6.mid), channel_id=1, source_target_pairs={{0,1},{1,0},{2,3},{3,2},{4,5},{5,4},{6,7},{7,6},{8,9},{9,8},{10,11... | collective-permute-start | bytes 1179656 | tf_op jit(solution)/shard_map/ppermute | solution.py:60
  162.7 10.1 %collective-permute-start.17 = (f32[2,24,2,8,128]{4,3,2,1,0:T(8,128)S(1)}, f32[2,24,2,8,128]{4,3,2,1,0:T(8,128)S(1)}, u32[]{:S(2)}, u32[]{:S(2)}) collective-permute-start(f32[2,24,2,8,128]{4,3,2,1,0:T(8,128)S(1)} %constant_dynamic-update-slice_fusion.6.mid), channel_id=1, source_target_pairs={{0,61},{1,16},{2,63},{3,18},{4,49},{5,20},{6,51},{7,22},{8,53},{9,... | collective-permute-start | bytes 1179656 | tf_op jit(solution)/shard_map/ppermute | solution.py:60
  177.1 7.2 %collective-permute-start.19 = (f32[16,256]{1,0:T(8,128)S(1)}, f32[16,256]{1,0:T(8,128)S(1)}, u32[]{:S(2)}, u32[]{:S(2)}) collective-permute-start(f32[16,256]{1,0:T(8,128)S(1)} %get-tuple-element.35), channel_id=1, source_target_pairs={{0,64},{1,65},{2,66},{3,67},{4,68},{5,69},{6,70},{7,71},{8,72},{9,... | collective-permute-start | bytes 49160 | tf_op jit(solution)/shard_map/ppermute | solution.py:60
  182.4 4.8 %collective-permute-start.20 = (f32[16,256]{1,0:T(8,128)S(1)}, f32[16,256]{1,0:T(8,128)S(1)}, u32[]{:S(2)}, u32[]{:S(2)}) collective-permute-start(f32[16,256]{1,0:T(8,128)S(1)} %get-tuple-element.35), channel_id=1, source_target_pairs={{0,450},{1,451},{2,448},{3,449},{4,454},{5,455},{6,452},{7,453},{8... | collective-permute-start | bytes 49160 | tf_op jit(solution)/shard_map/ppermute | solution.py:60
  187.2 6.5 %collective-permute-start.21 = (f32[16,256]{1,0:T(8,128)S(1)}, f32[16,256]{1,0:T(8,128)S(1)}, u32[]{:S(2)}, u32[]{:S(2)}) collective-permute-start(f32[16,256]{1,0:T(8,128)S(1)} %compare_select_fusion.9), channel_id=1, source_target_pairs={{0,61},{1,16},{2,63},{3,18},{4,49},{5,20},{6,51},{7,22},{8,53},{9,... | collective-permute-start | bytes 49160 | tf_op jit(solution)/shard_map/ppermute | solution.py:60
  191.6 3.1 collective-permute-start.22
  202.7 7.0 %collective-permute-start.23 = (f32[2,8,2,8,128]{4,3,2,1,0:T(8,128)S(1)}, f32[2,8,2,8,128]{4,3,2,1,0:T(8,128)S(1)}, u32[]{:S(2)}, u32[]{:S(2)}) collective-permute-start(f32[2,8,2,8,128]{4,3,2,1,0:T(8,128)S(1)} %get-tuple-element.36), channel_id=1, source_target_pairs={{0,64},{1,65},{2,66},{3,67},{4,68},{5,69},{6,70},{7,71},{8,72},{9,... | collective-permute-start | bytes 393224 | tf_op jit(solution)/shard_map/ppermute | solution.py:60
  206.9 6.6 %collective-permute-start.24 = (f32[2,8,2,8,128]{4,3,2,1,0:T(8,128)S(1)}, f32[2,8,2,8,128]{4,3,2,1,0:T(8,128)S(1)}, u32[]{:S(2)}, u32[]{:S(2)}) collective-permute-start(f32[2,8,2,8,128]{4,3,2,1,0:T(8,128)S(1)} %get-tuple-element.36), channel_id=1, source_target_pairs={{0,450},{1,451},{2,448},{3,449},{4,454},{5,455},{6,452},{7,453},{8... | collective-permute-start | bytes 393224 | tf_op jit(solution)/shard_map/ppermute | solution.py:60
  213.5 33.8 %collective-permute-start.26 = (f32[2,24,2,8,128]{4,3,2,1,0:T(8,128)S(1)}, f32[2,24,2,8,128]{4,3,2,1,0:T(8,128)S(1)}, u32[]{:S(2)}, u32[]{:S(2)}) collective-permute-start(f32[2,24,2,8,128]{4,3,2,1,0:T(8,128)S(1)} %constant_dynamic-update-slice_fusion.9.mid), channel_id=1, source_target_pairs={{0,1},{1,0},{2,3},{3,2},{4,5},{5,4},{6,7},{7,6},{8,9},{9,8},{10,11... | collective-permute-start | bytes 1179656 | tf_op jit(solution)/shard_map/ppermute | solution.py:60
  216.6 30.8 %collective-permute-start.25 = (f32[2,24,2,8,128]{4,3,2,1,0:T(8,128)S(1)}, f32[2,24,2,8,128]{4,3,2,1,0:T(8,128)S(1)}, u32[]{:S(2)}, u32[]{:S(2)}) collective-permute-start(f32[2,24,2,8,128]{4,3,2,1,0:T(8,128)S(1)} %constant_dynamic-update-slice_fusion.9.mid), channel_id=1, source_target_pairs={{0,61},{1,16},{2,63},{3,18},{4,49},{5,20},{6,51},{7,22},{8,53},{9,... | collective-permute-start | bytes 1179656 | tf_op jit(solution)/shard_map/ppermute | solution.py:60
  224.8 14.9 %collective-permute-start.45 = (f32[4,2,8,128]{3,2,0,1:T(8,128)S(1)}, f32[4,2,8,128]{3,2,0,1:T(8,128)S(1)}, u32[]{:S(2)}, u32[]{:S(2)}) collective-permute-start(f32[4,2,8,128]{3,2,0,1:T(8,128)S(1)} %get-tuple-element.52), channel_id=1, source_target_pairs={{0,0},{1,1},{2,256},{3,257},{4,4},{5,5},{6,260},{7,261},{8,8},{9,9... | collective-permute-start | bytes 98312 | tf_op jit(solution)/shard_map/ppermute | solution.py:60
  233.9 13.5 %collective-permute-start.46 = (f32[4,2,8,128]{3,2,0,1:T(8,128)S(1)}, f32[4,2,8,128]{3,2,0,1:T(8,128)S(1)}, u32[]{:S(2)}, u32[]{:S(2)}) collective-permute-start(f32[4,2,8,128]{3,2,0,1:T(8,128)S(1)} %get-tuple-element.53), channel_id=1, source_target_pairs={{0,16},{1,17},{2,272},{3,273},{4,20},{5,21},{6,276},{7,277},{8,24}... | collective-permute-start | bytes 98312 | tf_op jit(solution)/shard_map/ppermute | solution.py:60
  236.3 20.8 %collective-permute-start.38 = (f32[16,256]{1,0:T(8,128)S(1)}, f32[16,256]{1,0:T(8,128)S(1)}, u32[]{:S(2)}, u32[]{:S(2)}) collective-permute-start(f32[16,256]{1,0:T(8,128)S(1)} %compare_select_fusion.7.traces), channel_id=1, source_target_pairs={{0,192},{1,193},{2,194},{3,195},{4,196},{5,197},{6,198},{7,199},{8... | collective-permute-start | bytes 49160 | tf_op jit(solution)/shard_map/ppermute | solution.py:60
  239.7 17.4 %collective-permute-start.39 = (f32[16,256]{1,0:T(8,128)S(1)}, f32[16,256]{1,0:T(8,128)S(1)}, u32[]{:S(2)}, u32[]{:S(2)}) collective-permute-start(f32[16,256]{1,0:T(8,128)S(1)} %compare_select_fusion.7.traces), channel_id=1, source_target_pairs={{0,322},{1,323},{2,320},{3,321},{4,326},{5,327},{6,324},{7,325},{8... | collective-permute-start | bytes 49160 | tf_op jit(solution)/shard_map/ppermute | solution.py:60
  255.2 10.5 %collective-permute-start.27 = (f32[2,8,2,8,128]{4,3,2,1,0:T(8,128)S(1)}, f32[2,8,2,8,128]{4,3,2,1,0:T(8,128)S(1)}, u32[]{:S(2)}, u32[]{:S(2)}) collective-permute-start(f32[2,8,2,8,128]{4,3,2,1,0:T(8,128)S(1)} %get-tuple-element.38), channel_id=1, source_target_pairs={{0,64},{1,65},{2,66},{3,67},{4,68},{5,69},{6,70},{7,71},{8,72},{9,... | collective-permute-start | bytes 393224 | tf_op jit(solution)/shard_map/ppermute | solution.py:60
  257.1 19.9 %collective-permute-start.40 = (f32[16,256]{1,0:T(8,128)S(1)}, f32[16,256]{1,0:T(8,128)S(1)}, u32[]{:S(2)}, u32[]{:S(2)}) collective-permute-start(f32[16,256]{1,0:T(8,128)S(1)} %compare_select_fusion.5), channel_id=1, source_target_pairs={{0,2},{1,3},{2,0},{3,1},{4,6},{5,7},{6,4},{7,5},{8,10},{9,11},{10,... | collective-permute-start | bytes 49160 | tf_op jit(solution)/shard_map/ppermute | solution.py:60
  262.3 5.9 %collective-permute-start.28 = (f32[2,8,2,8,128]{4,3,2,1,0:T(8,128)S(1)}, f32[2,8,2,8,128]{4,3,2,1,0:T(8,128)S(1)}, u32[]{:S(2)}, u32[]{:S(2)}) collective-permute-start(f32[2,8,2,8,128]{4,3,2,1,0:T(8,128)S(1)} %get-tuple-element.38), channel_id=1, source_target_pairs={{0,450},{1,451},{2,448},{3,449},{4,454},{5,455},{6,452},{7,453},{8... | collective-permute-start | bytes 393224 | tf_op jit(solution)/shard_map/ppermute | solution.py:60
  268.2 19.5 %collective-permute-start.30 = (f32[2,24,2,8,128]{4,3,2,1,0:T(8,128)S(1)}, f32[2,24,2,8,128]{4,3,2,1,0:T(8,128)S(1)}, u32[]{:S(2)}, u32[]{:S(2)}) collective-permute-start(f32[2,24,2,8,128]{4,3,2,1,0:T(8,128)S(1)} %constant_dynamic-update-slice_fusion.12.mid), channel_id=1, source_target_pairs={{0,1},{1,0},{2,3},{3,2},{4,5},{5,4},{6,7},{7,6},{8,9},{9,8},{10,11... | collective-permute-start | bytes 1179656 | tf_op jit(solution)/shard_map/ppermute | solution.py:60
  273.9 13.8 %collective-permute-start.29 = (f32[2,24,2,8,128]{4,3,2,1,0:T(8,128)S(1)}, f32[2,24,2,8,128]{4,3,2,1,0:T(8,128)S(1)}, u32[]{:S(2)}, u32[]{:S(2)}) collective-permute-start(f32[2,24,2,8,128]{4,3,2,1,0:T(8,128)S(1)} %constant_dynamic-update-slice_fusion.12.mid), channel_id=1, source_target_pairs={{0,61},{1,16},{2,63},{3,18},{4,49},{5,20},{6,51},{7,22},{8,53},{9,... | collective-permute-start | bytes 1179656 | tf_op jit(solution)/shard_map/ppermute | solution.py:60
  277.0 20.7 %collective-permute-start.41 = (f32[16,256]{1,0:T(8,128)S(1)}, f32[16,256]{1,0:T(8,128)S(1)}, u32[]{:S(2)}, u32[]{:S(2)}) collective-permute-start(f32[16,256]{1,0:T(8,128)S(1)} %compare_select_fusion.4), channel_id=1, source_target_pairs={{0,16},{1,17},{2,18},{3,19},{4,20},{5,21},{6,22},{7,23},{8,24},{9,... | collective-permute-start | bytes 49160 | tf_op jit(solution)/shard_map/ppermute | solution.py:60
  285.8 31.9 %collective-permute-start.47 = (f32[4,2,8,128]{3,2,0,1:T(8,128)S(1)}, f32[4,2,8,128]{3,2,0,1:T(8,128)S(1)}, u32[]{:S(2)}, u32[]{:S(2)}) collective-permute-start(f32[4,2,8,128]{3,2,0,1:T(8,128)S(1)} %get-tuple-element.55), channel_id=1, source_target_pairs={{0,1},{1,0},{2,3},{3,2},{4,5},{5,4},{6,7},{7,6},{8,9},{9,8},{10,11... | collective-permute-start | bytes 98312 | tf_op jit(solution)/shard_map/ppermute | solution.py:60
  295.5 8.6 %collective-permute-start.31 = (f32[2,8,2,8,128]{4,3,2,1,0:T(8,128)S(1)}, f32[2,8,2,8,128]{4,3,2,1,0:T(8,128)S(1)}, u32[]{:S(2)}, u32[]{:S(2)}) collective-permute-start(f32[2,8,2,8,128]{4,3,2,1,0:T(8,128)S(1)} %get-tuple-element.40), channel_id=1, source_target_pairs={{0,64},{1,65},{2,66},{3,67},{4,68},{5,69},{6,70},{7,71},{8,72},{9,... | collective-permute-start | bytes 393224 | tf_op jit(solution)/shard_map/ppermute | solution.py:60
  297.8 16.5 %collective-permute-start.42 = (f32[16,256]{1,0:T(8,128)S(1)}, f32[16,256]{1,0:T(8,128)S(1)}, u32[]{:S(2)}, u32[]{:S(2)}) collective-permute-start(f32[16,256]{1,0:T(8,128)S(1)} %compare_select_fusion.3), channel_id=1, source_target_pairs={{0,32},{1,33},{2,34},{3,35},{4,36},{5,37},{6,38},{7,39},{8,40},{9,... | collective-permute-start | bytes 49160 | tf_op jit(solution)/shard_map/ppermute | solution.py:60
  301.0 5.7 %collective-permute-start.32 = (f32[2,8,2,8,128]{4,3,2,1,0:T(8,128)S(1)}, f32[2,8,2,8,128]{4,3,2,1,0:T(8,128)S(1)}, u32[]{:S(2)}, u32[]{:S(2)}) collective-permute-start(f32[2,8,2,8,128]{4,3,2,1,0:T(8,128)S(1)} %get-tuple-element.40), channel_id=1, source_target_pairs={{0,450},{1,451},{2,448},{3,449},{4,454},{5,455},{6,452},{7,453},{8... | collective-permute-start | bytes 393224 | tf_op jit(solution)/shard_map/ppermute | solution.py:60
  306.8 19.7 %collective-permute-start.34 = (f32[2,24,2,8,128]{4,3,2,1,0:T(8,128)S(1)}, f32[2,24,2,8,128]{4,3,2,1,0:T(8,128)S(1)}, u32[]{:S(2)}, u32[]{:S(2)}) collective-permute-start(f32[2,24,2,8,128]{4,3,2,1,0:T(8,128)S(1)} %constant_dynamic-update-slice_fusion.15.mid), channel_id=1, source_target_pairs={{0,1},{1,0},{2,3},{3,2},{4,5},{5,4},{6,7},{7,6},{8,9},{9,8},{10,11... | collective-permute-start | bytes 1179656 | tf_op jit(solution)/shard_map/ppermute | solution.py:60
  312.3 14.2 %collective-permute-start.33 = (f32[2,24,2,8,128]{4,3,2,1,0:T(8,128)S(1)}, f32[2,24,2,8,128]{4,3,2,1,0:T(8,128)S(1)}, u32[]{:S(2)}, u32[]{:S(2)}) collective-permute-start(f32[2,24,2,8,128]{4,3,2,1,0:T(8,128)S(1)} %constant_dynamic-update-slice_fusion.15.mid), channel_id=1, source_target_pairs={{0,61},{1,16},{2,63},{3,18},{4,49},{5,20},{6,51},{7,22},{8,53},{9,... | collective-permute-start | bytes 1179656 | tf_op jit(solution)/shard_map/ppermute | solution.py:60
  314.3 4.9 %collective-permute-start.43 = (f32[16,256]{1,0:T(8,128)S(1)}, f32[16,256]{1,0:T(8,128)S(1)}, u32[]{:S(2)}, u32[]{:S(2)}) collective-permute-start(f32[16,256]{1,0:T(8,128)S(1)} %compare_select_fusion.2), channel_id=1, source_target_pairs={{0,4},{1,5},{2,6},{3,7},{4,8},{5,9},{6,10},{7,11},{8,12},{9,13},{1... | collective-permute-start | bytes 49160 | tf_op jit(solution)/shard_map/ppermute | solution.py:60
  319.2 25.3 %collective-permute-start.44 = (f32[16,256]{1,0:T(8,128)S(1)}, f32[16,256]{1,0:T(8,128)S(1)}, u32[]{:S(2)}, u32[]{:S(2)}) collective-permute-start(f32[16,256]{1,0:T(8,128)S(1)} %compare_select_fusion.1), channel_id=1, source_target_pairs={{0,8},{1,9},{2,10},{3,11},{4,12},{5,13},{6,14},{7,15},{8,0},{9,1},... | collective-permute-start | bytes 49160 | tf_op jit(solution)/shard_map/ppermute | solution.py:60
  332.5 15.0 %collective-permute-start.35 = (f32[4,2,8,128]{3,2,1,0:T(8,128)S(1)}, f32[4,2,8,128]{3,2,1,0:T(8,128)S(1)}, u32[]{:S(2)}, u32[]{:S(2)}) collective-permute-start(f32[4,2,8,128]{3,2,1,0:T(8,128)S(1)} %get-tuple-element.56), channel_id=1, source_target_pairs={{0,0},{1,1},{2,256},{3,257},{4,4},{5,5},{6,260},{7,261},{8,8},{9,9... | collective-permute-start | bytes 98312 | tf_op jit(solution)/shard_map/ppermute | solution.py:60
  342.6 13.4 %collective-permute-start.36 = (f32[4,2,8,128]{3,2,1,0:T(8,128)S(1)}, f32[4,2,8,128]{3,2,1,0:T(8,128)S(1)}, u32[]{:S(2)}, u32[]{:S(2)}) collective-permute-start(f32[4,2,8,128]{3,2,1,0:T(8,128)S(1)} %get-tuple-element.57), channel_id=1, source_target_pairs={{0,16},{1,17},{2,272},{3,273},{4,20},{5,21},{6,276},{7,277},{8,24}... | collective-permute-start | bytes 98312 | tf_op jit(solution)/shard_map/ppermute | solution.py:60
  356.0 4.9 %collective-permute-start.37 = (f32[4,2,8,128]{3,2,0,1:T(8,128)S(1)}, f32[4,2,8,128]{3,2,0,1:T(8,128)S(1)}, u32[]{:S(2)}, u32[]{:S(2)}) collective-permute-start(f32[4,2,8,128]{3,2,0,1:T(8,128)S(1)} %select_bitcast_fusion.6), channel_id=1, source_target_pairs={{0,1},{1,0},{2,3},{3,2},{4,5},{5,4},{6,7},{7,6},{8,9},{9,8},{10,11... | collective-permute-start | bytes 98312 | tf_op jit(solution)/shard_map/ppermute | solution.py:60

commit v2 on v1

--- a/solution.py
+++ b/solution.py
@@ -14,9 +14,6 @@
 R = 3 * B
 PAD = 8
 NT = 16
-near_coef = 4.0 / 3.0
-far_coef = -1.0 / 12.0
-center_coef = -7.5
 
 
 def linear(x, y, z, c):
@@ -64,53 +61,69 @@
     return sorted((target, source) for source, target in pairs)
 
 
-def lane_ids():
-    return lax.broadcasted_iota(jnp.int32, (8, 128), 1)
-
-
-def laplace_tile(buf, x, row):
-    lane = lane_ids()
-    here, near, far = [], [], []
+def merge(*parts):
+    total = parts[0]
+    for part in parts[1:]:
+        total = jnp.where(total == 0.0, part, total)
+    return total
+
+
+def band():
+    row = lax.broadcasted_iota(jnp.int32, (256, 256), 0)
+    gap = jnp.abs(row - lax.broadcasted_iota(jnp.int32, (256, 256), 1))
+    one = jnp.where(gap == 1, 16.0, jnp.where(gap == 2, -1.0, 0.0)).astype(jnp.bfloat16)
+    return jnp.concatenate([one, one], axis=0)
+
+
+def depth_part(buf, deep, bands, margin):
+    first, count = B - margin, B + 2 * margin
+    low, size = (PAD, R) if margin > 0 else (PAD + 8, 8)
+    field = jnp.concatenate(
+        [
+            buf[first : first + count, half, low : low + size, :].reshape(count * size, 128)
+            for half in range(2)
+        ],
+        axis=1,
+    )
+    high = field.astype(jnp.bfloat16)
+    rest = (field - high.astype(jnp.float32)).astype(jnp.bfloat16)
+    out = jnp.dot(
+        jnp.concatenate([high, rest], axis=1), bands[...], preferred_element_type=jnp.float32
+    )
     for half in range(2):
-        here.append(buf[x, half, row : row + 8, :])
-        near.append(
-            (buf[x - 1, half, row : row + 8, :] + buf[x + 1, half, row : row + 8, :])
-            + (buf[x, half, row - 1 : row + 7, :] + buf[x, half, row + 1 : row + 9, :])
-        )
-        far.append(
-            (buf[x - 2, half, row : row + 8, :] + buf[x + 2, half, row : row + 8, :])
-            + (buf[x, half, row - 2 : row + 6, :] + buf[x, half, row + 2 : row + 10, :])
-        )
-    low, high = here
-    up1 = [pltpu.roll(v, 127, 1) for v in here]
-    up2 = [pltpu.roll(v, 126, 1) for v in here]
-    dn1 = [pltpu.roll(v, 1, 1) for v in here]
-    dn2 = [pltpu.roll(v, 2, 1) for v in here]
-    near[0] += jnp.where(lane < 127, up1[0], up1[1]) + jnp.where(lane >= 1, dn1[0], 0.0)
-    near[1] += jnp.where(lane < 127, up1[1], 0.0) + jnp.where(lane >= 1, dn1[1], dn1[0])
-    far[0] += jnp.where(lane < 126, up2[0], up2[1]) + jnp.where(lane >= 2, dn2[0], 0.0)
-    far[1] += jnp.where(lane < 126, up2[1], 0.0) + jnp.where(lane >= 2, dn2[1], dn2[0])
-    return here, [
-        near_coef * near[h] + far_coef * far[h] + center_coef * here[h] for h in range(2)
-    ]
+        deep[first : first + count, half, low - PAD : low - PAD + size, :] = out[
+            :, 128 * half : 128 * half + 128
+        ].reshape(count, size, 128)
+
+
+def laplace_tile(buf, deep, x, half, row):
+    here = buf[x, half, row : row + 8, :]
+    near = (buf[x - 1, half, row : row + 8, :] + buf[x + 1, half, row : row + 8, :]) + (
+        buf[x, half, row - 1 : row + 7, :] + buf[x, half, row + 1 : row + 9, :]
+    )
+    far = (buf[x - 2, half, row : row + 8, :] + buf[x + 2, half, row : row + 8, :]) + (
+        buf[x, half, row - 2 : row + 6, :] + buf[x, half, row + 2 : row + 10, :]
+    )
+    depth = deep[x, half, row - PAD : row - PAD + 8, :]
+    return here, (16.0 * near - far) + (depth - 90.0 * here)
 
 
 def tiles_for(margin):
     return (PAD, PAD + 8, PAD + 16) if margin > 0 else (PAD + 8,)
 
 
-def assemble(buf, f, mid, inter, intra, core):
-    buf[:, :, PAD + 8 : PAD + 16, :] = mid[f]
+def assemble(buf, f, mid, intra, inter, core):
+    buf[:, :, PAD + 8 : PAD + 16, :] = mid[f, :R]
 
     @pl.when(core == 0)
     def _():
-        buf[:, :, PAD : PAD + 8, :] = inter[f]
-        buf[:, :, PAD + 16 : PAD + 24, :] = intra[f]
+        buf[:, :, PAD : PAD + 8, :] = inter[f, :R]
+        buf[:, :, PAD + 16 : PAD + 24, :] = intra[f, :R]
 
     @pl.when(core == 1)
     def _():
-        buf[:, :, PAD : PAD + 8, :] = intra[f]
-        buf[:, :, PAD + 16 : PAD + 24, :] = inter[f]
+        buf[:, :, PAD : PAD + 8, :] = intra[f, :R]
+        buf[:, :, PAD + 16 : PAD + 24, :] = inter[f, :R]
 
 
 def own(buf):
@@ -134,20 +147,20 @@
     lax.fori_loop(0, counts[0], body, 0)
 
 
-def forward_steps(steps, a, b, vel, src, place, checkpoints, receivers, mine, counts, traces):
+def forward_steps(steps, a, b, deep, bands, vel, src, place, checkpoints, receivers, mine, counts, traces):
     for done, step in enumerate(steps):
         margin = 2 * (len(steps) - 1 - done)
         ck = checkpoints[step]
 
+        depth_part(b, deep, bands, margin)
+
         def plane(x, _, a=a, b=b, margin=margin, ck=ck):
             for row in tiles_for(margin):
-                here, lap = laplace_tile(b, x, row)
                 for half in range(2):
+                    here, lap = laplace_tile(b, deep, x, half, row)
                     at = (x, half, slice(row, row + 8), slice(None))
                     cell = (x, half, slice(row - PAD, row - PAD + 8), slice(None))
-                    a[at] = (
-                        2.0 * here[half] - a[at] + vel[cell] * lap[half] + src[(ck, *cell)]
-                    )
+                    a[at] = 2.0 * here - a[at] + vel[cell] * lap + src[(ck, *cell)]
             return 0
 
         lax.fori_loop(B - margin, 2 * B + margin, plane, 0)
@@ -157,7 +170,7 @@
 
 
 def first_forward(
-    place, checkpoints, receivers, mine, counts, mid, inter, intra, vel, src, pair, traces, a, b
+    place, checkpoints, receivers, mine, counts, mid, intra, inter, vel, src, pair, traces, a, b, deep, bands
 ):
     core = place[2]
     for f in range(5):
@@ -174,26 +187,28 @@
             into[:, :, 0:8, :] = intra[f]
             into[:, :, 16:24, :] = inter[f]
 
+    bands[...] = band()
     traces[...] = jnp.zeros_like(traces)
     a[...] = jnp.zeros_like(a)
     b[:, :, PAD : PAD + R, :] = src[checkpoints[0]]
     sample(b, 0, place, receivers, mine, counts, traces)
     prev, cur = forward_steps(
-        range(1, 5), a, b, vel, src, place, checkpoints, receivers, mine, counts, traces
+        range(1, 5), a, b, deep, bands, vel, src, place, checkpoints, receivers, mine, counts, traces
     )
     pair[0] = own(prev)
     pair[1] = own(cur)
 
 
 def later_forward(
-    steps, place, checkpoints, receivers, mine, counts, vel, src, mid, inter, intra, held,
-    pair, traces, a, b,
+    steps, place, checkpoints, receivers, mine, counts, vel, src, mid, intra, inter, held,
+    pair, traces, a, b, deep, bands,
 ):
-    assemble(a, 0, mid, inter, intra, place[2])
-    assemble(b, 1, mid, inter, intra, place[2])
+    assemble(a, 0, mid, intra, inter, place[2])
+    assemble(b, 1, mid, intra, inter, place[2])
+    bands[...] = band()
     traces[...] = held[...]
     prev, cur = forward_steps(
-        steps, a, b, vel, src, place, checkpoints, receivers, mine, counts, traces
+        steps, a, b, deep, bands, vel, src, place, checkpoints, receivers, mine, counts, traces
     )
     pair[0] = own(prev)
     pair[1] = own(cur)
@@ -220,7 +235,7 @@
 
 
 def adjoint_steps(
-    steps, a, b, w, vel, back_own, place, checkpoints, receivers, near, counts, traces, image
+    steps, a, b, w, deep, bands, vel, back_own, place, checkpoints, receivers, near, counts, traces, image
 ):
     for done, step in enumerate(steps):
         margin = 2 * (len(steps) - 1 - done)
@@ -234,12 +249,14 @@
 
         lax.fori_loop(B - margin - 2, 2 * B + margin + 2, scale, 0)
 
+        depth_part(w, deep, bands, margin)
+
         def plane(x, _, a=a, b=b, margin=margin):
             for row in tiles_for(margin):
-                _, lap = laplace_tile(w, x, row)
                 for half in range(2):
+                    _, lap = laplace_tile(w, deep, x, half, row)
                     at = (x, half, slice(row, row + 8), slice(None))
-                    a[at] = 2.0 * b[at] - a[at] + lap[half]
+                    a[at] = 2.0 * b[at] - a[at] + lap
             return 0
 
         lax.fori_loop(B - margin, 2 * B + margin, plane, 0)
@@ -250,33 +267,37 @@
 
 
 def first_adjoint(
-    place, checkpoints, receivers, near, counts, traces, vel, back_own, pair, image, a, b, w
+    place, checkpoints, receivers, near, counts, traces, vel, back_own, carried, pair, image, a, b, w, deep, bands
 ):
     a[...] = jnp.zeros_like(a)
     b[...] = jnp.zeros_like(b)
     image[...] = jnp.zeros_like(image)
+    bands[...] = band()
     inject(b, NT - 1, place, receivers, near, counts, traces)
     add_image(image, b, back_own, checkpoints[NT - 1])
     later, now = adjoint_steps(
-        range(14, 10, -1), a, b, w, vel, back_own, place, checkpoints, receivers, near, counts,
+        range(14, 10, -1), a, b, w, deep, bands, vel, back_own, place, checkpoints, receivers, near, counts,
         traces, image,
     )
-    pair[0] = own(later)
-    pair[1] = own(now)
+    for f, buf in enumerate((later, now)):
+        pair[f, :B] = own(buf)
+        pair[f, B] = carried[f]
 
 
 def later_adjoint(
-    steps, place, checkpoints, receivers, near, counts, traces, vel, back_own, mid, inter, intra,
-    held, pair, image, a, b, w,
+    steps, place, checkpoints, receivers, near, counts, traces, vel, back_own, mid, intra, inter,
+    held, far, pair, image, a, b, w, deep, bands,
 ):
-    assemble(a, 0, mid, inter, intra, place[2])
-    assemble(b, 1, mid, inter, intra, place[2])
+    assemble(a, 0, mid, intra, inter, place[2])
+    assemble(b, 1, mid, intra, inter, place[2])
     image[...] = held[...]
+    bands[...] = band()
     later, now = adjoint_steps(
-        steps, a, b, w, vel, back_own, place, checkpoints, receivers, near, counts, traces, image
-    )
-    pair[0] = own(later)
-    pair[1] = own(now)
+        steps, a, b, w, deep, bands, vel, back_own, place, checkpoints, receivers, near, counts, traces, image
+    )
+    for f, buf in enumerate((later, now)):
+        pair[f, :B] = own(buf)
+        pair[f, B] = merge(mid[f, R], intra[f, R], inter[f, R], far[f])
 
 
 def list_receivers(place, receivers, mine, near, counts):
@@ -323,7 +344,8 @@
         in_specs=ins,
         out_specs=out_specs,
         out_shape=outs,
-        scratch_shapes=[pltpu.VMEM(FIELD, jnp.float32)] * fields,
+        scratch_shapes=[pltpu.VMEM(FIELD, jnp.float32)] * fields
+        + [pltpu.VMEM((R, 2, R, 128), jnp.float32), pltpu.VMEM((512, 256), jnp.bfloat16)],
         compiler_params=pltpu.CompilerParams(vmem_limit_bytes=48 * 1024 * 1024),
     )
 
@@ -332,7 +354,16 @@
     low = send(block, UP)
     high = send(block, DOWN)
     mid = jnp.concatenate([low, block, high], axis=1)
-    return mid, send(mid, ACROSS), send(mid, SWAP)
+    return mid, send(mid, SWAP), send(mid, ACROSS)
+
+
+def exchange_carrying(block, more, beside):
+    low = send(block, UP)
+    high = send(block, DOWN)
+    known = merge(block[:, B:], low[:, B:], high[:, B:], more[:, None])
+    mid = jnp.concatenate([low[:, :B], block[:, :B], high[:, :B], known], axis=1)
+    mid, beside = lax.optimization_barrier((mid, beside))
+    return (mid, send(mid, SWAP), send(mid, ACROSS)), beside
 
 
 def pick(two, index):
@@ -358,22 +389,18 @@
     return ordered(got, other, odd, 1).reshape(count, 8, 2, 8, 128)
 
 
-def outward(block, core, odd):
+def outward_far(block, odd):
     first, second = block[:4], block[4:]
     got = send(pick((first, second), odd), back(spread(0)))
-    other = send(pick((second, first), odd), back(spread(1)))
+    return got, send(pick((second, first), odd), back(spread(1)))
+
+
+def outward_near(got, other, core, odd):
     whole = ordered(got, other, odd, 1)
     front, rear = whole[:, :, 0], whole[:, :, 1]
     kept = pick((front, rear), core)
     came = send(pick((rear, front), core), SWAP)
     return ordered(kept, came, core, 2).reshape(4, 32, 128)
-
-
-def merge(*parts):
-    total = parts[0]
-    for part in parts[1:]:
-        total = jnp.where(total == 0.0, part, total)
-    return total
 
 
 def on_device(velocity_term, model_step, background, receivers, checkpoints):
@@ -390,7 +417,7 @@
         out_shape=[i32(256), i32(256), i32(2)],
     )(place, receivers)
     stacked = jnp.concatenate(
-        [velocity_term[None], model_step[None], background.astype(jnp.float32)], axis=0
+        [velocity_term[None] * (1.0 / 12.0), model_step[None], background.astype(jnp.float32)], axis=0
     )
     inner = inward(stacked, core, odd)
     back_own = inner[2:]
@@ -410,33 +437,35 @@
             [VM] * 2,
             2,
         )(place, checkpoints, receivers, mine, counts, vel, src, *exchange(pair), traces)
-    wavefield = outward(pair[1], core, odd)
-    traces = merge(traces, send(traces, UP), send(traces, DOWN))
-    traces = merge(traces, send(traces, ACROSS), send(traces, SWAP))
-    local = traces
-    traces = merge(traces, send(traces, shifted(dz=3)), send(traces, shifted(dz=-3)))
-    traces = merge(traces, send(traces, shifted(dz=8)))
-    traces = merge(traces, send(traces, shifted(dx=1)))
-    traces = merge(traces, send(traces, shifted(dx=2)))
-    traces = merge(traces, send(traces, shifted(dy=1)))
-    traces = merge(traces, send(traces, shifted(dy=2)))
+    field = pair[1]
+    local = merge(traces, send(traces, UP), send(traces, DOWN))
+    local = merge(local, send(local, ACROSS), send(local, SWAP))
+    carried = local.reshape(2, 8, 2, 128).transpose(0, 2, 1, 3)
+    swapped = send(carried, SWAP)
     scalars = (place, checkpoints, receivers, near, counts, local)
-    pair, image = call(
-        first_adjoint,
-        [SM] * 6 + [VM] * 2,
-        [f32(2, B, 2, B, 128), f32(B, 2, B, 128)],
-        [VM] * 2,
-        3,
-    )(*scalars, vel, back_own)
-    for steps in (range(10, 6, -1), range(6, 2, -1), range(2, -1, -1)):
+    outs = [f32(2, B + 1, 2, B, 128), f32(B, 2, B, 128)]
+    pair, image = call(first_adjoint, [SM] * 6 + [VM] * 3, outs, [VM] * 2, 3)(
+        *scalars, vel, back_own, carried
+    )
+    beside = ()
+    for number, steps in enumerate((range(10, 6, -1), range(6, 2, -1), range(2, -1, -1))):
+        parts, beside = exchange_carrying(pair, swapped, beside)
+        if number == 0:
+            far = send(parts[0][:, R], shifted(dz=8))
+            beside = (field,)
+        elif number == 1:
+            far = carried
+            beside = outward_far(beside[0], odd)
+        else:
+            wavefield = outward_near(*beside, core, odd)
         pair, image = call(
-            functools.partial(later_adjoint, steps),
-            [SM] * 6 + [VM] * 6,
-            [f32(2, B, 2, B, 128), f32(B, 2, B, 128)],
-            [VM] * 2,
-            3,
-        )(*scalars, vel, back_own, *exchange(pair), image)
-    image = outward(image, core, odd)
+            functools.partial(later_adjoint, steps), [SM] * 6 + [VM] * 7, outs, [VM] * 2, 3
+        )(*scalars, vel, back_own, *parts, image, far)
+    carried = pair[:, B]
+    carried = merge(carried, send(carried, shifted(dy=1)))
+    carried = merge(carried, send(carried, shifted(dy=2)))
+    traces = carried.transpose(0, 2, 1, 3).reshape(NT, 256)
+    image = outward_near(*outward_far(image, odd), core, odd)
     column_image = lax.psum(jnp.sum(image, axis=2), "c") / 256.0
     return (image, traces, column_image, wavefield)
 

time: 366 us -> 340 us (0.929)
  the two profiles are of different devices: /device:TPU:213 before, /device:TPU:79 now
where the time goes in v2:
time: 340 us; the launch traced here: 338 us
  starting transfers between devices  183 us (54%)
  waiting for transfers between devices  101 us (30%)
  Pallas kernels  41.1 us (12%)
  other arithmetic  4.99 us (1%)
  local copies, waits for them, and re-layouts  3.9 us (1%)
    ppermute x45, starting transfers between devices, send(): return lax.ppermute(value, AXES, pairs)  183 us
    ppermute x45, waiting for transfers between devices, send(): return lax.ppermute(value, AXES, pairs)  101 us
    pallas_call x3, Pallas kernels, on_device(): call(functools.partial(later_forward, steps), [SM] * 5 + [VM] * 6, [f32(2...  12.5 us
    pallas_call x3, Pallas kernels, on_device(): call(functools.partial(later_adjoint, steps), [SM] * 6 + [VM] * 7, outs,...  12.4 us
  transfers between devices with their start and end apart: 45, of which 27 were waited for; matrix products, arithmetic and copies ran while one was open for 1% of the time, Pallas kernels for 2%

profile of v2, /device:TPU:79, one launch (start us, length us, event | category | flops | bytes accessed | tf_op | source)
XLA Modules:
  0.0 338.2 jit_solution(14576389620326261406)
XLA Ops:
  3.4 2.6 collective-permute-start
  7.1 8.3 %collective-permute-start.1 = (f32[6,4,2,8,128]{4,3,2,1,0:T(8,128)S(1)}, f32[6,4,2,8,128]{4,3,2,1,0:T(8,128)S(1)}, u32[]{:S(2)}, u32[]{:S(2)}) collective-permute-start(f32[6,4,2,8,128]{4,3,2,1,0:T(8,128)S(1)} %get-tuple-element.60), channel_id=1, source_target_pairs={{0,0},{1,1},{2,32},{3,33},{4,4},{5,5},{6,36},{7,37},{8,8},{9,9},{1... | collective-permute-start | bytes 589832 | tf_op jit(solution)/shard_map/ppermute | solution.py:57
  15.4 7.4 %collective-permute-start.2 = (f32[6,4,2,8,128]{4,3,2,1,0:T(8,128)S(1)}, f32[6,4,2,8,128]{4,3,2,1,0:T(8,128)S(1)}, u32[]{:S(2)}, u32[]{:S(2)}) collective-permute-start(f32[6,4,2,8,128]{4,3,2,1,0:T(8,128)S(1)} %get-tuple-element.61), channel_id=1, source_target_pairs={{0,16},{1,17},{2,48},{3,49},{4,20},{5,21},{6,52},{7,53},{8,24},{9,... | collective-permute-start | bytes 589832 | tf_op jit(solution)/shard_map/ppermute | solution.py:57
  22.8 28.9 %collective-permute-done.1 = f32[6,4,2,8,128]{4,3,2,1,0:T(8,128)S(1)} collective-permute-done((f32[6,4,2,8,128]{4,3,2,1,0:T(8,128)S(1)}, f32[6,4,2,8,128]{4,3,2,1,0:T(8,128)S(1)}, u32[]{:S(2)}, u32[]{:S(2)}) %collective-permute-start.1) | collective-permute-done | bytes 196640 | tf_op jit(solution)/shard_map/ppermute | solution.py:57
  51.8 3.4 collective-permute-done.2
  55.3 2.5 collective-permute-start.4
  57.8 2.7 collective-permute-start.3
  60.6 4.3 %collective-permute-done.4 = f32[5,8,2,8,128]{4,3,2,1,0:T(8,128)S(1)} collective-permute-done((f32[5,8,2,8,128]{4,3,2,1,0:T(8,128)S(1)}, f32[5,8,2,8,128]{4,3,2,1,0:T(8,128)S(1)}, u32[]{:S(2)}, u32[]{:S(2)}) %collective-permute-start.4) | collective-permute-done | bytes 327712 | tf_op jit(solution)/shard_map/ppermute | solution.py:57
  64.9 2.6 collective-permute-done.3
  67.6 1.9 collective-permute-start.6
  69.5 4.2 %collective-permute-start.5 = (f32[5,24,2,8,128]{4,3,2,1,0:T(8,128)S(1)}, f32[5,24,2,8,128]{4,3,2,1,0:T(8,128)S(1)}, u32[]{:S(2)}, u32[]{:S(2)}) collective-permute-start(f32[5,24,2,8,128]{4,3,2,1,0:T(8,128)S(1)} %pad_maximum_fusion.mid), channel_id=1, source_target_pairs={{0,1},{1,0},{2,3},{3,2},{4,5},{5,4},{6,7},{7,6},{8,9},{9,8},{10,11... | collective-permute-start | bytes 2949128 | tf_op jit(solution)/shard_map/ppermute | solution.py:57
  74.4 6.4 %shard_map.84 = (s32[256]{0:T(256)}, s32[256]{0:T(256)}, s32[2]{0:T(128)}) custom-call(s32[4]{0:T(128)} %pad_add_fusion.place, s32[3,256]{1,0:T(4,128)} %receivers.17), custom_call_target="tpu_custom_call" | custom-call | tf_op jit(solution)/shard_map/pallas_call | solution.py:413
  80.8 4.3 %collective-permute-done.6.inter = f32[5,24,2,8,128]{4,3,2,1,0:T(8,128)S(1)} collective-permute-done((f32[5,24,2,8,128]{4,3,2,1,0:T(8,128)S(1)}, f32[5,24,2,8,128]{4,3,2,1,0:T(8,128)S(1)}, u32[]{:S(2)}, u32[]{:S(2)}) %collective-permute-start.6) | collective-permute-done | bytes 983072 | tf_op jit(solution)/shard_map/ppermute | solution.py:57
  87.2 5.1 %shard_map.85 = (f32[24,2,24,128]{3,2,1,0:T(8,128)S(1)}, f32[4,24,2,24,128]{4,3,2,1,0:T(8,128)S(1)}, f32[2,8,2,8,128]{4,3,2,1,0:T(8,128)S(1)}, f32[16,256]{1,0:T(8,128)S(1)}) custom-call(s32[4]{0:T(128)S(1)} %copy-done.1, s32[16]{0:T(128)S(1)} %copy-done.2, s32[3,256]{1,0:T(4,128)S(1)} %copy-done, s32[256]{0:T(256)S(1)} %copy-done.5, s32[2]{0:T(128)S(1)} %copy-done.3, ...), custom_call_target="tpu_custom_call" | custom-call | tf_op jit(solution)/shard_map/pallas_call | solution.py:425
  92.2 1.9 collective-permute-start.7
  94.1 6.0 %collective-permute-start.8 = (f32[2,8,2,8,128]{4,3,2,1,0:T(8,128)S(1)}, f32[2,8,2,8,128]{4,3,2,1,0:T(8,128)S(1)}, u32[]{:S(2)}, u32[]{:S(2)}) collective-permute-start(f32[2,8,2,8,128]{4,3,2,1,0:T(8,128)S(1)} %get-tuple-element.35), channel_id=1, source_target_pairs={{0,450},{1,451},{2,448},{3,449},{4,454},{5,455},{6,452},{7,453},{8... | collective-permute-start | bytes 393224 | tf_op jit(solution)/shard_map/ppermute | solution.py:57
  102.6 5.4 %collective-permute-start.10 = (f32[2,24,2,8,128]{4,3,2,1,0:T(8,128)S(1)}, f32[2,24,2,8,128]{4,3,2,1,0:T(8,128)S(1)}, u32[]{:S(2)}, u32[]{:S(2)}) collective-permute-start(f32[2,24,2,8,128]{4,3,2,1,0:T(8,128)S(1)} %constant_dynamic-update-slice_fusion.mid), channel_id=1, source_target_pairs={{0,61},{1,16},{2,63},{3,18},{4,49},{5,20},{6,51},{7,22},{8,53},{9,... | collective-permute-start | bytes 1179656 | tf_op jit(solution)/shard_map/ppermute | solution.py:57
  108.0 1.9 collective-permute-start.9
  110.0 3.9 %collective-permute-done.10.inter = f32[2,24,2,8,128]{4,3,2,1,0:T(8,128)S(1)} collective-permute-done((f32[2,24,2,8,128]{4,3,2,1,0:T(8,128)S(1)}, f32[2,24,2,8,128]{4,3,2,1,0:T(8,128)S(1)}, u32[]{:S(2)}, u32[]{:S(2)}) %collective-permute-start.10) | collective-permute-done | bytes 393248 | tf_op jit(solution)/shard_map/ppermute | solution.py:57
  113.8 4.6 %shard_map.86 = (f32[2,8,2,8,128]{4,3,2,1,0:T(8,128)S(1)}, f32[16,256]{1,0:T(8,128)S(1)}) custom-call(s32[4]{0:T(128)S(1)} %copy-done.1, s32[16]{0:T(128)S(1)} %copy-done.2, s32[3,256]{1,0:T(4,128)S(1)} %copy-done, s32[256]{0:T(256)S(1)} %copy-done.5, s32[2]{0:T(128)S(1)} %copy-done.3, f32[24,2,24,128]{3,2,1,0:T(8,128)S(1)} %get-tuple-element.33.vel, ...), custom_call_target="tpu_custom_call" | custom-call | tf_op jit(solution)/shard_map/pallas_call | solution.py:433
  118.4 2.9 collective-permute-start.11
  121.3 3.9 %collective-permute-start.12 = (f32[2,8,2,8,128]{4,3,2,1,0:T(8,128)S(1)}, f32[2,8,2,8,128]{4,3,2,1,0:T(8,128)S(1)}, u32[]{:S(2)}, u32[]{:S(2)}) collective-permute-start(f32[2,8,2,8,128]{4,3,2,1,0:T(8,128)S(1)} %get-tuple-element.37), channel_id=1, source_target_pairs={{0,450},{1,451},{2,448},{3,449},{4,454},{5,455},{6,452},{7,453},{8... | collective-permute-start | bytes 393224 | tf_op jit(solution)/shard_map/ppermute | solution.py:57
  127.1 4.9 %collective-permute-start.14 = (f32[2,24,2,8,128]{4,3,2,1,0:T(8,128)S(1)}, f32[2,24,2,8,128]{4,3,2,1,0:T(8,128)S(1)}, u32[]{:S(2)}, u32[]{:S(2)}) collective-permute-start(f32[2,24,2,8,128]{4,3,2,1,0:T(8,128)S(1)} %constant_dynamic-update-slice_fusion.3.mid), channel_id=1, source_target_pairs={{0,61},{1,16},{2,63},{3,18},{4,49},{5,20},{6,51},{7,22},{8,53},{9,... | collective-permute-start | bytes 1179656 | tf_op jit(solution)/shard_map/ppermute | solution.py:57
  134.0 4.4 %collective-permute-done.14.inter = f32[2,24,2,8,128]{4,3,2,1,0:T(8,128)S(1)} collective-permute-done((f32[2,24,2,8,128]{4,3,2,1,0:T(8,128)S(1)}, f32[2,24,2,8,128]{4,3,2,1,0:T(8,128)S(1)}, u32[]{:S(2)}, u32[]{:S(2)}) %collective-permute-start.14) | collective-permute-done | bytes 393248 | tf_op jit(solution)/shard_map/ppermute | solution.py:57
  138.3 4.6 %shard_map.87 = (f32[2,8,2,8,128]{4,3,2,1,0:T(8,128)S(1)}, f32[16,256]{1,0:T(8,128)S(1)}) custom-call(s32[4]{0:T(128)S(1)} %copy-done.1, s32[16]{0:T(128)S(1)} %copy-done.2, s32[3,256]{1,0:T(4,128)S(1)} %copy-done, s32[256]{0:T(256)S(1)} %copy-done.5, s32[2]{0:T(128)S(1)} %copy-done.3, f32[24,2,24,128]{3,2,1,0:T(8,128)S(1)} %get-tuple-element.33.vel, ...), custom_call_target="tpu_custom_call" | custom-call | tf_op jit(solution)/shard_map/pallas_call | solution.py:433
  142.9 3.1 collective-permute-start.15
  146.0 3.9 %collective-permute-start.16 = (f32[2,8,2,8,128]{4,3,2,1,0:T(8,128)S(1)}, f32[2,8,2,8,128]{4,3,2,1,0:T(8,128)S(1)}, u32[]{:S(2)}, u32[]{:S(2)}) collective-permute-start(f32[2,8,2,8,128]{4,3,2,1,0:T(8,128)S(1)} %get-tuple-element.39), channel_id=1, source_target_pairs={{0,450},{1,451},{2,448},{3,449},{4,454},{5,455},{6,452},{7,453},{8... | collective-permute-start | bytes 393224 | tf_op jit(solution)/shard_map/ppermute | solution.py:57
  151.9 4.4 %collective-permute-start.18 = (f32[2,24,2,8,128]{4,3,2,1,0:T(8,128)S(1)}, f32[2,24,2,8,128]{4,3,2,1,0:T(8,128)S(1)}, u32[]{:S(2)}, u32[]{:S(2)}) collective-permute-start(f32[2,24,2,8,128]{4,3,2,1,0:T(8,128)S(1)} %constant_dynamic-update-slice_fusion.6.mid), channel_id=1, source_target_pairs={{0,61},{1,16},{2,63},{3,18},{4,49},{5,20},{6,51},{7,22},{8,53},{9,... | collective-permute-start | bytes 1179656 | tf_op jit(solution)/shard_map/ppermute | solution.py:57
  156.3 1.9 collective-permute-start.17
  158.2 4.9 %collective-permute-done.18.inter = f32[2,24,2,8,128]{4,3,2,1,0:T(8,128)S(1)} collective-permute-done((f32[2,24,2,8,128]{4,3,2,1,0:T(8,128)S(1)}, f32[2,24,2,8,128]{4,3,2,1,0:T(8,128)S(1)}, u32[]{:S(2)}, u32[]{:S(2)}) %collective-permute-start.18) | collective-permute-done | bytes 393248 | tf_op jit(solution)/shard_map/ppermute | solution.py:57
  163.1 3.3 shard_map.88
  166.5 3.3 collective-permute-start.19
  169.7 3.9 %collective-permute-start.20 = (f32[16,256]{1,0:T(8,128)S(1)}, f32[16,256]{1,0:T(8,128)S(1)}, u32[]{:S(2)}, u32[]{:S(2)}) collective-permute-start(f32[16,256]{1,0:T(8,128)S(1)} %get-tuple-element.41), channel_id=1, source_target_pairs={{0,450},{1,451},{2,448},{3,449},{4,454},{5,455},{6,452},{7,453},{8... | collective-permute-start | bytes 49160 | tf_op jit(solution)/shard_map/ppermute | solution.py:57
  174.5 6.6 %collective-permute-start.21 = (f32[16,256]{1,0:T(8,128)S(1)}, f32[16,256]{1,0:T(8,128)S(1)}, u32[]{:S(2)}, u32[]{:S(2)}) collective-permute-start(f32[16,256]{1,0:T(8,128)S(1)} %compare_select_fusion.13), channel_id=1, source_target_pairs={{0,61},{1,16},{2,63},{3,18},{4,49},{5,20},{6,51},{7,22},{8,53},{9,... | collective-permute-start | bytes 49160 | tf_op jit(solution)/shard_map/ppermute | solution.py:57
  184.2 4.7 %shard_map.89 = (f32[2,9,2,8,128]{4,3,2,1,0:T(8,128)S(1)}, f32[8,2,8,128]{3,2,1,0:T(8,128)S(1)}) custom-call(s32[4]{0:T(128)S(1)} %copy-done.1, s32[16]{0:T(128)S(1)} %copy-done.2, s32[3,256]{1,0:T(4,128)S(1)} %copy-done, s32[256]{0:T(256)S(1)} %copy-done.4, s32[2]{0:T(128)S(1)} %copy-done.3, f32[16,256]{1,0:T(8,128)S(1)} %compare_select_fusion.11.traces, ...), custom_call_target="tpu_custom_call" | custom-call | tf_op jit(solution)/shard_map/pallas_call | solution.py:447
  189.0 4.2 %collective-permute-start.24 = (f32[2,9,2,8,128]{4,3,2,0,1:T(8,128)S(1)}, f32[2,9,2,8,128]{4,3,2,0,1:T(8,128)S(1)}, u32[]{:S(2)}, u32[]{:S(2)}) collective-permute-start(f32[2,9,2,8,128]{4,3,2,0,1:T(8,128)S(1)} %copy.97), channel_id=1, source_target_pairs={{0,450},{1,451},{2,448},{3,449},{4,454},{5,455},{6,452},{7,453},{8... | collective-permute-start | bytes 442376 | tf_op jit(solution)/shard_map/ppermute | solution.py:57
  193.2 2.4 collective-permute-start.23
  195.5 2.2 collective-permute-start.25
  197.8 4.9 %collective-permute-done.23 = f32[2,9,2,8,128]{4,3,2,0,1:T(8,128)S(1)} collective-permute-done((f32[2,9,2,8,128]{4,3,2,0,1:T(8,128)S(1)}, f32[2,9,2,8,128]{4,3,2,0,1:T(8,128)S(1)}, u32[]{:S(2)}, u32[]{:S(2)}) %collective-permute-start.23) | collective-permute-done | bytes 147488 | tf_op jit(solution)/shard_map/ppermute | solution.py:57
  202.7 3.8 %collective-permute-start.27 = (f32[2,25,2,8,128]{4,3,2,0,1:T(8,128)S(1)}, f32[2,25,2,8,128]{4,3,2,0,1:T(8,128)S(1)}, u32[]{:S(2)}, u32[]{:S(2)}) collective-permute-start(f32[2,25,2,8,128]{4,3,2,0,1:T(8,128)S(1)} %pad_maximum_fusion.1), channel_id=1, source_target_pairs={{0,61},{1,16},{2,63},{3,18},{4,49},{5,20},{6,51},{7,22},{8,53},{9,... | collective-permute-start | bytes 1228808 | tf_op jit(solution)/shard_map/ppermute | solution.py:57
  208.5 8.9 %collective-permute-start.28 = (f32[2,2,8,128]{3,2,1,0:T(8,128)S(1)}, f32[2,2,8,128]{3,2,1,0:T(8,128)S(1)}, u32[]{:S(2)}, u32[]{:S(2)}) collective-permute-start(f32[2,2,8,128]{3,2,1,0:T(8,128)S(1)} %slice_bitcast_fusion.1), channel_id=1, source_target_pairs={{0,2},{1,3},{2,0},{3,1},{4,6},{5,7},{6,4},{7,5},{8,10},{9,11},{10,... | collective-permute-start | bytes 49160 | tf_op jit(solution)/shard_map/ppermute | solution.py:57
  217.6 4.2 %collective-permute-done.28.far = f32[2,2,8,128]{3,2,1,0:T(8,128)S(1)} collective-permute-done((f32[2,2,8,128]{3,2,1,0:T(8,128)S(1)}, f32[2,2,8,128]{3,2,1,0:T(8,128)S(1)}, u32[]{:S(2)}, u32[]{:S(2)}) %collective-permute-start.28) | collective-permute-done | bytes 16416 | tf_op jit(solution)/shard_map/ppermute | solution.py:57
  221.8 4.5 %shard_map.90 = (f32[2,9,2,8,128]{4,3,2,1,0:T(8,128)S(1)}, f32[8,2,8,128]{3,2,1,0:T(8,128)S(1)}) custom-call(s32[4]{0:T(128)S(1)} %copy-done.1, s32[16]{0:T(128)S(1)} %copy-done.2, s32[3,256]{1,0:T(4,128)S(1)} %copy-done, s32[256]{0:T(256)S(1)} %copy-done.4, s32[2]{0:T(128)S(1)} %copy-done.3, f32[16,256]{1,0:T(8,128)S(1)} %compare_select_fusion.11.traces, ...), custom_call_target="tpu_custom_call" | custom-call | tf_op jit(solution)/shard_map/pallas_call | solution.py:461
  226.4 5.1 %collective-permute-start.30 = (f32[2,9,2,8,128]{4,3,2,0,1:T(8,128)S(1)}, f32[2,9,2,8,128]{4,3,2,0,1:T(8,128)S(1)}, u32[]{:S(2)}, u32[]{:S(2)}) collective-permute-start(f32[2,9,2,8,128]{4,3,2,0,1:T(8,128)S(1)} %copy.104), channel_id=1, source_target_pairs={{0,450},{1,451},{2,448},{3,449},{4,454},{5,455},{6,452},{7,453},{8... | collective-permute-start | bytes 442376 | tf_op jit(solution)/shard_map/ppermute | solution.py:57
  233.6 5.2 %collective-permute-done.29 = f32[2,9,2,8,128]{4,3,2,0,1:T(8,128)S(1)} collective-permute-done((f32[2,9,2,8,128]{4,3,2,0,1:T(8,128)S(1)}, f32[2,9,2,8,128]{4,3,2,0,1:T(8,128)S(1)}, u32[]{:S(2)}, u32[]{:S(2)}) %collective-permute-start.29) | collective-permute-done | bytes 147488 | tf_op jit(solution)/shard_map/ppermute | solution.py:57
  238.8 5.6 %collective-permute-start.32 = (f32[2,25,2,8,128]{4,3,2,0,1:T(8,128)S(1)}, f32[2,25,2,8,128]{4,3,2,0,1:T(8,128)S(1)}, u32[]{:S(2)}, u32[]{:S(2)}) collective-permute-start(f32[2,25,2,8,128]{4,3,2,0,1:T(8,128)S(1)} %pad_maximum_fusion.2), channel_id=1, source_target_pairs={{0,61},{1,16},{2,63},{3,18},{4,49},{5,20},{6,51},{7,22},{8,53},{9,... | collective-permute-start | bytes 1228808 | tf_op jit(solution)/shard_map/ppermute | solution.py:57
  244.4 1.9 collective-permute-start.31
  246.4 3.8 %collective-permute-done.32 = f32[2,25,2,8,128]{4,3,2,0,1:T(8,128)S(1)} collective-permute-done((f32[2,25,2,8,128]{4,3,2,0,1:T(8,128)S(1)}, f32[2,25,2,8,128]{4,3,2,0,1:T(8,128)S(1)}, u32[]{:S(2)}, u32[]{:S(2)}) %collective-permute-start.32) | collective-permute-done | bytes 409632 | tf_op jit(solution)/shard_map/ppermute | solution.py:57
  250.3 4.5 %shard_map.91 = (f32[2,9,2,8,128]{4,3,2,1,0:T(8,128)S(1)}, f32[8,2,8,128]{3,2,1,0:T(8,128)S(1)}) custom-call(s32[4]{0:T(128)S(1)} %copy-done.1, s32[16]{0:T(128)S(1)} %copy-done.2, s32[3,256]{1,0:T(4,128)S(1)} %copy-done, s32[256]{0:T(256)S(1)} %copy-done.4, s32[2]{0:T(128)S(1)} %copy-done.3, f32[16,256]{1,0:T(8,128)S(1)} %compare_select_fusion.11.traces, ...), custom_call_target="tpu_custom_call" | custom-call | tf_op jit(solution)/shard_map/pallas_call | solution.py:461
  254.8 3.5 %collective-permute-start.34 = (f32[2,9,2,8,128]{4,3,2,0,1:T(8,128)S(1)}, f32[2,9,2,8,128]{4,3,2,0,1:T(8,128)S(1)}, u32[]{:S(2)}, u32[]{:S(2)}) collective-permute-start(f32[2,9,2,8,128]{4,3,2,0,1:T(8,128)S(1)} %copy.112), channel_id=1, source_target_pairs={{0,450},{1,451},{2,448},{3,449},{4,454},{5,455},{6,452},{7,453},{8... | collective-permute-start | bytes 442376 | tf_op jit(solution)/shard_map/ppermute | solution.py:57
  258.3 1.9 collective-permute-start.33
  260.3 4.5 %collective-permute-start.36 = (f32[4,2,8,128]{3,2,0,1:T(8,128)S(1)}, f32[4,2,8,128]{3,2,0,1:T(8,128)S(1)}, u32[]{:S(2)}, u32[]{:S(2)}) collective-permute-start(f32[4,2,8,128]{3,2,0,1:T(8,128)S(1)} %get-tuple-element.68), channel_id=1, source_target_pairs={{0,16},{1,17},{2,272},{3,273},{4,20},{5,21},{6,276},{7,277},{8,24}... | collective-permute-start | bytes 98312 | tf_op jit(solution)/shard_map/ppermute | solution.py:57
  264.8 6.4 %collective-permute-start.35 = (f32[4,2,8,128]{3,2,0,1:T(8,128)S(1)}, f32[4,2,8,128]{3,2,0,1:T(8,128)S(1)}, u32[]{:S(2)}, u32[]{:S(2)}) collective-permute-start(f32[4,2,8,128]{3,2,0,1:T(8,128)S(1)} %get-tuple-element.69), channel_id=1, source_target_pairs={{0,0},{1,1},{2,256},{3,257},{4,4},{5,5},{6,260},{7,261},{8,8},{9,9... | collective-permute-start | bytes 98312 | tf_op jit(solution)/shard_map/ppermute | solution.py:57
  271.3 3.5 %collective-permute-done.35 = f32[4,2,8,128]{3,2,0,1:T(8,128)S(1)} collective-permute-done((f32[4,2,8,128]{3,2,0,1:T(8,128)S(1)}, f32[4,2,8,128]{3,2,0,1:T(8,128)S(1)}, u32[]{:S(2)}, u32[]{:S(2)}) %collective-permute-start.35) | collective-permute-done | bytes 32800 | tf_op jit(solution)/shard_map/ppermute | solution.py:57
  276.8 8.1 %collective-permute-start.37 = (f32[2,25,2,8,128]{4,3,2,0,1:T(8,128)S(1)}, f32[2,25,2,8,128]{4,3,2,0,1:T(8,128)S(1)}, u32[]{:S(2)}, u32[]{:S(2)}) collective-permute-start(f32[2,25,2,8,128]{4,3,2,0,1:T(8,128)S(1)} %pad_maximum_fusion.3), channel_id=1, source_target_pairs={{0,1},{1,0},{2,3},{3,2},{4,5},{5,4},{6,7},{7,6},{8,9},{9,8},{10,11... | collective-permute-start | bytes 1228808 | tf_op jit(solution)/shard_map/ppermute | solution.py:57
  288.8 3.4 %shard_map.92 = (f32[2,9,2,8,128]{4,3,2,1,0:T(8,128)S(1)}, f32[8,2,8,128]{3,2,1,0:T(8,128)S(1)}) custom-call(s32[4]{0:T(128)S(1)} %copy-done.1, s32[16]{0:T(128)S(1)} %copy-done.2, s32[3,256]{1,0:T(4,128)S(1)} %copy-done, s32[256]{0:T(256)S(1)} %copy-done.4, s32[2]{0:T(128)S(1)} %copy-done.3, f32[16,256]{1,0:T(8,128)S(1)} %compare_select_fusion.11.traces, ...), custom_call_target="tpu_custom_call" | custom-call | tf_op jit(solution)/shard_map/pallas_call | solution.py:461
  292.2 4.0 %collective-permute-start.42 = (f32[2,2,8,128]{3,2,1,0:T(8,128)S(1)}, f32[2,2,8,128]{3,2,1,0:T(8,128)S(1)}, u32[]{:S(2)}, u32[]{:S(2)}) collective-permute-start(f32[2,2,8,128]{3,2,1,0:T(8,128)S(1)} %slice_bitcast_fusion.2), channel_id=1, source_target_pairs={{0,4},{1,5},{2,6},{3,7},{4,8},{5,9},{6,10},{7,11},{8,12},{9,13},{1... | collective-permute-start | bytes 49160 | tf_op jit(solution)/shard_map/ppermute | solution.py:57
  296.2 6.4 %collective-permute-done.42 = f32[2,2,8,128]{3,2,1,0:T(8,128)S(1)} collective-permute-done((f32[2,2,8,128]{3,2,1,0:T(8,128)S(1)}, f32[2,2,8,128]{3,2,1,0:T(8,128)S(1)}, u32[]{:S(2)}, u32[]{:S(2)}) %collective-permute-start.42) | collective-permute-done | bytes 16416 | tf_op jit(solution)/shard_map/ppermute | solution.py:57
  302.6 3.4 %collective-permute-start.43 = (f32[2,2,8,128]{3,2,1,0:T(8,128)S(1)}, f32[2,2,8,128]{3,2,1,0:T(8,128)S(1)}, u32[]{:S(2)}, u32[]{:S(2)}) collective-permute-start(f32[2,2,8,128]{3,2,1,0:T(8,128)S(1)} %compare_select_fusion.1), channel_id=1, source_target_pairs={{0,8},{1,9},{2,10},{3,11},{4,12},{5,13},{6,14},{7,15},{8,0},{9,1},... | collective-permute-start | bytes 49160 | tf_op jit(solution)/shard_map/ppermute | solution.py:57
  306.0 9.6 %collective-permute-start.40 = (f32[4,2,8,128]{3,2,1,0:T(8,128)S(1)}, f32[4,2,8,128]{3,2,1,0:T(8,128)S(1)}, u32[]{:S(2)}, u32[]{:S(2)}) collective-permute-start(f32[4,2,8,128]{3,2,1,0:T(8,128)S(1)} %get-tuple-element.66), channel_id=1, source_target_pairs={{0,16},{1,17},{2,272},{3,273},{4,20},{5,21},{6,276},{7,277},{8,24}... | collective-permute-start | bytes 98312 | tf_op jit(solution)/shard_map/ppermute | solution.py:57
  315.6 4.7 %collective-permute-start.39 = (f32[4,2,8,128]{3,2,0,1:T(8,128)S(1)}, f32[4,2,8,128]{3,2,0,1:T(8,128)S(1)}, u32[]{:S(2)}, u32[]{:S(2)}) collective-permute-start(f32[4,2,8,128]{3,2,0,1:T(8,128)S(1)} %copy_select_fusion.1), channel_id=1, source_target_pairs={{0,0},{1,1},{2,256},{3,257},{4,4},{5,5},{6,260},{7,261},{8,8},{9,9... | collective-permute-start | bytes 98312 | tf_op jit(solution)/shard_map/ppermute | solution.py:57
  321.0 4.7 %collective-permute-done.39 = f32[4,2,8,128]{3,2,0,1:T(8,128)S(1)} collective-permute-done((f32[4,2,8,128]{3,2,0,1:T(8,128)S(1)}, f32[4,2,8,128]{3,2,0,1:T(8,128)S(1)}, u32[]{:S(2)}, u32[]{:S(2)}) %collective-permute-start.39) | collective-permute-done | bytes 32800 | tf_op jit(solution)/shard_map/ppermute | solution.py:57
  325.7 7.8 %collective-permute-start.41 = (f32[4,2,8,128]{3,2,0,1:T(8,128)S(1)}, f32[4,2,8,128]{3,2,0,1:T(8,128)S(1)}, u32[]{:S(2)}, u32[]{:S(2)}) collective-permute-start(f32[4,2,8,128]{3,2,0,1:T(8,128)S(1)} %select_bitcast_fusion.4), channel_id=1, source_target_pairs={{0,1},{1,0},{2,3},{3,2},{4,5},{5,4},{6,7},{7,6},{8,9},{9,8},{10,11... | collective-permute-start | bytes 98312 | tf_op jit(solution)/shard_map/ppermute | solution.py:57
  334.6 2.5 psum.7
  (121 shorter events, 31.7 us)
Async XLA Ops:
  3.4 3.6 %collective-permute-start = (f32[6,4,2,8,128]{4,3,1,0,2:T(8,128)S(1)}, f32[6,4,2,8,128]{4,3,1,0,2:T(8,128)S(1)}, u32[]{:S(2)}, u32[]{:S(2)}) collective-permute-start(f32[6,4,2,8,128]{4,3,1,0,2:T(8,128)S(1)} %select_bitcast_fusion.2), channel_id=1, source_target_pairs={{0,1},{1,0},{2,3},{3,2},{4,5},{5,4},{6,7},{7,6},{8,9},{9,8},{10,11... | collective-permute-start | bytes 589832 | tf_op jit(solution)/shard_map/ppermute | solution.py:57
  7.1 44.7 %collective-permute-start.1 = (f32[6,4,2,8,128]{4,3,2,1,0:T(8,128)S(1)}, f32[6,4,2,8,128]{4,3,2,1,0:T(8,128)S(1)}, u32[]{:S(2)}, u32[]{:S(2)}) collective-permute-start(f32[6,4,2,8,128]{4,3,2,1,0:T(8,128)S(1)} %get-tuple-element.60), channel_id=1, source_target_pairs={{0,0},{1,1},{2,32},{3,33},{4,4},{5,5},{6,36},{7,37},{8,8},{9,9},{1... | collective-permute-start | bytes 589832 | tf_op jit(solution)/shard_map/ppermute | solution.py:57
  15.4 39.7 %collective-permute-start.2 = (f32[6,4,2,8,128]{4,3,2,1,0:T(8,128)S(1)}, f32[6,4,2,8,128]{4,3,2,1,0:T(8,128)S(1)}, u32[]{:S(2)}, u32[]{:S(2)}) collective-permute-start(f32[6,4,2,8,128]{4,3,2,1,0:T(8,128)S(1)} %get-tuple-element.61), channel_id=1, source_target_pairs={{0,16},{1,17},{2,48},{3,49},{4,20},{5,21},{6,52},{7,53},{8,24},{9,... | collective-permute-start | bytes 589832 | tf_op jit(solution)/shard_map/ppermute | solution.py:57
  55.1 30.0 %copy-start = (s32[3,256]{1,0:T(4,128)S(1)}, s32[3,256]{1,0:T(4,128)}, u32[]{:S(2)}) copy-start(s32[3,256]{1,0:T(4,128)} %receivers.17) | copy-start | bytes 9220
  55.1 30.0 %copy-start.2 = (s32[16]{0:T(128)S(1)}, s32[16]{0:T(128)}, u32[]{:S(2)}) copy-start(s32[16]{0:T(128)} %checkpoints.15) | copy-start | bytes 196
  55.3 9.6 %collective-permute-start.4 = (f32[5,8,2,8,128]{4,3,2,1,0:T(8,128)S(1)}, f32[5,8,2,8,128]{4,3,2,1,0:T(8,128)S(1)}, u32[]{:S(2)}, u32[]{:S(2)}) collective-permute-start(f32[5,8,2,8,128]{4,3,2,1,0:T(8,128)S(1)} %pad_maximum_fusion.5), channel_id=1, source_target_pairs={{0,450},{1,451},{2,448},{3,449},{4,454},{5,455},{6,452},{7,453},{8... | collective-permute-start | bytes 983048 | tf_op jit(solution)/shard_map/ppermute | solution.py:57
  57.8 9.7 %collective-permute-start.3 = (f32[5,8,2,8,128]{4,3,2,1,0:T(8,128)S(1)}, f32[5,8,2,8,128]{4,3,2,1,0:T(8,128)S(1)}, u32[]{:S(2)}, u32[]{:S(2)}) collective-permute-start(f32[5,8,2,8,128]{4,3,2,1,0:T(8,128)S(1)} %pad_maximum_fusion.5), channel_id=1, source_target_pairs={{0,64},{1,65},{2,66},{3,67},{4,68},{5,69},{6,70},{7,71},{8,72},{9,... | collective-permute-start | bytes 983048 | tf_op jit(solution)/shard_map/ppermute | solution.py:57
  67.6 17.5 %collective-permute-start.6 = (f32[5,24,2,8,128]{4,3,2,1,0:T(8,128)S(1)}, f32[5,24,2,8,128]{4,3,2,1,0:T(8,128)S(1)}, u32[]{:S(2)}, u32[]{:S(2)}) collective-permute-start(f32[5,24,2,8,128]{4,3,2,1,0:T(8,128)S(1)} %pad_maximum_fusion.mid), channel_id=1, source_target_pairs={{0,61},{1,16},{2,63},{3,18},{4,49},{5,20},{6,51},{7,22},{8,53},{9,... | collective-permute-start | bytes 2949128 | tf_op jit(solution)/shard_map/ppermute | solution.py:57
  69.5 15.6 %collective-permute-start.5 = (f32[5,24,2,8,128]{4,3,2,1,0:T(8,128)S(1)}, f32[5,24,2,8,128]{4,3,2,1,0:T(8,128)S(1)}, u32[]{:S(2)}, u32[]{:S(2)}) collective-permute-start(f32[5,24,2,8,128]{4,3,2,1,0:T(8,128)S(1)} %pad_maximum_fusion.mid), channel_id=1, source_target_pairs={{0,1},{1,0},{2,3},{3,2},{4,5},{5,4},{6,7},{7,6},{8,9},{9,8},{10,11... | collective-permute-start | bytes 2949128 | tf_op jit(solution)/shard_map/ppermute | solution.py:57
  85.2 0.7 copy-start.1
  85.8 0.7 copy-start.3
  86.5 0.7 copy-start.5
  92.2 8.6 %collective-permute-start.7 = (f32[2,8,2,8,128]{4,3,2,1,0:T(8,128)S(1)}, f32[2,8,2,8,128]{4,3,2,1,0:T(8,128)S(1)}, u32[]{:S(2)}, u32[]{:S(2)}) collective-permute-start(f32[2,8,2,8,128]{4,3,2,1,0:T(8,128)S(1)} %get-tuple-element.35), channel_id=1, source_target_pairs={{0,64},{1,65},{2,66},{3,67},{4,68},{5,69},{6,70},{7,71},{8,72},{9,... | collective-permute-start | bytes 393224 | tf_op jit(solution)/shard_map/ppermute | solution.py:57
  94.1 8.4 %collective-permute-start.8 = (f32[2,8,2,8,128]{4,3,2,1,0:T(8,128)S(1)}, f32[2,8,2,8,128]{4,3,2,1,0:T(8,128)S(1)}, u32[]{:S(2)}, u32[]{:S(2)}) collective-permute-start(f32[2,8,2,8,128]{4,3,2,1,0:T(8,128)S(1)} %get-tuple-element.35), channel_id=1, source_target_pairs={{0,450},{1,451},{2,448},{3,449},{4,454},{5,455},{6,452},{7,453},{8... | collective-permute-start | bytes 393224 | tf_op jit(solution)/shard_map/ppermute | solution.py:57
  102.6 11.2 %collective-permute-start.10 = (f32[2,24,2,8,128]{4,3,2,1,0:T(8,128)S(1)}, f32[2,24,2,8,128]{4,3,2,1,0:T(8,128)S(1)}, u32[]{:S(2)}, u32[]{:S(2)}) collective-permute-start(f32[2,24,2,8,128]{4,3,2,1,0:T(8,128)S(1)} %constant_dynamic-update-slice_fusion.mid), channel_id=1, source_target_pairs={{0,61},{1,16},{2,63},{3,18},{4,49},{5,20},{6,51},{7,22},{8,53},{9,... | collective-permute-start | bytes 1179656 | tf_op jit(solution)/shard_map/ppermute | solution.py:57
  108.0 5.8 %collective-permute-start.9 = (f32[2,24,2,8,128]{4,3,2,1,0:T(8,128)S(1)}, f32[2,24,2,8,128]{4,3,2,1,0:T(8,128)S(1)}, u32[]{:S(2)}, u32[]{:S(2)}) collective-permute-start(f32[2,24,2,8,128]{4,3,2,1,0:T(8,128)S(1)} %constant_dynamic-update-slice_fusion.mid), channel_id=1, source_target_pairs={{0,1},{1,0},{2,3},{3,2},{4,5},{5,4},{6,7},{7,6},{8,9},{9,8},{10,11... | collective-permute-start | bytes 1179656 | tf_op jit(solution)/shard_map/ppermute | solution.py:57
  118.4 7.3 %collective-permute-start.11 = (f32[2,8,2,8,128]{4,3,2,1,0:T(8,128)S(1)}, f32[2,8,2,8,128]{4,3,2,1,0:T(8,128)S(1)}, u32[]{:S(2)}, u32[]{:S(2)}) collective-permute-start(f32[2,8,2,8,128]{4,3,2,1,0:T(8,128)S(1)} %get-tuple-element.37), channel_id=1, source_target_pairs={{0,64},{1,65},{2,66},{3,67},{4,68},{5,69},{6,70},{7,71},{8,72},{9,... | collective-permute-start | bytes 393224 | tf_op jit(solution)/shard_map/ppermute | solution.py:57
  121.3 5.8 %collective-permute-start.12 = (f32[2,8,2,8,128]{4,3,2,1,0:T(8,128)S(1)}, f32[2,8,2,8,128]{4,3,2,1,0:T(8,128)S(1)}, u32[]{:S(2)}, u32[]{:S(2)}) collective-permute-start(f32[2,8,2,8,128]{4,3,2,1,0:T(8,128)S(1)} %get-tuple-element.37), channel_id=1, source_target_pairs={{0,450},{1,451},{2,448},{3,449},{4,454},{5,455},{6,452},{7,453},{8... | collective-permute-start | bytes 393224 | tf_op jit(solution)/shard_map/ppermute | solution.py:57
  127.1 11.2 %collective-permute-start.14 = (f32[2,24,2,8,128]{4,3,2,1,0:T(8,128)S(1)}, f32[2,24,2,8,128]{4,3,2,1,0:T(8,128)S(1)}, u32[]{:S(2)}, u32[]{:S(2)}) collective-permute-start(f32[2,24,2,8,128]{4,3,2,1,0:T(8,128)S(1)} %constant_dynamic-update-slice_fusion.3.mid), channel_id=1, source_target_pairs={{0,61},{1,16},{2,63},{3,18},{4,49},{5,20},{6,51},{7,22},{8,53},{9,... | collective-permute-start | bytes 1179656 | tf_op jit(solution)/shard_map/ppermute | solution.py:57
  132.0 6.3 %collective-permute-start.13 = (f32[2,24,2,8,128]{4,3,2,1,0:T(8,128)S(1)}, f32[2,24,2,8,128]{4,3,2,1,0:T(8,128)S(1)}, u32[]{:S(2)}, u32[]{:S(2)}) collective-permute-start(f32[2,24,2,8,128]{4,3,2,1,0:T(8,128)S(1)} %constant_dynamic-update-slice_fusion.3.mid), channel_id=1, source_target_pairs={{0,1},{1,0},{2,3},{3,2},{4,5},{5,4},{6,7},{7,6},{8,9},{9,8},{10,11... | collective-permute-start | bytes 1179656 | tf_op jit(solution)/shard_map/ppermute | solution.py:57
  142.9 7.5 %collective-permute-start.15 = (f32[2,8,2,8,128]{4,3,2,1,0:T(8,128)S(1)}, f32[2,8,2,8,128]{4,3,2,1,0:T(8,128)S(1)}, u32[]{:S(2)}, u32[]{:S(2)}) collective-permute-start(f32[2,8,2,8,128]{4,3,2,1,0:T(8,128)S(1)} %get-tuple-element.39), channel_id=1, source_target_pairs={{0,64},{1,65},{2,66},{3,67},{4,68},{5,69},{6,70},{7,71},{8,72},{9,... | collective-permute-start | bytes 393224 | tf_op jit(solution)/shard_map/ppermute | solution.py:57
  146.0 5.9 %collective-permute-start.16 = (f32[2,8,2,8,128]{4,3,2,1,0:T(8,128)S(1)}, f32[2,8,2,8,128]{4,3,2,1,0:T(8,128)S(1)}, u32[]{:S(2)}, u32[]{:S(2)}) collective-permute-start(f32[2,8,2,8,128]{4,3,2,1,0:T(8,128)S(1)} %get-tuple-element.39), channel_id=1, source_target_pairs={{0,450},{1,451},{2,448},{3,449},{4,454},{5,455},{6,452},{7,453},{8... | collective-permute-start | bytes 393224 | tf_op jit(solution)/shard_map/ppermute | solution.py:57
  150.4 33.9 %copy-start.4 = (s32[256]{0:T(256)S(1)}, s32[256]{0:T(256)}, u32[]{:S(2)}) copy-start(s32[256]{0:T(256)} %get-tuple-element.30.near) | copy-start | bytes 3076
  151.9 11.2 %collective-permute-start.18 = (f32[2,24,2,8,128]{4,3,2,1,0:T(8,128)S(1)}, f32[2,24,2,8,128]{4,3,2,1,0:T(8,128)S(1)}, u32[]{:S(2)}, u32[]{:S(2)}) collective-permute-start(f32[2,24,2,8,128]{4,3,2,1,0:T(8,128)S(1)} %constant_dynamic-update-slice_fusion.6.mid), channel_id=1, source_target_pairs={{0,61},{1,16},{2,63},{3,18},{4,49},{5,20},{6,51},{7,22},{8,53},{9,... | collective-permute-start | bytes 1179656 | tf_op jit(solution)/shard_map/ppermute | solution.py:57
  156.3 6.8 %collective-permute-start.17 = (f32[2,24,2,8,128]{4,3,2,1,0:T(8,128)S(1)}, f32[2,24,2,8,128]{4,3,2,1,0:T(8,128)S(1)}, u32[]{:S(2)}, u32[]{:S(2)}) collective-permute-start(f32[2,24,2,8,128]{4,3,2,1,0:T(8,128)S(1)} %constant_dynamic-update-slice_fusion.6.mid), channel_id=1, source_target_pairs={{0,1},{1,0},{2,3},{3,2},{4,5},{5,4},{6,7},{7,6},{8,9},{9,8},{10,11... | collective-permute-start | bytes 1179656 | tf_op jit(solution)/shard_map/ppermute | solution.py:57
  166.5 7.2 %collective-permute-start.19 = (f32[16,256]{1,0:T(8,128)S(1)}, f32[16,256]{1,0:T(8,128)S(1)}, u32[]{:S(2)}, u32[]{:S(2)}) collective-permute-start(f32[16,256]{1,0:T(8,128)S(1)} %get-tuple-element.41), channel_id=1, source_target_pairs={{0,64},{1,65},{2,66},{3,67},{4,68},{5,69},{6,70},{7,71},{8,72},{9,... | collective-permute-start | bytes 49160 | tf_op jit(solution)/shard_map/ppermute | solution.py:57
  169.7 4.8 %collective-permute-start.20 = (f32[16,256]{1,0:T(8,128)S(1)}, f32[16,256]{1,0:T(8,128)S(1)}, u32[]{:S(2)}, u32[]{:S(2)}) collective-permute-start(f32[16,256]{1,0:T(8,128)S(1)} %get-tuple-element.41), channel_id=1, source_target_pairs={{0,450},{1,451},{2,448},{3,449},{4,454},{5,455},{6,452},{7,453},{8... | collective-permute-start | bytes 49160 | tf_op jit(solution)/shard_map/ppermute | solution.py:57
  174.5 8.5 %collective-permute-start.21 = (f32[16,256]{1,0:T(8,128)S(1)}, f32[16,256]{1,0:T(8,128)S(1)}, u32[]{:S(2)}, u32[]{:S(2)}) collective-permute-start(f32[16,256]{1,0:T(8,128)S(1)} %compare_select_fusion.13), channel_id=1, source_target_pairs={{0,61},{1,16},{2,63},{3,18},{4,49},{5,20},{6,51},{7,22},{8,53},{9,... | collective-permute-start | bytes 49160 | tf_op jit(solution)/shard_map/ppermute | solution.py:57
  181.1 3.1 collective-permute-start.22
  189.0 8.8 %collective-permute-start.24 = (f32[2,9,2,8,128]{4,3,2,0,1:T(8,128)S(1)}, f32[2,9,2,8,128]{4,3,2,0,1:T(8,128)S(1)}, u32[]{:S(2)}, u32[]{:S(2)}) collective-permute-start(f32[2,9,2,8,128]{4,3,2,0,1:T(8,128)S(1)} %copy.97), channel_id=1, source_target_pairs={{0,450},{1,451},{2,448},{3,449},{4,454},{5,455},{6,452},{7,453},{8... | collective-permute-start | bytes 442376 | tf_op jit(solution)/shard_map/ppermute | solution.py:57
  193.2 9.5 %collective-permute-start.23 = (f32[2,9,2,8,128]{4,3,2,0,1:T(8,128)S(1)}, f32[2,9,2,8,128]{4,3,2,0,1:T(8,128)S(1)}, u32[]{:S(2)}, u32[]{:S(2)}) collective-permute-start(f32[2,9,2,8,128]{4,3,2,0,1:T(8,128)S(1)} %copy.97), channel_id=1, source_target_pairs={{0,64},{1,65},{2,66},{3,67},{4,68},{5,69},{6,70},{7,71},{8,72},{9,... | collective-permute-start | bytes 442376 | tf_op jit(solution)/shard_map/ppermute | solution.py:57
  195.5 7.2 %collective-permute-start.25 = (f32[2,2,8,128]{3,2,1,0:T(8,128)S(1)}, f32[2,2,8,128]{3,2,1,0:T(8,128)S(1)}, u32[]{:S(2)}, u32[]{:S(2)}) collective-permute-start(f32[2,2,8,128]{3,2,1,0:T(8,128)S(1)} %bitcast.70), channel_id=1, source_target_pairs={{0,1},{1,0},{2,3},{3,2},{4,5},{5,4},{6,7},{7,6},{8,9},{9,8},{10,11... | collective-permute-start | bytes 49160 | tf_op jit(solution)/shard_map/ppermute | solution.py:57
  202.7 14.8 %collective-permute-start.27 = (f32[2,25,2,8,128]{4,3,2,0,1:T(8,128)S(1)}, f32[2,25,2,8,128]{4,3,2,0,1:T(8,128)S(1)}, u32[]{:S(2)}, u32[]{:S(2)}) collective-permute-start(f32[2,25,2,8,128]{4,3,2,0,1:T(8,128)S(1)} %pad_maximum_fusion.1), channel_id=1, source_target_pairs={{0,61},{1,16},{2,63},{3,18},{4,49},{5,20},{6,51},{7,22},{8,53},{9,... | collective-permute-start | bytes 1228808 | tf_op jit(solution)/shard_map/ppermute | solution.py:57
  206.6 11.0 %collective-permute-start.26 = (f32[2,25,2,8,128]{4,3,2,0,1:T(8,128)S(1)}, f32[2,25,2,8,128]{4,3,2,0,1:T(8,128)S(1)}, u32[]{:S(2)}, u32[]{:S(2)}) collective-permute-start(f32[2,25,2,8,128]{4,3,2,0,1:T(8,128)S(1)} %pad_maximum_fusion.1), channel_id=1, source_target_pairs={{0,1},{1,0},{2,3},{3,2},{4,5},{5,4},{6,7},{7,6},{8,9},{9,8},{10,11... | collective-permute-start | bytes 1228808 | tf_op jit(solution)/shard_map/ppermute | solution.py:57
  208.5 13.3 %collective-permute-start.28 = (f32[2,2,8,128]{3,2,1,0:T(8,128)S(1)}, f32[2,2,8,128]{3,2,1,0:T(8,128)S(1)}, u32[]{:S(2)}, u32[]{:S(2)}) collective-permute-start(f32[2,2,8,128]{3,2,1,0:T(8,128)S(1)} %slice_bitcast_fusion.1), channel_id=1, source_target_pairs={{0,2},{1,3},{2,0},{3,1},{4,6},{5,7},{6,4},{7,5},{8,10},{9,11},{10,... | collective-permute-start | bytes 49160 | tf_op jit(solution)/shard_map/ppermute | solution.py:57
  226.4 7.2 %collective-permute-start.30 = (f32[2,9,2,8,128]{4,3,2,0,1:T(8,128)S(1)}, f32[2,9,2,8,128]{4,3,2,0,1:T(8,128)S(1)}, u32[]{:S(2)}, u32[]{:S(2)}) collective-permute-start(f32[2,9,2,8,128]{4,3,2,0,1:T(8,128)S(1)} %copy.104), channel_id=1, source_target_pairs={{0,450},{1,451},{2,448},{3,449},{4,454},{5,455},{6,452},{7,453},{8... | collective-permute-start | bytes 442376 | tf_op jit(solution)/shard_map/ppermute | solution.py:57
  231.5 7.3 %collective-permute-start.29 = (f32[2,9,2,8,128]{4,3,2,0,1:T(8,128)S(1)}, f32[2,9,2,8,128]{4,3,2,0,1:T(8,128)S(1)}, u32[]{:S(2)}, u32[]{:S(2)}) collective-permute-start(f32[2,9,2,8,128]{4,3,2,0,1:T(8,128)S(1)} %copy.104), channel_id=1, source_target_pairs={{0,64},{1,65},{2,66},{3,67},{4,68},{5,69},{6,70},{7,71},{8,72},{9,... | collective-permute-start | bytes 442376 | tf_op jit(solution)/shard_map/ppermute | solution.py:57
  238.8 11.4 %collective-permute-start.32 = (f32[2,25,2,8,128]{4,3,2,0,1:T(8,128)S(1)}, f32[2,25,2,8,128]{4,3,2,0,1:T(8,128)S(1)}, u32[]{:S(2)}, u32[]{:S(2)}) collective-permute-start(f32[2,25,2,8,128]{4,3,2,0,1:T(8,128)S(1)} %pad_maximum_fusion.2), channel_id=1, source_target_pairs={{0,61},{1,16},{2,63},{3,18},{4,49},{5,20},{6,51},{7,22},{8,53},{9,... | collective-permute-start | bytes 1228808 | tf_op jit(solution)/shard_map/ppermute | solution.py:57
  244.4 5.8 %collective-permute-start.31 = (f32[2,25,2,8,128]{4,3,2,0,1:T(8,128)S(1)}, f32[2,25,2,8,128]{4,3,2,0,1:T(8,128)S(1)}, u32[]{:S(2)}, u32[]{:S(2)}) collective-permute-start(f32[2,25,2,8,128]{4,3,2,0,1:T(8,128)S(1)} %pad_maximum_fusion.2), channel_id=1, source_target_pairs={{0,1},{1,0},{2,3},{3,2},{4,5},{5,4},{6,7},{7,6},{8,9},{9,8},{10,11... | collective-permute-start | bytes 1228808 | tf_op jit(solution)/shard_map/ppermute | solution.py:57
  254.8 16.4 %collective-permute-start.34 = (f32[2,9,2,8,128]{4,3,2,0,1:T(8,128)S(1)}, f32[2,9,2,8,128]{4,3,2,0,1:T(8,128)S(1)}, u32[]{:S(2)}, u32[]{:S(2)}) collective-permute-start(f32[2,9,2,8,128]{4,3,2,0,1:T(8,128)S(1)} %copy.112), channel_id=1, source_target_pairs={{0,450},{1,451},{2,448},{3,449},{4,454},{5,455},{6,452},{7,453},{8... | collective-permute-start | bytes 442376 | tf_op jit(solution)/shard_map/ppermute | solution.py:57
  258.3 12.9 %collective-permute-start.33 = (f32[2,9,2,8,128]{4,3,2,0,1:T(8,128)S(1)}, f32[2,9,2,8,128]{4,3,2,0,1:T(8,128)S(1)}, u32[]{:S(2)}, u32[]{:S(2)}) collective-permute-start(f32[2,9,2,8,128]{4,3,2,0,1:T(8,128)S(1)} %copy.112), channel_id=1, source_target_pairs={{0,64},{1,65},{2,66},{3,67},{4,68},{5,69},{6,70},{7,71},{8,72},{9,... | collective-permute-start | bytes 442376 | tf_op jit(solution)/shard_map/ppermute | solution.py:57
  260.3 11.1 %collective-permute-start.36 = (f32[4,2,8,128]{3,2,0,1:T(8,128)S(1)}, f32[4,2,8,128]{3,2,0,1:T(8,128)S(1)}, u32[]{:S(2)}, u32[]{:S(2)}) collective-permute-start(f32[4,2,8,128]{3,2,0,1:T(8,128)S(1)} %get-tuple-element.68), channel_id=1, source_target_pairs={{0,16},{1,17},{2,272},{3,273},{4,20},{5,21},{6,276},{7,277},{8,24}... | collective-permute-start | bytes 98312 | tf_op jit(solution)/shard_map/ppermute | solution.py:57
  264.8 10.1 %collective-permute-start.35 = (f32[4,2,8,128]{3,2,0,1:T(8,128)S(1)}, f32[4,2,8,128]{3,2,0,1:T(8,128)S(1)}, u32[]{:S(2)}, u32[]{:S(2)}) collective-permute-start(f32[4,2,8,128]{3,2,0,1:T(8,128)S(1)} %get-tuple-element.69), channel_id=1, source_target_pairs={{0,0},{1,1},{2,256},{3,257},{4,4},{5,5},{6,260},{7,261},{8,8},{9,9... | collective-permute-start | bytes 98312 | tf_op jit(solution)/shard_map/ppermute | solution.py:57
  274.9 13.8 %collective-permute-start.38 = (f32[2,25,2,8,128]{4,3,2,0,1:T(8,128)S(1)}, f32[2,25,2,8,128]{4,3,2,0,1:T(8,128)S(1)}, u32[]{:S(2)}, u32[]{:S(2)}) collective-permute-start(f32[2,25,2,8,128]{4,3,2,0,1:T(8,128)S(1)} %pad_maximum_fusion.3), channel_id=1, source_target_pairs={{0,61},{1,16},{2,63},{3,18},{4,49},{5,20},{6,51},{7,22},{8,53},{9,... | collective-permute-start | bytes 1228808 | tf_op jit(solution)/shard_map/ppermute | solution.py:57
  276.8 11.9 %collective-permute-start.37 = (f32[2,25,2,8,128]{4,3,2,0,1:T(8,128)S(1)}, f32[2,25,2,8,128]{4,3,2,0,1:T(8,128)S(1)}, u32[]{:S(2)}, u32[]{:S(2)}) collective-permute-start(f32[2,25,2,8,128]{4,3,2,0,1:T(8,128)S(1)} %pad_maximum_fusion.3), channel_id=1, source_target_pairs={{0,1},{1,0},{2,3},{3,2},{4,5},{5,4},{6,7},{7,6},{8,9},{9,8},{10,11... | collective-permute-start | bytes 1228808 | tf_op jit(solution)/shard_map/ppermute | solution.py:57
  284.9 3.1 collective-permute-start.44
  292.2 10.4 %collective-permute-start.42 = (f32[2,2,8,128]{3,2,1,0:T(8,128)S(1)}, f32[2,2,8,128]{3,2,1,0:T(8,128)S(1)}, u32[]{:S(2)}, u32[]{:S(2)}) collective-permute-start(f32[2,2,8,128]{3,2,1,0:T(8,128)S(1)} %slice_bitcast_fusion.2), channel_id=1, source_target_pairs={{0,4},{1,5},{2,6},{3,7},{4,8},{5,9},{6,10},{7,11},{8,12},{9,13},{1... | collective-permute-start | bytes 49160 | tf_op jit(solution)/shard_map/ppermute | solution.py:57
  302.6 17.8 %collective-permute-start.43 = (f32[2,2,8,128]{3,2,1,0:T(8,128)S(1)}, f32[2,2,8,128]{3,2,1,0:T(8,128)S(1)}, u32[]{:S(2)}, u32[]{:S(2)}) collective-permute-start(f32[2,2,8,128]{3,2,1,0:T(8,128)S(1)} %compare_select_fusion.1), channel_id=1, source_target_pairs={{0,8},{1,9},{2,10},{3,11},{4,12},{5,13},{6,14},{7,15},{8,0},{9,1},... | collective-permute-start | bytes 49160 | tf_op jit(solution)/shard_map/ppermute | solution.py:57
  306.0 15.0 %collective-permute-start.40 = (f32[4,2,8,128]{3,2,1,0:T(8,128)S(1)}, f32[4,2,8,128]{3,2,1,0:T(8,128)S(1)}, u32[]{:S(2)}, u32[]{:S(2)}) collective-permute-start(f32[4,2,8,128]{3,2,1,0:T(8,128)S(1)} %get-tuple-element.66), channel_id=1, source_target_pairs={{0,16},{1,17},{2,272},{3,273},{4,20},{5,21},{6,276},{7,277},{8,24}... | collective-permute-start | bytes 98312 | tf_op jit(solution)/shard_map/ppermute | solution.py:57
  315.6 10.1 %collective-permute-start.39 = (f32[4,2,8,128]{3,2,0,1:T(8,128)S(1)}, f32[4,2,8,128]{3,2,0,1:T(8,128)S(1)}, u32[]{:S(2)}, u32[]{:S(2)}) collective-permute-start(f32[4,2,8,128]{3,2,0,1:T(8,128)S(1)} %copy_select_fusion.1), channel_id=1, source_target_pairs={{0,0},{1,1},{2,256},{3,257},{4,4},{5,5},{6,260},{7,261},{8,8},{9,9... | collective-permute-start | bytes 98312 | tf_op jit(solution)/shard_map/ppermute | solution.py:57
  325.7 8.6 %collective-permute-start.41 = (f32[4,2,8,128]{3,2,0,1:T(8,128)S(1)}, f32[4,2,8,128]{3,2,0,1:T(8,128)S(1)}, u32[]{:S(2)}, u32[]{:S(2)}) collective-permute-start(f32[4,2,8,128]{3,2,0,1:T(8,128)S(1)} %select_bitcast_fusion.4), channel_id=1, source_target_pairs={{0,1},{1,0},{2,3},{3,2},{4,5},{5,4},{6,7},{7,6},{8,9},{9,8},{10,11... | collective-permute-start | bytes 98312 | tf_op jit(solution)/shard_map/ppermute | solution.py:57

commit v3 on v2

--- a/solution.py
+++ b/solution.py
@@ -47,6 +47,14 @@
     return (index % 4, index // 4, z, 1 - c)
 
 
+def around(by):
+    def place(x, y, z, c):
+        index = (4 * y + x + by) % 16
+        return (index % 4, index // 4, z, c)
+
+    return table(place)
+
+
 SWAP = shifted(dc=1)
 ACROSS = table(across)
 UP = shifted(dz=1)
@@ -75,9 +83,7 @@
     return jnp.concatenate([one, one], axis=0)
 
 
-def depth_part(buf, deep, bands, margin):
-    first, count = B - margin, B + 2 * margin
-    low, size = (PAD, R) if margin > 0 else (PAD + 8, 8)
+def depth_part(buf, bands, first, count, low, size):
     field = jnp.concatenate(
         [
             buf[first : first + count, half, low : low + size, :].reshape(count * size, 128)
@@ -87,29 +93,42 @@
     )
     high = field.astype(jnp.bfloat16)
     rest = (field - high.astype(jnp.float32)).astype(jnp.bfloat16)
-    out = jnp.dot(
+    return jnp.dot(
         jnp.concatenate([high, rest], axis=1), bands[...], preferred_element_type=jnp.float32
     )
-    for half in range(2):
-        deep[first : first + count, half, low - PAD : low - PAD + size, :] = out[
-            :, 128 * half : 128 * half + 128
-        ].reshape(count, size, 128)
-
-
-def laplace_tile(buf, deep, x, half, row):
-    here = buf[x, half, row : row + 8, :]
-    near = (buf[x - 1, half, row : row + 8, :] + buf[x + 1, half, row : row + 8, :]) + (
-        buf[x, half, row - 1 : row + 7, :] + buf[x, half, row + 1 : row + 9, :]
-    )
-    far = (buf[x - 2, half, row : row + 8, :] + buf[x + 2, half, row : row + 8, :]) + (
-        buf[x, half, row - 2 : row + 6, :] + buf[x, half, row + 2 : row + 10, :]
-    )
-    depth = deep[x, half, row - PAD : row - PAD + 8, :]
-    return here, (16.0 * near - far) + (depth - 90.0 * here)
-
-
-def tiles_for(margin):
-    return (PAD, PAD + 8, PAD + 16) if margin > 0 else (PAD + 8,)
+
+
+def laplace_planes(buf, bands, first, count, low, size, update):
+    deep = depth_part(buf, bands, first, count, low, size)
+    for i in range(count):
+        x = first + i
+        for row in range(low, low + size, 8):
+            at = i * size + row - low
+            for half in range(2):
+                here = buf[x, half, row : row + 8, :]
+                near = (buf[x - 1, half, row : row + 8, :] + buf[x + 1, half, row : row + 8, :]) + (
+                    buf[x, half, row - 1 : row + 7, :] + buf[x, half, row + 1 : row + 9, :]
+                )
+                far = (buf[x - 2, half, row : row + 8, :] + buf[x + 2, half, row : row + 8, :]) + (
+                    buf[x, half, row - 2 : row + 6, :] + buf[x, half, row + 2 : row + 10, :]
+                )
+                depth = deep[at : at + 8, 128 * half : 128 * half + 128]
+                update((x, half, row), (16.0 * near - far) + (depth - 90.0 * here), here)
+
+
+GROUP = 4
+
+
+def laplace_step(buf, bands, left, update):
+    margin = 2 * left
+    if left == 0:
+        laplace_planes(buf, bands, B, B, PAD + 8, 8, update)
+        return
+
+    for first in range(B - margin + 2, 2 * B + margin - 2, GROUP):
+        laplace_planes(buf, bands, first, GROUP, PAD, R, update)
+    laplace_planes(buf, bands, B - margin, 2, PAD + 8, 8, update)
+    laplace_planes(buf, bands, 2 * B + margin - 2, 2, PAD + 8, 8, update)
 
 
 def assemble(buf, f, mid, intra, inter, core):
@@ -147,30 +166,24 @@
     lax.fori_loop(0, counts[0], body, 0)
 
 
-def forward_steps(steps, a, b, deep, bands, vel, src, place, checkpoints, receivers, mine, counts, traces):
+def forward_steps(steps, a, b, bands, vel, src, place, checkpoints, receivers, mine, counts, traces):
     for done, step in enumerate(steps):
-        margin = 2 * (len(steps) - 1 - done)
         ck = checkpoints[step]
 
-        depth_part(b, deep, bands, margin)
-
-        def plane(x, _, a=a, b=b, margin=margin, ck=ck):
-            for row in tiles_for(margin):
-                for half in range(2):
-                    here, lap = laplace_tile(b, deep, x, half, row)
-                    at = (x, half, slice(row, row + 8), slice(None))
-                    cell = (x, half, slice(row - PAD, row - PAD + 8), slice(None))
-                    a[at] = 2.0 * here - a[at] + vel[cell] * lap + src[(ck, *cell)]
-            return 0
-
-        lax.fori_loop(B - margin, 2 * B + margin, plane, 0)
+        def update(cell, lap, here, a=a, ck=ck):
+            x, half, row = cell
+            at = (x, half, slice(row, row + 8), slice(None))
+            fixed = (x, half, slice(row - PAD, row - PAD + 8), slice(None))
+            a[at] = (2.0 * here - a[at]) + (vel[fixed] * lap + src[(ck, *fixed)])
+
+        laplace_step(b, bands, len(steps) - 1 - done, update)
         a, b = b, a
         sample(b, step, place, receivers, mine, counts, traces)
     return a, b
 
 
 def first_forward(
-    place, checkpoints, receivers, mine, counts, mid, intra, inter, vel, src, pair, traces, a, b, deep, bands
+    place, checkpoints, receivers, mine, counts, mid, intra, inter, vel, src, pair, traces, a, b, bands
 ):
     core = place[2]
     for f in range(5):
@@ -188,12 +201,13 @@
             into[:, :, 16:24, :] = inter[f]
 
     bands[...] = band()
+    vel[...] = vel[...] * (1.0 / 12.0)
     traces[...] = jnp.zeros_like(traces)
     a[...] = jnp.zeros_like(a)
     b[:, :, PAD : PAD + R, :] = src[checkpoints[0]]
     sample(b, 0, place, receivers, mine, counts, traces)
     prev, cur = forward_steps(
-        range(1, 5), a, b, deep, bands, vel, src, place, checkpoints, receivers, mine, counts, traces
+        range(1, 5), a, b, bands, vel, src, place, checkpoints, receivers, mine, counts, traces
     )
     pair[0] = own(prev)
     pair[1] = own(cur)
@@ -201,14 +215,14 @@
 
 def later_forward(
     steps, place, checkpoints, receivers, mine, counts, vel, src, mid, intra, inter, held,
-    pair, traces, a, b, deep, bands,
+    pair, traces, a, b, bands,
 ):
     assemble(a, 0, mid, intra, inter, place[2])
     assemble(b, 1, mid, intra, inter, place[2])
     bands[...] = band()
     traces[...] = held[...]
     prev, cur = forward_steps(
-        steps, a, b, deep, bands, vel, src, place, checkpoints, receivers, mine, counts, traces
+        steps, a, b, bands, vel, src, place, checkpoints, receivers, mine, counts, traces
     )
     pair[0] = own(prev)
     pair[1] = own(cur)
@@ -235,31 +249,23 @@
 
 
 def adjoint_steps(
-    steps, a, b, w, deep, bands, vel, back_own, place, checkpoints, receivers, near, counts, traces, image
+    steps, a, b, w, bands, vel, back_own, place, checkpoints, receivers, near, counts, traces, image
 ):
     for done, step in enumerate(steps):
         margin = 2 * (len(steps) - 1 - done)
 
-        def scale(x, _, b=b):
-            for row in tiles_for(1):
+        for x in range(B - margin - 2, 2 * B + margin + 2):
+            for row in (PAD, PAD + 8, PAD + 16):
                 for half in range(2):
                     at = (x, half, slice(row, row + 8), slice(None))
                     w[at] = b[at] * vel[x, half, row - PAD : row - PAD + 8, :]
-            return 0
-
-        lax.fori_loop(B - margin - 2, 2 * B + margin + 2, scale, 0)
-
-        depth_part(w, deep, bands, margin)
-
-        def plane(x, _, a=a, b=b, margin=margin):
-            for row in tiles_for(margin):
-                for half in range(2):
-                    _, lap = laplace_tile(w, deep, x, half, row)
-                    at = (x, half, slice(row, row + 8), slice(None))
-                    a[at] = 2.0 * b[at] - a[at] + lap
-            return 0
-
-        lax.fori_loop(B - margin, 2 * B + margin, plane, 0)
+
+        def update(cell, lap, here, a=a, b=b):
+            x, half, row = cell
+            at = (x, half, slice(row, row + 8), slice(None))
+            a[at] = (2.0 * b[at] - a[at]) + lap
+
+        laplace_step(w, bands, len(steps) - 1 - done, update)
         a, b = b, a
         inject(b, step, place, receivers, near, counts, traces)
         add_image(image, b, back_own, checkpoints[step])
@@ -267,7 +273,7 @@
 
 
 def first_adjoint(
-    place, checkpoints, receivers, near, counts, traces, vel, back_own, carried, pair, image, a, b, w, deep, bands
+    place, checkpoints, receivers, near, counts, traces, vel, back_own, carried, pair, image, a, b, w, bands
 ):
     a[...] = jnp.zeros_like(a)
     b[...] = jnp.zeros_like(b)
@@ -276,7 +282,7 @@
     inject(b, NT - 1, place, receivers, near, counts, traces)
     add_image(image, b, back_own, checkpoints[NT - 1])
     later, now = adjoint_steps(
-        range(14, 10, -1), a, b, w, deep, bands, vel, back_own, place, checkpoints, receivers, near, counts,
+        range(14, 10, -1), a, b, w, bands, vel, back_own, place, checkpoints, receivers, near, counts,
         traces, image,
     )
     for f, buf in enumerate((later, now)):
@@ -286,14 +292,14 @@
 
 def later_adjoint(
     steps, place, checkpoints, receivers, near, counts, traces, vel, back_own, mid, intra, inter,
-    held, far, pair, image, a, b, w, deep, bands,
+    held, far, pair, image, a, b, w, bands,
 ):
     assemble(a, 0, mid, intra, inter, place[2])
     assemble(b, 1, mid, intra, inter, place[2])
     image[...] = held[...]
     bands[...] = band()
     later, now = adjoint_steps(
-        steps, a, b, w, deep, bands, vel, back_own, place, checkpoints, receivers, near, counts, traces, image
+        steps, a, b, w, bands, vel, back_own, place, checkpoints, receivers, near, counts, traces, image
     )
     for f, buf in enumerate((later, now)):
         pair[f, :B] = own(buf)
@@ -345,7 +351,7 @@
         out_specs=out_specs,
         out_shape=outs,
         scratch_shapes=[pltpu.VMEM(FIELD, jnp.float32)] * fields
-        + [pltpu.VMEM((R, 2, R, 128), jnp.float32), pltpu.VMEM((512, 256), jnp.bfloat16)],
+        + [pltpu.VMEM((512, 256), jnp.bfloat16)],
         compiler_params=pltpu.CompilerParams(vmem_limit_bytes=48 * 1024 * 1024),
     )
 
@@ -357,13 +363,12 @@
     return mid, send(mid, SWAP), send(mid, ACROSS)
 
 
-def exchange_carrying(block, more, beside):
+def exchange_carrying(block, jump):
     low = send(block, UP)
     high = send(block, DOWN)
-    known = merge(block[:, B:], low[:, B:], high[:, B:], more[:, None])
+    known = merge(block[:, B:], low[:, B:], high[:, B:])
     mid = jnp.concatenate([low[:, :B], block[:, :B], high[:, :B], known], axis=1)
-    mid, beside = lax.optimization_barrier((mid, beside))
-    return (mid, send(mid, SWAP), send(mid, ACROSS)), beside
+    return (mid, send(mid, SWAP), send(mid, ACROSS)), send(mid[:, R], jump)
 
 
 def pick(two, index):
@@ -389,18 +394,18 @@
     return ordered(got, other, odd, 1).reshape(count, 8, 2, 8, 128)
 
 
-def outward_far(block, odd):
-    first, second = block[:4], block[4:]
+def outward_far(blocks, odd):
+    first, second = blocks[:, :4], blocks[:, 4:]
     got = send(pick((first, second), odd), back(spread(0)))
     return got, send(pick((second, first), odd), back(spread(1)))
 
 
 def outward_near(got, other, core, odd):
-    whole = ordered(got, other, odd, 1)
-    front, rear = whole[:, :, 0], whole[:, :, 1]
+    whole = ordered(got, other, odd, 2)
+    front, rear = whole[:, :, :, 0], whole[:, :, :, 1]
     kept = pick((front, rear), core)
     came = send(pick((rear, front), core), SWAP)
-    return ordered(kept, came, core, 2).reshape(4, 32, 128)
+    return ordered(kept, came, core, 3).reshape(-1, 4, 32, 128)
 
 
 def on_device(velocity_term, model_step, background, receivers, checkpoints):
@@ -416,12 +421,14 @@
         out_specs=[SM, SM, SM],
         out_shape=[i32(256), i32(256), i32(2)],
     )(place, receivers)
+    receivers_of = (mine, near, counts)
     stacked = jnp.concatenate(
-        [velocity_term[None] * (1.0 / 12.0), model_step[None], background.astype(jnp.float32)], axis=0
+        [velocity_term[None], model_step[None], background.astype(jnp.float32)], axis=0
     )
     inner = inward(stacked, core, odd)
     back_own = inner[2:]
     fields = jnp.concatenate([inner[:1], inner[1:2] * back_own], axis=0)
+    fields, (mine, near, counts) = lax.optimization_barrier((fields, receivers_of))
     vel, src, pair, traces = call(
         first_forward,
         [SM] * 5 + [VM] * 3,
@@ -441,31 +448,21 @@
     local = merge(traces, send(traces, UP), send(traces, DOWN))
     local = merge(local, send(local, ACROSS), send(local, SWAP))
     carried = local.reshape(2, 8, 2, 128).transpose(0, 2, 1, 3)
-    swapped = send(carried, SWAP)
     scalars = (place, checkpoints, receivers, near, counts, local)
     outs = [f32(2, B + 1, 2, B, 128), f32(B, 2, B, 128)]
     pair, image = call(first_adjoint, [SM] * 6 + [VM] * 3, outs, [VM] * 2, 3)(
         *scalars, vel, back_own, carried
     )
-    beside = ()
-    for number, steps in enumerate((range(10, 6, -1), range(6, 2, -1), range(2, -1, -1))):
-        parts, beside = exchange_carrying(pair, swapped, beside)
-        if number == 0:
-            far = send(parts[0][:, R], shifted(dz=8))
-            beside = (field,)
-        elif number == 1:
-            far = carried
-            beside = outward_far(beside[0], odd)
-        else:
-            wavefield = outward_near(*beside, core, odd)
+    jumps = (around(3), around(-3), shifted(dz=8))
+    for steps, jump in zip((range(10, 6, -1), range(6, 2, -1), range(2, -1, -1)), jumps):
+        parts, more = exchange_carrying(pair, jump)
         pair, image = call(
             functools.partial(later_adjoint, steps), [SM] * 6 + [VM] * 7, outs, [VM] * 2, 3
-        )(*scalars, vel, back_own, *parts, image, far)
-    carried = pair[:, B]
-    carried = merge(carried, send(carried, shifted(dy=1)))
+        )(*scalars, vel, back_own, *parts, image, more if steps.stop > -1 else carried)
+    image, wavefield = outward_near(*outward_far(jnp.stack([image, field]), odd), core, odd)
+    carried = merge(pair[:, B], more)
     carried = merge(carried, send(carried, shifted(dy=2)))
     traces = carried.transpose(0, 2, 1, 3).reshape(NT, 256)
-    image = outward_near(*outward_far(image, odd), core, odd)
     column_image = lax.psum(jnp.sum(image, axis=2), "c") / 256.0
     return (image, traces, column_image, wavefield)
 

time: 340 us -> 315 us (0.926)
  the two profiles are of different devices: /device:TPU:79 before, /device:TPU:137 now
where the time goes in v3:
time: 315 us; the launch traced here: 313 us
  starting transfers between devices  201 us (64%)
  waiting for transfers between devices  76.5 us (24%)
  Pallas kernels  26.3 us (8%)
  other arithmetic  4.07 us (1%)
    ppermute x42, starting transfers between devices, send(): return lax.ppermute(value, AXES, pairs)  201 us
    ppermute x42, waiting for transfers between devices, send(): return lax.ppermute(value, AXES, pairs)  76.5 us
    pallas_call x3, Pallas kernels, on_device(): call(functools.partial(later_adjoint, steps), [SM] * 6 + [VM] * 7, outs,...  8.23 us
    pallas_call x1, Pallas kernels, on_device(): pl.pallas_call(list_receivers, in_specs=[SM, SM], out_specs=[SM, SM, SM],...  6.44 us
  transfers between devices with their start and end apart: 42, of which 29 were waited for; matrix products, arithmetic and copies ran while one was open for 0% of the time, Pallas kernels for 3%

profile of v3, /device:TPU:137, one launch (start us, length us, event | category | flops | bytes accessed | tf_op | source)
XLA Modules:
  0.0 313.3 jit_solution(16053505955724324610)
XLA Ops:
  2.5 2.6 collective-permute-start
  6.3 8.8 %collective-permute-start.1 = (f32[6,4,2,8,128]{4,3,2,1,0:T(8,128)S(1)}, f32[6,4,2,8,128]{4,3,2,1,0:T(8,128)S(1)}, u32[]{:S(2)}, u32[]{:S(2)}) collective-permute-start(f32[6,4,2,8,128]{4,3,2,1,0:T(8,128)S(1)} %get-tuple-element.56), channel_id=1, source_target_pairs={{0,0},{1,1},{2,32},{3,33},{4,4},{5,5},{6,36},{7,37},{8,8},{9,9},{1... | collective-permute-start | bytes 589832 | tf_op jit(solution)/shard_map/ppermute | solution.py:65
  15.1 2.8 collective-permute-start.2
  18.5 6.4 %shard_map.84 = (s32[256]{0:T(256)}, s32[256]{0:T(256)}, s32[2]{0:T(128)}) custom-call(s32[4]{0:T(128)} %pad_add_fusion.place, s32[3,256]{1,0:T(4,128)} %receivers.17), custom_call_target="tpu_custom_call" | custom-call | tf_op jit(solution)/shard_map/pallas_call | solution.py:418
  25.0 6.6 %collective-permute-done.2 = f32[6,4,2,8,128]{4,3,2,1,0:T(8,128)S(1)} collective-permute-done((f32[6,4,2,8,128]{4,3,2,1,0:T(8,128)S(1)}, f32[6,4,2,8,128]{4,3,2,1,0:T(8,128)S(1)}, u32[]{:S(2)}, u32[]{:S(2)}) %collective-permute-start.2) | collective-permute-done | bytes 196640 | tf_op jit(solution)/shard_map/ppermute | solution.py:65
  31.8 12.2 %collective-permute-start.3 = (f32[5,8,2,8,128]{4,3,2,1,0:T(8,128)S(1)}, f32[5,8,2,8,128]{4,3,2,1,0:T(8,128)S(1)}, u32[]{:S(2)}, u32[]{:S(2)}) collective-permute-start(f32[5,8,2,8,128]{4,3,2,1,0:T(8,128)S(1)} %pad_maximum_fusion.4), channel_id=1, source_target_pairs={{0,64},{1,65},{2,66},{3,67},{4,68},{5,69},{6,70},{7,71},{8,72},{9,... | collective-permute-start | bytes 983048 | tf_op jit(solution)/shard_map/ppermute | solution.py:65
  44.0 1.9 collective-permute-start.4
  45.9 4.7 %collective-permute-done.3 = f32[5,8,2,8,128]{4,3,2,1,0:T(8,128)S(1)} collective-permute-done((f32[5,8,2,8,128]{4,3,2,1,0:T(8,128)S(1)}, f32[5,8,2,8,128]{4,3,2,1,0:T(8,128)S(1)}, u32[]{:S(2)}, u32[]{:S(2)}) %collective-permute-start.3) | collective-permute-done | bytes 327712 | tf_op jit(solution)/shard_map/ppermute | solution.py:65
  50.7 7.2 %collective-permute-done.4 = f32[5,8,2,8,128]{4,3,2,1,0:T(8,128)S(1)} collective-permute-done((f32[5,8,2,8,128]{4,3,2,1,0:T(8,128)S(1)}, f32[5,8,2,8,128]{4,3,2,1,0:T(8,128)S(1)}, u32[]{:S(2)}, u32[]{:S(2)}) %collective-permute-start.4) | collective-permute-done | bytes 327712 | tf_op jit(solution)/shard_map/ppermute | solution.py:65
  57.9 3.6 %collective-permute-start.6 = (f32[5,24,2,8,128]{4,3,2,1,0:T(8,128)S(1)}, f32[5,24,2,8,128]{4,3,2,1,0:T(8,128)S(1)}, u32[]{:S(2)}, u32[]{:S(2)}) collective-permute-start(f32[5,24,2,8,128]{4,3,2,1,0:T(8,128)S(1)} %constant_dynamic-update-slice_fusion.mid), channel_id=1, source_target_pairs={{0,61},{1,16},{2,63},{3,18},{4,49},{5,20},{6,51},{7,22},{8,53},{9,... | collective-permute-start | bytes 2949128 | tf_op jit(solution)/shard_map/ppermute | solution.py:65
  61.5 9.2 %collective-permute-start.5 = (f32[5,24,2,8,128]{4,3,2,1,0:T(8,128)S(1)}, f32[5,24,2,8,128]{4,3,2,1,0:T(8,128)S(1)}, u32[]{:S(2)}, u32[]{:S(2)}) collective-permute-start(f32[5,24,2,8,128]{4,3,2,1,0:T(8,128)S(1)} %constant_dynamic-update-slice_fusion.mid), channel_id=1, source_target_pairs={{0,1},{1,0},{2,3},{3,2},{4,5},{5,4},{6,7},{7,6},{8,9},{9,8},{10,11... | collective-permute-start | bytes 2949128 | tf_op jit(solution)/shard_map/ppermute | solution.py:65
  70.7 2.9 collective-permute-done.6.inter
  73.6 2.5 shard_map.85
  76.1 10.2 %collective-permute-start.7 = (f32[2,8,2,8,128]{4,3,2,1,0:T(8,128)S(1)}, f32[2,8,2,8,128]{4,3,2,1,0:T(8,128)S(1)}, u32[]{:S(2)}, u32[]{:S(2)}) collective-permute-start(f32[2,8,2,8,128]{4,3,2,1,0:T(8,128)S(1)} %get-tuple-element.38), channel_id=1, source_target_pairs={{0,64},{1,65},{2,66},{3,67},{4,68},{5,69},{6,70},{7,71},{8,72},{9,... | collective-permute-start | bytes 393224 | tf_op jit(solution)/shard_map/ppermute | solution.py:65
  86.3 1.9 collective-permute-start.8
  88.3 3.7 %collective-permute-done.8 = f32[2,8,2,8,128]{4,3,2,1,0:T(8,128)S(1)} collective-permute-done((f32[2,8,2,8,128]{4,3,2,1,0:T(8,128)S(1)}, f32[2,8,2,8,128]{4,3,2,1,0:T(8,128)S(1)}, u32[]{:S(2)}, u32[]{:S(2)}) %collective-permute-start.8) | collective-permute-done | bytes 131104 | tf_op jit(solution)/shard_map/ppermute | solution.py:65
  92.0 4.1 %collective-permute-start.10 = (f32[2,24,2,8,128]{4,3,2,1,0:T(8,128)S(1)}, f32[2,24,2,8,128]{4,3,2,1,0:T(8,128)S(1)}, u32[]{:S(2)}, u32[]{:S(2)}) collective-permute-start(f32[2,24,2,8,128]{4,3,2,1,0:T(8,128)S(1)} %constant_dynamic-update-slice_fusion.3.mid), channel_id=1, source_target_pairs={{0,61},{1,16},{2,63},{3,18},{4,49},{5,20},{6,51},{7,22},{8,53},{9,... | collective-permute-start | bytes 1179656 | tf_op jit(solution)/shard_map/ppermute | solution.py:65
  96.1 4.8 %collective-permute-start.9 = (f32[2,24,2,8,128]{4,3,2,1,0:T(8,128)S(1)}, f32[2,24,2,8,128]{4,3,2,1,0:T(8,128)S(1)}, u32[]{:S(2)}, u32[]{:S(2)}) collective-permute-start(f32[2,24,2,8,128]{4,3,2,1,0:T(8,128)S(1)} %constant_dynamic-update-slice_fusion.3.mid), channel_id=1, source_target_pairs={{0,1},{1,0},{2,3},{3,2},{4,5},{5,4},{6,7},{7,6},{8,9},{9,8},{10,11... | collective-permute-start | bytes 1179656 | tf_op jit(solution)/shard_map/ppermute | solution.py:65
  102.2 2.2 shard_map.86
  104.4 4.8 %collective-permute-start.11 = (f32[2,8,2,8,128]{4,3,2,1,0:T(8,128)S(1)}, f32[2,8,2,8,128]{4,3,2,1,0:T(8,128)S(1)}, u32[]{:S(2)}, u32[]{:S(2)}) collective-permute-start(f32[2,8,2,8,128]{4,3,2,1,0:T(8,128)S(1)} %get-tuple-element.40), channel_id=1, source_target_pairs={{0,64},{1,65},{2,66},{3,67},{4,68},{5,69},{6,70},{7,71},{8,72},{9,... | collective-permute-start | bytes 393224 | tf_op jit(solution)/shard_map/ppermute | solution.py:65
  109.3 2.3 collective-permute-start.12
  112.1 3.2 %collective-permute-done.12 = f32[2,8,2,8,128]{4,3,2,1,0:T(8,128)S(1)} collective-permute-done((f32[2,8,2,8,128]{4,3,2,1,0:T(8,128)S(1)}, f32[2,8,2,8,128]{4,3,2,1,0:T(8,128)S(1)}, u32[]{:S(2)}, u32[]{:S(2)}) %collective-permute-start.12) | collective-permute-done | bytes 131104 | tf_op jit(solution)/shard_map/ppermute | solution.py:65
  115.3 3.9 %collective-permute-start.14 = (f32[2,24,2,8,128]{4,3,2,1,0:T(8,128)S(1)}, f32[2,24,2,8,128]{4,3,2,1,0:T(8,128)S(1)}, u32[]{:S(2)}, u32[]{:S(2)}) collective-permute-start(f32[2,24,2,8,128]{4,3,2,1,0:T(8,128)S(1)} %constant_dynamic-update-slice_fusion.6.mid), channel_id=1, source_target_pairs={{0,61},{1,16},{2,63},{3,18},{4,49},{5,20},{6,51},{7,22},{8,53},{9,... | collective-permute-start | bytes 1179656 | tf_op jit(solution)/shard_map/ppermute | solution.py:65
  119.3 4.2 %collective-permute-start.13 = (f32[2,24,2,8,128]{4,3,2,1,0:T(8,128)S(1)}, f32[2,24,2,8,128]{4,3,2,1,0:T(8,128)S(1)}, u32[]{:S(2)}, u32[]{:S(2)}) collective-permute-start(f32[2,24,2,8,128]{4,3,2,1,0:T(8,128)S(1)} %constant_dynamic-update-slice_fusion.6.mid), channel_id=1, source_target_pairs={{0,1},{1,0},{2,3},{3,2},{4,5},{5,4},{6,7},{7,6},{8,9},{9,8},{10,11... | collective-permute-start | bytes 1179656 | tf_op jit(solution)/shard_map/ppermute | solution.py:65
  124.8 2.2 shard_map.87
  127.0 3.8 %collective-permute-start.15 = (f32[2,8,2,8,128]{4,3,2,1,0:T(8,128)S(1)}, f32[2,8,2,8,128]{4,3,2,1,0:T(8,128)S(1)}, u32[]{:S(2)}, u32[]{:S(2)}) collective-permute-start(f32[2,8,2,8,128]{4,3,2,1,0:T(8,128)S(1)} %get-tuple-element.42), channel_id=1, source_target_pairs={{0,64},{1,65},{2,66},{3,67},{4,68},{5,69},{6,70},{7,71},{8,72},{9,... | collective-permute-start | bytes 393224 | tf_op jit(solution)/shard_map/ppermute | solution.py:65
  130.8 3.7 %collective-permute-start.16 = (f32[2,8,2,8,128]{4,3,2,1,0:T(8,128)S(1)}, f32[2,8,2,8,128]{4,3,2,1,0:T(8,128)S(1)}, u32[]{:S(2)}, u32[]{:S(2)}) collective-permute-start(f32[2,8,2,8,128]{4,3,2,1,0:T(8,128)S(1)} %get-tuple-element.42), channel_id=1, source_target_pairs={{0,450},{1,451},{2,448},{3,449},{4,454},{5,455},{6,452},{7,453},{8... | collective-permute-start | bytes 393224 | tf_op jit(solution)/shard_map/ppermute | solution.py:65
  136.6 4.8 %collective-permute-start.18 = (f32[2,24,2,8,128]{4,3,2,1,0:T(8,128)S(1)}, f32[2,24,2,8,128]{4,3,2,1,0:T(8,128)S(1)}, u32[]{:S(2)}, u32[]{:S(2)}) collective-permute-start(f32[2,24,2,8,128]{4,3,2,1,0:T(8,128)S(1)} %constant_dynamic-update-slice_fusion.9.mid), channel_id=1, source_target_pairs={{0,61},{1,16},{2,63},{3,18},{4,49},{5,20},{6,51},{7,22},{8,53},{9,... | collective-permute-start | bytes 1179656 | tf_op jit(solution)/shard_map/ppermute | solution.py:65
  141.3 4.8 %collective-permute-start.17 = (f32[2,24,2,8,128]{4,3,2,1,0:T(8,128)S(1)}, f32[2,24,2,8,128]{4,3,2,1,0:T(8,128)S(1)}, u32[]{:S(2)}, u32[]{:S(2)}) collective-permute-start(f32[2,24,2,8,128]{4,3,2,1,0:T(8,128)S(1)} %constant_dynamic-update-slice_fusion.9.mid), channel_id=1, source_target_pairs={{0,1},{1,0},{2,3},{3,2},{4,5},{5,4},{6,7},{7,6},{8,9},{9,8},{10,11... | collective-permute-start | bytes 1179656 | tf_op jit(solution)/shard_map/ppermute | solution.py:65
  147.5 1.7 shard_map.88
  149.2 9.6 %collective-permute-start.19 = (f32[16,256]{1,0:T(8,128)S(1)}, f32[16,256]{1,0:T(8,128)S(1)}, u32[]{:S(2)}, u32[]{:S(2)}) collective-permute-start(f32[16,256]{1,0:T(8,128)S(1)} %get-tuple-element.44), channel_id=1, source_target_pairs={{0,64},{1,65},{2,66},{3,67},{4,68},{5,69},{6,70},{7,71},{8,72},{9,... | collective-permute-start | bytes 49160 | tf_op jit(solution)/shard_map/ppermute | solution.py:65
  158.7 1.9 collective-permute-start.20
  160.7 3.1 collective-permute-done.20
  163.8 1.9 collective-permute-start.21
  165.7 9.1 %collective-permute-start.22 = (f32[16,256]{1,0:T(8,128)S(1)}, f32[16,256]{1,0:T(8,128)S(1)}, u32[]{:S(2)}, u32[]{:S(2)}) collective-permute-start(f32[16,256]{1,0:T(8,128)S(1)} %compare_select_fusion.10), channel_id=1, source_target_pairs={{0,1},{1,0},{2,3},{3,2},{4,5},{5,4},{6,7},{7,6},{8,9},{9,8},{10,11... | collective-permute-start | bytes 49160 | tf_op jit(solution)/shard_map/ppermute | solution.py:65
  175.6 3.0 shard_map.89
  178.7 1.9 collective-permute-start.24
  180.6 4.8 %collective-permute-start.23 = (f32[2,9,2,8,128]{4,3,2,1,0:T(8,128)S(1)}, f32[2,9,2,8,128]{4,3,2,1,0:T(8,128)S(1)}, u32[]{:S(2)}, u32[]{:S(2)}) collective-permute-start(f32[2,9,2,8,128]{4,3,2,1,0:T(8,128)S(1)} %get-tuple-element.45), channel_id=1, source_target_pairs={{0,64},{1,65},{2,66},{3,67},{4,68},{5,69},{6,70},{7,71},{8,72},{9,... | collective-permute-start | bytes 442376 | tf_op jit(solution)/shard_map/ppermute | solution.py:65
  186.0 1.7 collective-permute-done.23
  187.8 1.9 collective-permute-start.26
  189.7 6.7 %collective-permute-start.25 = (f32[2,25,2,8,128]{4,3,2,1,0:T(8,128)S(1)}, f32[2,25,2,8,128]{4,3,2,1,0:T(8,128)S(1)}, u32[]{:S(2)}, u32[]{:S(2)}) collective-permute-start(f32[2,25,2,8,128]{4,3,2,1,0:T(8,128)S(1)} %pad_maximum_fusion.mid), channel_id=1, source_target_pairs={{0,1},{1,0},{2,3},{3,2},{4,5},{5,4},{6,7},{7,6},{8,9},{9,8},{10,11... | collective-permute-start | bytes 1228808 | tf_op jit(solution)/shard_map/ppermute | solution.py:65
  196.4 4.9 %collective-permute-start.27 = (f32[2,2,8,128]{3,2,1,0:T(8,128)S(1)}, f32[2,2,8,128]{3,2,1,0:T(8,128)S(1)}, u32[]{:S(2)}, u32[]{:S(2)}) collective-permute-start(f32[2,2,8,128]{3,2,1,0:T(8,128)S(1)} %bitcast.74), channel_id=1, source_target_pairs={{0,48},{1,49},{2,50},{3,51},{4,52},{5,53},{6,54},{7,55},{8,56},{9,... | collective-permute-start | bytes 49160 | tf_op jit(solution)/shard_map/ppermute | solution.py:65
  202.2 3.1 shard_map.90
  205.3 1.9 collective-permute-start.29
  207.2 3.7 %collective-permute-start.28 = (f32[2,9,2,8,128]{4,3,2,1,0:T(8,128)S(1)}, f32[2,9,2,8,128]{4,3,2,1,0:T(8,128)S(1)}, u32[]{:S(2)}, u32[]{:S(2)}) collective-permute-start(f32[2,9,2,8,128]{4,3,2,1,0:T(8,128)S(1)} %get-tuple-element.47), channel_id=1, source_target_pairs={{0,64},{1,65},{2,66},{3,67},{4,68},{5,69},{6,70},{7,71},{8,72},{9,... | collective-permute-start | bytes 442376 | tf_op jit(solution)/shard_map/ppermute | solution.py:65
  211.8 2.5 collective-permute-done.28
  214.4 4.3 %collective-permute-start.31 = (f32[2,25,2,8,128]{4,3,2,1,0:T(8,128)S(1)}, f32[2,25,2,8,128]{4,3,2,1,0:T(8,128)S(1)}, u32[]{:S(2)}, u32[]{:S(2)}) collective-permute-start(f32[2,25,2,8,128]{4,3,2,1,0:T(8,128)S(1)} %pad_maximum_fusion.1.mid), channel_id=1, source_target_pairs={{0,61},{1,16},{2,63},{3,18},{4,49},{5,20},{6,51},{7,22},{8,53},{9,... | collective-permute-start | bytes 1228808 | tf_op jit(solution)/shard_map/ppermute | solution.py:65
  218.7 5.5 %collective-permute-start.30 = (f32[2,25,2,8,128]{4,3,2,1,0:T(8,128)S(1)}, f32[2,25,2,8,128]{4,3,2,1,0:T(8,128)S(1)}, u32[]{:S(2)}, u32[]{:S(2)}) collective-permute-start(f32[2,25,2,8,128]{4,3,2,1,0:T(8,128)S(1)} %pad_maximum_fusion.1.mid), channel_id=1, source_target_pairs={{0,1},{1,0},{2,3},{3,2},{4,5},{5,4},{6,7},{7,6},{8,9},{9,8},{10,11... | collective-permute-start | bytes 1228808 | tf_op jit(solution)/shard_map/ppermute | solution.py:65
  224.2 6.0 %collective-permute-start.32 = (f32[2,2,8,128]{3,2,1,0:T(8,128)S(1)}, f32[2,2,8,128]{3,2,1,0:T(8,128)S(1)}, u32[]{:S(2)}, u32[]{:S(2)}) collective-permute-start(f32[2,2,8,128]{3,2,1,0:T(8,128)S(1)} %bitcast.75), channel_id=1, source_target_pairs={{0,28},{1,29},{2,30},{3,31},{4,16},{5,17},{6,18},{7,19},{8,20},{9,... | collective-permute-start | bytes 49160 | tf_op jit(solution)/shard_map/ppermute | solution.py:65
  231.1 2.9 shard_map.91
  234.0 1.9 collective-permute-start.34
  235.9 3.4 %collective-permute-start.33 = (f32[2,9,2,8,128]{4,3,2,1,0:T(8,128)S(1)}, f32[2,9,2,8,128]{4,3,2,1,0:T(8,128)S(1)}, u32[]{:S(2)}, u32[]{:S(2)}) collective-permute-start(f32[2,9,2,8,128]{4,3,2,1,0:T(8,128)S(1)} %get-tuple-element.49), channel_id=1, source_target_pairs={{0,64},{1,65},{2,66},{3,67},{4,68},{5,69},{6,70},{7,71},{8,72},{9,... | collective-permute-start | bytes 442376 | tf_op jit(solution)/shard_map/ppermute | solution.py:65
  239.9 3.1 collective-permute-done.33
  243.1 4.1 %collective-permute-start.36 = (f32[2,25,2,8,128]{4,3,2,1,0:T(8,128)S(1)}, f32[2,25,2,8,128]{4,3,2,1,0:T(8,128)S(1)}, u32[]{:S(2)}, u32[]{:S(2)}) collective-permute-start(f32[2,25,2,8,128]{4,3,2,1,0:T(8,128)S(1)} %pad_maximum_fusion.2.mid), channel_id=1, source_target_pairs={{0,61},{1,16},{2,63},{3,18},{4,49},{5,20},{6,51},{7,22},{8,53},{9,... | collective-permute-start | bytes 1228808 | tf_op jit(solution)/shard_map/ppermute | solution.py:65
  247.2 2.5 collective-permute-start.35
  249.7 12.5 %collective-permute-start.40 = (f32[2,2,8,128]{3,2,1,0:T(8,128)S(1)}, f32[2,2,8,128]{3,2,1,0:T(8,128)S(1)}, u32[]{:S(2)}, u32[]{:S(2)}) collective-permute-start(f32[2,2,8,128]{3,2,1,0:T(8,128)S(1)} %bitcast.73), channel_id=1, source_target_pairs={{0,2},{1,3},{2,0},{3,1},{4,6},{5,7},{6,4},{7,5},{8,10},{9,11},{10,... | collective-permute-start | bytes 49160 | tf_op jit(solution)/shard_map/ppermute | solution.py:65
  262.3 2.3 shard_map.92
  264.6 5.5 %collective-permute-start.41 = (f32[2,2,8,128]{3,2,1,0:T(8,128)S(1)}, f32[2,2,8,128]{3,2,1,0:T(8,128)S(1)}, u32[]{:S(2)}, u32[]{:S(2)}) collective-permute-start(f32[2,2,8,128]{3,2,1,0:T(8,128)S(1)} %compare_select_fusion.1), channel_id=1, source_target_pairs={{0,8},{1,9},{2,10},{3,11},{4,12},{5,13},{6,14},{7,15},{8,0},{9,1},... | collective-permute-start | bytes 49160 | tf_op jit(solution)/shard_map/ppermute | solution.py:65
  270.1 4.1 %collective-permute-start.37 = (f32[2,4,2,8,128]{4,3,2,1,0:T(8,128)S(1)}, f32[2,4,2,8,128]{4,3,2,1,0:T(8,128)S(1)}, u32[]{:S(2)}, u32[]{:S(2)}) collective-permute-start(f32[2,4,2,8,128]{4,3,2,1,0:T(8,128)S(1)} %get-tuple-element.63), channel_id=1, source_target_pairs={{0,0},{1,1},{2,256},{3,257},{4,4},{5,5},{6,260},{7,261},{8,8},{9,9... | collective-permute-start | bytes 196616 | tf_op jit(solution)/shard_map/ppermute | solution.py:65
  274.2 5.4 %collective-permute-start.38 = (f32[2,4,2,8,128]{4,3,2,1,0:T(8,128)S(1)}, f32[2,4,2,8,128]{4,3,2,1,0:T(8,128)S(1)}, u32[]{:S(2)}, u32[]{:S(2)}) collective-permute-start(f32[2,4,2,8,128]{4,3,2,1,0:T(8,128)S(1)} %get-tuple-element.64), channel_id=1, source_target_pairs={{0,16},{1,17},{2,272},{3,273},{4,20},{5,21},{6,276},{7,277},{8,24}... | collective-permute-start | bytes 196616 | tf_op jit(solution)/shard_map/ppermute | solution.py:65
  280.2 1.7 collective-permute-done.37
  281.8 23.2 %collective-permute-done.38 = f32[2,4,2,8,128]{4,3,2,1,0:T(8,128)S(1)} collective-permute-done((f32[2,4,2,8,128]{4,3,2,1,0:T(8,128)S(1)}, f32[2,4,2,8,128]{4,3,2,1,0:T(8,128)S(1)}, u32[]{:S(2)}, u32[]{:S(2)}) %collective-permute-start.38) | collective-permute-done | bytes 65568 | tf_op jit(solution)/shard_map/ppermute | solution.py:65
  305.1 2.8 collective-permute-start.39
  309.6 2.5 psum.7
  (98 shorter events, 18.6 us)
Async XLA Ops:
  2.5 3.6 %collective-permute-start = (f32[6,4,2,8,128]{4,3,1,0,2:T(8,128)S(1)}, f32[6,4,2,8,128]{4,3,1,0,2:T(8,128)S(1)}, u32[]{:S(2)}, u32[]{:S(2)}) collective-permute-start(f32[6,4,2,8,128]{4,3,1,0,2:T(8,128)S(1)} %select_bitcast_fusion.2), channel_id=1, source_target_pairs={{0,1},{1,0},{2,3},{3,2},{4,5},{5,4},{6,7},{7,6},{8,9},{9,8},{10,11... | collective-permute-start | bytes 589832 | tf_op jit(solution)/shard_map/ppermute | solution.py:65
  6.3 18.7 %collective-permute-start.1 = (f32[6,4,2,8,128]{4,3,2,1,0:T(8,128)S(1)}, f32[6,4,2,8,128]{4,3,2,1,0:T(8,128)S(1)}, u32[]{:S(2)}, u32[]{:S(2)}) collective-permute-start(f32[6,4,2,8,128]{4,3,2,1,0:T(8,128)S(1)} %get-tuple-element.56), channel_id=1, source_target_pairs={{0,0},{1,1},{2,32},{3,33},{4,4},{5,5},{6,36},{7,37},{8,8},{9,9},{1... | collective-permute-start | bytes 589832 | tf_op jit(solution)/shard_map/ppermute | solution.py:65
  15.1 16.6 %collective-permute-start.2 = (f32[6,4,2,8,128]{4,3,2,1,0:T(8,128)S(1)}, f32[6,4,2,8,128]{4,3,2,1,0:T(8,128)S(1)}, u32[]{:S(2)}, u32[]{:S(2)}) collective-permute-start(f32[6,4,2,8,128]{4,3,2,1,0:T(8,128)S(1)} %get-tuple-element.57), channel_id=1, source_target_pairs={{0,16},{1,17},{2,48},{3,49},{4,20},{5,21},{6,52},{7,53},{8,24},{9,... | collective-permute-start | bytes 589832 | tf_op jit(solution)/shard_map/ppermute | solution.py:65
  31.6 41.9 %copy-start = (s32[3,256]{1,0:T(4,128)S(1)}, s32[3,256]{1,0:T(4,128)}, u32[]{:S(2)}) copy-start(s32[3,256]{1,0:T(4,128)} %receivers.17) | copy-start | bytes 9220
  31.6 41.9 %copy-start.1 = (s32[4]{0:T(128)S(1)}, s32[4]{0:T(128)}, u32[]{:S(2)}) copy-start(s32[4]{0:T(128)} %pad_add_fusion.place) | copy-start | bytes 52
  31.6 42.0 %copy-start.2 = (s32[16]{0:T(128)S(1)}, s32[16]{0:T(128)}, u32[]{:S(2)}) copy-start(s32[16]{0:T(128)} %checkpoints.15) | copy-start | bytes 196
  31.7 42.0 %copy-start.3 = (s32[2]{0:T(128)S(1)}, s32[2]{0:T(128)}, u32[]{:S(2)}) copy-start(s32[2]{0:T(128)} %get-tuple-element.33.counts) | copy-start | bytes 28
  31.7 42.0 %copy-start.5 = (s32[256]{0:T(256)S(1)}, s32[256]{0:T(256)}, u32[]{:S(2)}) copy-start(s32[256]{0:T(256)} %get-tuple-element.34.mine) | copy-start | bytes 3076
  31.8 18.8 %collective-permute-start.3 = (f32[5,8,2,8,128]{4,3,2,1,0:T(8,128)S(1)}, f32[5,8,2,8,128]{4,3,2,1,0:T(8,128)S(1)}, u32[]{:S(2)}, u32[]{:S(2)}) collective-permute-start(f32[5,8,2,8,128]{4,3,2,1,0:T(8,128)S(1)} %pad_maximum_fusion.4), channel_id=1, source_target_pairs={{0,64},{1,65},{2,66},{3,67},{4,68},{5,69},{6,70},{7,71},{8,72},{9,... | collective-permute-start | bytes 983048 | tf_op jit(solution)/shard_map/ppermute | solution.py:65
  44.0 13.8 %collective-permute-start.4 = (f32[5,8,2,8,128]{4,3,2,1,0:T(8,128)S(1)}, f32[5,8,2,8,128]{4,3,2,1,0:T(8,128)S(1)}, u32[]{:S(2)}, u32[]{:S(2)}) collective-permute-start(f32[5,8,2,8,128]{4,3,2,1,0:T(8,128)S(1)} %pad_maximum_fusion.4), channel_id=1, source_target_pairs={{0,450},{1,451},{2,448},{3,449},{4,454},{5,455},{6,452},{7,453},{8... | collective-permute-start | bytes 983048 | tf_op jit(solution)/shard_map/ppermute | solution.py:65
  57.9 15.7 %collective-permute-start.6 = (f32[5,24,2,8,128]{4,3,2,1,0:T(8,128)S(1)}, f32[5,24,2,8,128]{4,3,2,1,0:T(8,128)S(1)}, u32[]{:S(2)}, u32[]{:S(2)}) collective-permute-start(f32[5,24,2,8,128]{4,3,2,1,0:T(8,128)S(1)} %constant_dynamic-update-slice_fusion.mid), channel_id=1, source_target_pairs={{0,61},{1,16},{2,63},{3,18},{4,49},{5,20},{6,51},{7,22},{8,53},{9,... | collective-permute-start | bytes 2949128 | tf_op jit(solution)/shard_map/ppermute | solution.py:65
  61.5 12.1 %collective-permute-start.5 = (f32[5,24,2,8,128]{4,3,2,1,0:T(8,128)S(1)}, f32[5,24,2,8,128]{4,3,2,1,0:T(8,128)S(1)}, u32[]{:S(2)}, u32[]{:S(2)}) collective-permute-start(f32[5,24,2,8,128]{4,3,2,1,0:T(8,128)S(1)} %constant_dynamic-update-slice_fusion.mid), channel_id=1, source_target_pairs={{0,1},{1,0},{2,3},{3,2},{4,5},{5,4},{6,7},{7,6},{8,9},{9,8},{10,11... | collective-permute-start | bytes 2949128 | tf_op jit(solution)/shard_map/ppermute | solution.py:65
  76.1 12.1 %collective-permute-start.7 = (f32[2,8,2,8,128]{4,3,2,1,0:T(8,128)S(1)}, f32[2,8,2,8,128]{4,3,2,1,0:T(8,128)S(1)}, u32[]{:S(2)}, u32[]{:S(2)}) collective-permute-start(f32[2,8,2,8,128]{4,3,2,1,0:T(8,128)S(1)} %get-tuple-element.38), channel_id=1, source_target_pairs={{0,64},{1,65},{2,66},{3,67},{4,68},{5,69},{6,70},{7,71},{8,72},{9,... | collective-permute-start | bytes 393224 | tf_op jit(solution)/shard_map/ppermute | solution.py:65
  86.3 5.7 %collective-permute-start.8 = (f32[2,8,2,8,128]{4,3,2,1,0:T(8,128)S(1)}, f32[2,8,2,8,128]{4,3,2,1,0:T(8,128)S(1)}, u32[]{:S(2)}, u32[]{:S(2)}) collective-permute-start(f32[2,8,2,8,128]{4,3,2,1,0:T(8,128)S(1)} %get-tuple-element.38), channel_id=1, source_target_pairs={{0,450},{1,451},{2,448},{3,449},{4,454},{5,455},{6,452},{7,453},{8... | collective-permute-start | bytes 393224 | tf_op jit(solution)/shard_map/ppermute | solution.py:65
  92.0 9.8 %collective-permute-start.10 = (f32[2,24,2,8,128]{4,3,2,1,0:T(8,128)S(1)}, f32[2,24,2,8,128]{4,3,2,1,0:T(8,128)S(1)}, u32[]{:S(2)}, u32[]{:S(2)}) collective-permute-start(f32[2,24,2,8,128]{4,3,2,1,0:T(8,128)S(1)} %constant_dynamic-update-slice_fusion.3.mid), channel_id=1, source_target_pairs={{0,61},{1,16},{2,63},{3,18},{4,49},{5,20},{6,51},{7,22},{8,53},{9,... | collective-permute-start | bytes 1179656 | tf_op jit(solution)/shard_map/ppermute | solution.py:65
  96.1 6.1 %collective-permute-start.9 = (f32[2,24,2,8,128]{4,3,2,1,0:T(8,128)S(1)}, f32[2,24,2,8,128]{4,3,2,1,0:T(8,128)S(1)}, u32[]{:S(2)}, u32[]{:S(2)}) collective-permute-start(f32[2,24,2,8,128]{4,3,2,1,0:T(8,128)S(1)} %constant_dynamic-update-slice_fusion.3.mid), channel_id=1, source_target_pairs={{0,1},{1,0},{2,3},{3,2},{4,5},{5,4},{6,7},{7,6},{8,9},{9,8},{10,11... | collective-permute-start | bytes 1179656 | tf_op jit(solution)/shard_map/ppermute | solution.py:65
  104.4 7.6 %collective-permute-start.11 = (f32[2,8,2,8,128]{4,3,2,1,0:T(8,128)S(1)}, f32[2,8,2,8,128]{4,3,2,1,0:T(8,128)S(1)}, u32[]{:S(2)}, u32[]{:S(2)}) collective-permute-start(f32[2,8,2,8,128]{4,3,2,1,0:T(8,128)S(1)} %get-tuple-element.40), channel_id=1, source_target_pairs={{0,64},{1,65},{2,66},{3,67},{4,68},{5,69},{6,70},{7,71},{8,72},{9,... | collective-permute-start | bytes 393224 | tf_op jit(solution)/shard_map/ppermute | solution.py:65
  109.3 6.0 %collective-permute-start.12 = (f32[2,8,2,8,128]{4,3,2,1,0:T(8,128)S(1)}, f32[2,8,2,8,128]{4,3,2,1,0:T(8,128)S(1)}, u32[]{:S(2)}, u32[]{:S(2)}) collective-permute-start(f32[2,8,2,8,128]{4,3,2,1,0:T(8,128)S(1)} %get-tuple-element.40), channel_id=1, source_target_pairs={{0,450},{1,451},{2,448},{3,449},{4,454},{5,455},{6,452},{7,453},{8... | collective-permute-start | bytes 393224 | tf_op jit(solution)/shard_map/ppermute | solution.py:65
  115.3 9.4 %collective-permute-start.14 = (f32[2,24,2,8,128]{4,3,2,1,0:T(8,128)S(1)}, f32[2,24,2,8,128]{4,3,2,1,0:T(8,128)S(1)}, u32[]{:S(2)}, u32[]{:S(2)}) collective-permute-start(f32[2,24,2,8,128]{4,3,2,1,0:T(8,128)S(1)} %constant_dynamic-update-slice_fusion.6.mid), channel_id=1, source_target_pairs={{0,61},{1,16},{2,63},{3,18},{4,49},{5,20},{6,51},{7,22},{8,53},{9,... | collective-permute-start | bytes 1179656 | tf_op jit(solution)/shard_map/ppermute | solution.py:65
  119.3 5.6 %collective-permute-start.13 = (f32[2,24,2,8,128]{4,3,2,1,0:T(8,128)S(1)}, f32[2,24,2,8,128]{4,3,2,1,0:T(8,128)S(1)}, u32[]{:S(2)}, u32[]{:S(2)}) collective-permute-start(f32[2,24,2,8,128]{4,3,2,1,0:T(8,128)S(1)} %constant_dynamic-update-slice_fusion.6.mid), channel_id=1, source_target_pairs={{0,1},{1,0},{2,3},{3,2},{4,5},{5,4},{6,7},{7,6},{8,9},{9,8},{10,11... | collective-permute-start | bytes 1179656 | tf_op jit(solution)/shard_map/ppermute | solution.py:65
  127.0 7.9 %collective-permute-start.15 = (f32[2,8,2,8,128]{4,3,2,1,0:T(8,128)S(1)}, f32[2,8,2,8,128]{4,3,2,1,0:T(8,128)S(1)}, u32[]{:S(2)}, u32[]{:S(2)}) collective-permute-start(f32[2,8,2,8,128]{4,3,2,1,0:T(8,128)S(1)} %get-tuple-element.42), channel_id=1, source_target_pairs={{0,64},{1,65},{2,66},{3,67},{4,68},{5,69},{6,70},{7,71},{8,72},{9,... | collective-permute-start | bytes 393224 | tf_op jit(solution)/shard_map/ppermute | solution.py:65
  130.8 5.7 %collective-permute-start.16 = (f32[2,8,2,8,128]{4,3,2,1,0:T(8,128)S(1)}, f32[2,8,2,8,128]{4,3,2,1,0:T(8,128)S(1)}, u32[]{:S(2)}, u32[]{:S(2)}) collective-permute-start(f32[2,8,2,8,128]{4,3,2,1,0:T(8,128)S(1)} %get-tuple-element.42), channel_id=1, source_target_pairs={{0,450},{1,451},{2,448},{3,449},{4,454},{5,455},{6,452},{7,453},{8... | collective-permute-start | bytes 393224 | tf_op jit(solution)/shard_map/ppermute | solution.py:65
  135.0 40.7 %copy-start.4 = (s32[256]{0:T(256)S(1)}, s32[256]{0:T(256)}, u32[]{:S(2)}) copy-start(s32[256]{0:T(256)} %get-tuple-element.32.near) | copy-start | bytes 3076
  136.6 10.2 %collective-permute-start.18 = (f32[2,24,2,8,128]{4,3,2,1,0:T(8,128)S(1)}, f32[2,24,2,8,128]{4,3,2,1,0:T(8,128)S(1)}, u32[]{:S(2)}, u32[]{:S(2)}) collective-permute-start(f32[2,24,2,8,128]{4,3,2,1,0:T(8,128)S(1)} %constant_dynamic-update-slice_fusion.9.mid), channel_id=1, source_target_pairs={{0,61},{1,16},{2,63},{3,18},{4,49},{5,20},{6,51},{7,22},{8,53},{9,... | collective-permute-start | bytes 1179656 | tf_op jit(solution)/shard_map/ppermute | solution.py:65
  141.3 6.2 %collective-permute-start.17 = (f32[2,24,2,8,128]{4,3,2,1,0:T(8,128)S(1)}, f32[2,24,2,8,128]{4,3,2,1,0:T(8,128)S(1)}, u32[]{:S(2)}, u32[]{:S(2)}) collective-permute-start(f32[2,24,2,8,128]{4,3,2,1,0:T(8,128)S(1)} %constant_dynamic-update-slice_fusion.9.mid), channel_id=1, source_target_pairs={{0,1},{1,0},{2,3},{3,2},{4,5},{5,4},{6,7},{7,6},{8,9},{9,8},{10,11... | collective-permute-start | bytes 1179656 | tf_op jit(solution)/shard_map/ppermute | solution.py:65
  149.2 11.5 %collective-permute-start.19 = (f32[16,256]{1,0:T(8,128)S(1)}, f32[16,256]{1,0:T(8,128)S(1)}, u32[]{:S(2)}, u32[]{:S(2)}) collective-permute-start(f32[16,256]{1,0:T(8,128)S(1)} %get-tuple-element.44), channel_id=1, source_target_pairs={{0,64},{1,65},{2,66},{3,67},{4,68},{5,69},{6,70},{7,71},{8,72},{9,... | collective-permute-start | bytes 49160 | tf_op jit(solution)/shard_map/ppermute | solution.py:65
  158.7 5.0 %collective-permute-start.20 = (f32[16,256]{1,0:T(8,128)S(1)}, f32[16,256]{1,0:T(8,128)S(1)}, u32[]{:S(2)}, u32[]{:S(2)}) collective-permute-start(f32[16,256]{1,0:T(8,128)S(1)} %get-tuple-element.44), channel_id=1, source_target_pairs={{0,450},{1,451},{2,448},{3,449},{4,454},{5,455},{6,452},{7,453},{8... | collective-permute-start | bytes 49160 | tf_op jit(solution)/shard_map/ppermute | solution.py:65
  163.8 11.0 %collective-permute-start.21 = (f32[16,256]{1,0:T(8,128)S(1)}, f32[16,256]{1,0:T(8,128)S(1)}, u32[]{:S(2)}, u32[]{:S(2)}) collective-permute-start(f32[16,256]{1,0:T(8,128)S(1)} %compare_select_fusion.10), channel_id=1, source_target_pairs={{0,61},{1,16},{2,63},{3,18},{4,49},{5,20},{6,51},{7,22},{8,53},{9,... | collective-permute-start | bytes 49160 | tf_op jit(solution)/shard_map/ppermute | solution.py:65
  165.7 9.9 %collective-permute-start.22 = (f32[16,256]{1,0:T(8,128)S(1)}, f32[16,256]{1,0:T(8,128)S(1)}, u32[]{:S(2)}, u32[]{:S(2)}) collective-permute-start(f32[16,256]{1,0:T(8,128)S(1)} %compare_select_fusion.10), channel_id=1, source_target_pairs={{0,1},{1,0},{2,3},{3,2},{4,5},{5,4},{6,7},{7,6},{8,9},{9,8},{10,11... | collective-permute-start | bytes 49160 | tf_op jit(solution)/shard_map/ppermute | solution.py:65
  178.7 7.3 %collective-permute-start.24 = (f32[2,9,2,8,128]{4,3,2,1,0:T(8,128)S(1)}, f32[2,9,2,8,128]{4,3,2,1,0:T(8,128)S(1)}, u32[]{:S(2)}, u32[]{:S(2)}) collective-permute-start(f32[2,9,2,8,128]{4,3,2,1,0:T(8,128)S(1)} %get-tuple-element.45), channel_id=1, source_target_pairs={{0,450},{1,451},{2,448},{3,449},{4,454},{5,455},{6,452},{7,453},{8... | collective-permute-start | bytes 442376 | tf_op jit(solution)/shard_map/ppermute | solution.py:65
  180.6 7.1 %collective-permute-start.23 = (f32[2,9,2,8,128]{4,3,2,1,0:T(8,128)S(1)}, f32[2,9,2,8,128]{4,3,2,1,0:T(8,128)S(1)}, u32[]{:S(2)}, u32[]{:S(2)}) collective-permute-start(f32[2,9,2,8,128]{4,3,2,1,0:T(8,128)S(1)} %get-tuple-element.45), channel_id=1, source_target_pairs={{0,64},{1,65},{2,66},{3,67},{4,68},{5,69},{6,70},{7,71},{8,72},{9,... | collective-permute-start | bytes 442376 | tf_op jit(solution)/shard_map/ppermute | solution.py:65
  187.8 14.4 %collective-permute-start.26 = (f32[2,25,2,8,128]{4,3,2,1,0:T(8,128)S(1)}, f32[2,25,2,8,128]{4,3,2,1,0:T(8,128)S(1)}, u32[]{:S(2)}, u32[]{:S(2)}) collective-permute-start(f32[2,25,2,8,128]{4,3,2,1,0:T(8,128)S(1)} %pad_maximum_fusion.mid), channel_id=1, source_target_pairs={{0,61},{1,16},{2,63},{3,18},{4,49},{5,20},{6,51},{7,22},{8,53},{9,... | collective-permute-start | bytes 1228808 | tf_op jit(solution)/shard_map/ppermute | solution.py:65
  189.7 12.5 %collective-permute-start.25 = (f32[2,25,2,8,128]{4,3,2,1,0:T(8,128)S(1)}, f32[2,25,2,8,128]{4,3,2,1,0:T(8,128)S(1)}, u32[]{:S(2)}, u32[]{:S(2)}) collective-permute-start(f32[2,25,2,8,128]{4,3,2,1,0:T(8,128)S(1)} %pad_maximum_fusion.mid), channel_id=1, source_target_pairs={{0,1},{1,0},{2,3},{3,2},{4,5},{5,4},{6,7},{7,6},{8,9},{9,8},{10,11... | collective-permute-start | bytes 1228808 | tf_op jit(solution)/shard_map/ppermute | solution.py:65
  196.4 5.8 %collective-permute-start.27 = (f32[2,2,8,128]{3,2,1,0:T(8,128)S(1)}, f32[2,2,8,128]{3,2,1,0:T(8,128)S(1)}, u32[]{:S(2)}, u32[]{:S(2)}) collective-permute-start(f32[2,2,8,128]{3,2,1,0:T(8,128)S(1)} %bitcast.74), channel_id=1, source_target_pairs={{0,48},{1,49},{2,50},{3,51},{4,52},{5,53},{6,54},{7,55},{8,56},{9,... | collective-permute-start | bytes 49160 | tf_op jit(solution)/shard_map/ppermute | solution.py:65
  205.3 6.5 %collective-permute-start.29 = (f32[2,9,2,8,128]{4,3,2,1,0:T(8,128)S(1)}, f32[2,9,2,8,128]{4,3,2,1,0:T(8,128)S(1)}, u32[]{:S(2)}, u32[]{:S(2)}) collective-permute-start(f32[2,9,2,8,128]{4,3,2,1,0:T(8,128)S(1)} %get-tuple-element.47), channel_id=1, source_target_pairs={{0,450},{1,451},{2,448},{3,449},{4,454},{5,455},{6,452},{7,453},{8... | collective-permute-start | bytes 442376 | tf_op jit(solution)/shard_map/ppermute | solution.py:65
  207.2 7.1 %collective-permute-start.28 = (f32[2,9,2,8,128]{4,3,2,1,0:T(8,128)S(1)}, f32[2,9,2,8,128]{4,3,2,1,0:T(8,128)S(1)}, u32[]{:S(2)}, u32[]{:S(2)}) collective-permute-start(f32[2,9,2,8,128]{4,3,2,1,0:T(8,128)S(1)} %get-tuple-element.47), channel_id=1, source_target_pairs={{0,64},{1,65},{2,66},{3,67},{4,68},{5,69},{6,70},{7,71},{8,72},{9,... | collective-permute-start | bytes 442376 | tf_op jit(solution)/shard_map/ppermute | solution.py:65
  214.4 16.7 %collective-permute-start.31 = (f32[2,25,2,8,128]{4,3,2,1,0:T(8,128)S(1)}, f32[2,25,2,8,128]{4,3,2,1,0:T(8,128)S(1)}, u32[]{:S(2)}, u32[]{:S(2)}) collective-permute-start(f32[2,25,2,8,128]{4,3,2,1,0:T(8,128)S(1)} %pad_maximum_fusion.1.mid), channel_id=1, source_target_pairs={{0,61},{1,16},{2,63},{3,18},{4,49},{5,20},{6,51},{7,22},{8,53},{9,... | collective-permute-start | bytes 1228808 | tf_op jit(solution)/shard_map/ppermute | solution.py:65
  218.7 12.4 %collective-permute-start.30 = (f32[2,25,2,8,128]{4,3,2,1,0:T(8,128)S(1)}, f32[2,25,2,8,128]{4,3,2,1,0:T(8,128)S(1)}, u32[]{:S(2)}, u32[]{:S(2)}) collective-permute-start(f32[2,25,2,8,128]{4,3,2,1,0:T(8,128)S(1)} %pad_maximum_fusion.1.mid), channel_id=1, source_target_pairs={{0,1},{1,0},{2,3},{3,2},{4,5},{5,4},{6,7},{7,6},{8,9},{9,8},{10,11... | collective-permute-start | bytes 1228808 | tf_op jit(solution)/shard_map/ppermute | solution.py:65
  224.2 6.9 %collective-permute-start.32 = (f32[2,2,8,128]{3,2,1,0:T(8,128)S(1)}, f32[2,2,8,128]{3,2,1,0:T(8,128)S(1)}, u32[]{:S(2)}, u32[]{:S(2)}) collective-permute-start(f32[2,2,8,128]{3,2,1,0:T(8,128)S(1)} %bitcast.75), channel_id=1, source_target_pairs={{0,28},{1,29},{2,30},{3,31},{4,16},{5,17},{6,18},{7,19},{8,20},{9,... | collective-permute-start | bytes 49160 | tf_op jit(solution)/shard_map/ppermute | solution.py:65
  234.0 5.9 %collective-permute-start.34 = (f32[2,9,2,8,128]{4,3,2,1,0:T(8,128)S(1)}, f32[2,9,2,8,128]{4,3,2,1,0:T(8,128)S(1)}, u32[]{:S(2)}, u32[]{:S(2)}) collective-permute-start(f32[2,9,2,8,128]{4,3,2,1,0:T(8,128)S(1)} %get-tuple-element.49), channel_id=1, source_target_pairs={{0,450},{1,451},{2,448},{3,449},{4,454},{5,455},{6,452},{7,453},{8... | collective-permute-start | bytes 442376 | tf_op jit(solution)/shard_map/ppermute | solution.py:65
  235.9 7.1 %collective-permute-start.33 = (f32[2,9,2,8,128]{4,3,2,1,0:T(8,128)S(1)}, f32[2,9,2,8,128]{4,3,2,1,0:T(8,128)S(1)}, u32[]{:S(2)}, u32[]{:S(2)}) collective-permute-start(f32[2,9,2,8,128]{4,3,2,1,0:T(8,128)S(1)} %get-tuple-element.49), channel_id=1, source_target_pairs={{0,64},{1,65},{2,66},{3,67},{4,68},{5,69},{6,70},{7,71},{8,72},{9,... | collective-permute-start | bytes 442376 | tf_op jit(solution)/shard_map/ppermute | solution.py:65
  243.1 19.1 %collective-permute-start.36 = (f32[2,25,2,8,128]{4,3,2,1,0:T(8,128)S(1)}, f32[2,25,2,8,128]{4,3,2,1,0:T(8,128)S(1)}, u32[]{:S(2)}, u32[]{:S(2)}) collective-permute-start(f32[2,25,2,8,128]{4,3,2,1,0:T(8,128)S(1)} %pad_maximum_fusion.2.mid), channel_id=1, source_target_pairs={{0,61},{1,16},{2,63},{3,18},{4,49},{5,20},{6,51},{7,22},{8,53},{9,... | collective-permute-start | bytes 1228808 | tf_op jit(solution)/shard_map/ppermute | solution.py:65
  247.2 15.1 %collective-permute-start.35 = (f32[2,25,2,8,128]{4,3,2,1,0:T(8,128)S(1)}, f32[2,25,2,8,128]{4,3,2,1,0:T(8,128)S(1)}, u32[]{:S(2)}, u32[]{:S(2)}) collective-permute-start(f32[2,25,2,8,128]{4,3,2,1,0:T(8,128)S(1)} %pad_maximum_fusion.2.mid), channel_id=1, source_target_pairs={{0,1},{1,0},{2,3},{3,2},{4,5},{5,4},{6,7},{7,6},{8,9},{9,8},{10,11... | collective-permute-start | bytes 1228808 | tf_op jit(solution)/shard_map/ppermute | solution.py:65
  249.7 14.9 %collective-permute-start.40 = (f32[2,2,8,128]{3,2,1,0:T(8,128)S(1)}, f32[2,2,8,128]{3,2,1,0:T(8,128)S(1)}, u32[]{:S(2)}, u32[]{:S(2)}) collective-permute-start(f32[2,2,8,128]{3,2,1,0:T(8,128)S(1)} %bitcast.73), channel_id=1, source_target_pairs={{0,2},{1,3},{2,0},{3,1},{4,6},{5,7},{6,4},{7,5},{8,10},{9,11},{10,... | collective-permute-start | bytes 49160 | tf_op jit(solution)/shard_map/ppermute | solution.py:65
  264.6 15.0 %collective-permute-start.41 = (f32[2,2,8,128]{3,2,1,0:T(8,128)S(1)}, f32[2,2,8,128]{3,2,1,0:T(8,128)S(1)}, u32[]{:S(2)}, u32[]{:S(2)}) collective-permute-start(f32[2,2,8,128]{3,2,1,0:T(8,128)S(1)} %compare_select_fusion.1), channel_id=1, source_target_pairs={{0,8},{1,9},{2,10},{3,11},{4,12},{5,13},{6,14},{7,15},{8,0},{9,1},... | collective-permute-start | bytes 49160 | tf_op jit(solution)/shard_map/ppermute | solution.py:65
  270.1 11.8 %collective-permute-start.37 = (f32[2,4,2,8,128]{4,3,2,1,0:T(8,128)S(1)}, f32[2,4,2,8,128]{4,3,2,1,0:T(8,128)S(1)}, u32[]{:S(2)}, u32[]{:S(2)}) collective-permute-start(f32[2,4,2,8,128]{4,3,2,1,0:T(8,128)S(1)} %get-tuple-element.63), channel_id=1, source_target_pairs={{0,0},{1,1},{2,256},{3,257},{4,4},{5,5},{6,260},{7,261},{8,8},{9,9... | collective-permute-start | bytes 196616 | tf_op jit(solution)/shard_map/ppermute | solution.py:65
  274.2 30.9 %collective-permute-start.38 = (f32[2,4,2,8,128]{4,3,2,1,0:T(8,128)S(1)}, f32[2,4,2,8,128]{4,3,2,1,0:T(8,128)S(1)}, u32[]{:S(2)}, u32[]{:S(2)}) collective-permute-start(f32[2,4,2,8,128]{4,3,2,1,0:T(8,128)S(1)} %get-tuple-element.64), channel_id=1, source_target_pairs={{0,16},{1,17},{2,272},{3,273},{4,20},{5,21},{6,276},{7,277},{8,24}... | collective-permute-start | bytes 196616 | tf_op jit(solution)/shard_map/ppermute | solution.py:65
  305.1 3.7 %collective-permute-start.39 = (f32[2,4,2,8,128]{4,3,1,0,2:T(8,128)S(1)}, f32[2,4,2,8,128]{4,3,1,0,2:T(8,128)S(1)}, u32[]{:S(2)}, u32[]{:S(2)}) collective-permute-start(f32[2,4,2,8,128]{4,3,1,0,2:T(8,128)S(1)} %select_bitcast_fusion.3), channel_id=1, source_target_pairs={{0,1},{1,0},{2,3},{3,2},{4,5},{5,4},{6,7},{7,6},{8,9},{9,8},{10,11... | collective-permute-start | bytes 196616 | tf_op jit(solution)/shard_map/ppermute | solution.py:65

commit v4 on v3

--- a/solution.py
+++ b/solution.py
@@ -42,7 +42,7 @@
     return table(place)
 
 
-def across(x, y, z, c):
+def beside(x, y, z, c):
     index = (4 * y + x + (1 if c else -1)) % 16
     return (index % 4, index // 4, z, 1 - c)
 
@@ -56,7 +56,7 @@
 
 
 SWAP = shifted(dc=1)
-ACROSS = table(across)
+ACROSS = table(beside)
 UP = shifted(dz=1)
 DOWN = shifted(dz=-1)
 
@@ -131,18 +131,82 @@
     laplace_planes(buf, bands, 2 * B + margin - 2, 2, PAD + 8, 8, update)
 
 
-def assemble(buf, f, mid, intra, inter, core):
-    buf[:, :, PAD + 8 : PAD + 16, :] = mid[f, :R]
+PAIRS = ((1, 5, 6), (2, 6, 6), (3, 4, 4))
+PACKED = B + 2 * len(PAIRS)
+
+
+def side_planes():
+    for side in range(2):
+        for i, (one, two, rows) in enumerate(PAIRS):
+            tile = B + len(PAIRS) * side + i
+            planes = [B - d if side == 0 else 2 * B - 1 + d for d in (one, two)]
+            yield tile, planes[0], planes[1], rows
+
+
+def pack_first_rows(to, f, mid):
+    for tile, one, two, rows in side_planes():
+        to[f, tile, :, :rows] = mid[f, one, :, :rows]
+        to[f, tile, :, rows:] = mid[f, two, :, : 8 - rows]
+
+
+def pack_last_rows(to, f, mid):
+    for tile, one, two, rows in side_planes():
+        to[f, tile, :, 8 - rows :] = mid[f, one, :, 8 - rows :]
+        to[f, tile, :, : 8 - rows] = mid[f, two, :, rows:]
+
+
+def pack(count, place, low, block, high, mid, swapped, across):
+    for f in range(count):
+        mid[f, :B] = low[f, :B]
+        mid[f, B : 2 * B] = block[f, :B]
+        mid[f, 2 * B : R] = high[f, :B]
+        swapped[f, :B] = block[f, :B]
+        across[f, :B] = block[f, :B]
+        if block.shape[1] > B:
+            known = merge(block[f, B], low[f, B], high[f, B])
+            mid[f, R] = known
+            swapped[f, PACKED] = known
+            across[f, PACKED] = known
+
+    @pl.when(place[2] == 0)
+    def _():
+        for f in range(count):
+            pack_first_rows(across, f, mid)
+            pack_last_rows(swapped, f, mid)
+
+    @pl.when(place[2] == 1)
+    def _():
+        for f in range(count):
+            pack_last_rows(across, f, mid)
+            pack_first_rows(swapped, f, mid)
+
+
+def unpack_below(buf, base, f, came):
+    buf[B : 2 * B, :, base : base + 8, :] = came[f, :B]
+    for tile, one, two, rows in side_planes():
+        buf[one, :, base + 8 - rows : base + 8, :] = came[f, tile, :, 8 - rows :]
+        buf[two, :, base + rows : base + 8, :] = came[f, tile, :, : 8 - rows]
+
+
+def unpack_above(buf, base, f, came):
+    buf[B : 2 * B, :, base + 16 : base + 24, :] = came[f, :B]
+    for tile, one, two, rows in side_planes():
+        buf[one, :, base + 16 : base + 16 + rows, :] = came[f, tile, :, :rows]
+        buf[two, :, base + 16 : base + 24 - rows, :] = came[f, tile, :, rows:]
+
+
+def assemble(buf, base, f, mid, inter, intra, core):
+    buf[:, :, base + 8 : base + 16, :] = mid[f, :R]
 
     @pl.when(core == 0)
     def _():
-        buf[:, :, PAD : PAD + 8, :] = inter[f, :R]
-        buf[:, :, PAD + 16 : PAD + 24, :] = intra[f, :R]
+        unpack_below(buf, base, f, inter)
+        unpack_above(buf, base, f, intra)
 
     @pl.when(core == 1)
     def _():
-        buf[:, :, PAD : PAD + 8, :] = intra[f, :R]
-        buf[:, :, PAD + 16 : PAD + 24, :] = inter[f, :R]
+        unpack_below(buf, base, f, intra)
+        unpack_above(buf, base, f, inter)
 
 
 def own(buf):
@@ -183,23 +247,12 @@
 
 
 def first_forward(
-    place, checkpoints, receivers, mine, counts, mid, intra, inter, vel, src, pair, traces, a, b, bands
+    place, checkpoints, receivers, mine, counts, mid, inter, intra, vel, src, pair, traces, a, b, bands
 ):
-    core = place[2]
+    vel[...] = jnp.zeros_like(vel)
+    src[...] = jnp.zeros_like(src)
     for f in range(5):
-        into = vel if f == 0 else src.at[f - 1]
-        into[:, :, 8:16, :] = mid[f]
-
-        @pl.when(core == 0)
-        def _():
-            into[:, :, 0:8, :] = inter[f]
-            into[:, :, 16:24, :] = intra[f]
-
-        @pl.when(core == 1)
-        def _():
-            into[:, :, 0:8, :] = intra[f]
-            into[:, :, 16:24, :] = inter[f]
-
+        assemble(vel if f == 0 else src.at[f - 1], 0, f, mid, inter, intra, place[2])
     bands[...] = band()
     vel[...] = vel[...] * (1.0 / 12.0)
     traces[...] = jnp.zeros_like(traces)
@@ -214,11 +267,11 @@
 
 
 def later_forward(
-    steps, place, checkpoints, receivers, mine, counts, vel, src, mid, intra, inter, held,
+    steps, place, checkpoints, receivers, mine, counts, vel, src, mid, inter, intra, held,
     pair, traces, a, b, bands,
 ):
-    assemble(a, 0, mid, intra, inter, place[2])
-    assemble(b, 1, mid, intra, inter, place[2])
+    assemble(a, PAD, 0, mid, inter, intra, place[2])
+    assemble(b, PAD, 1, mid, inter, intra, place[2])
     bands[...] = band()
     traces[...] = held[...]
     prev, cur = forward_steps(
@@ -291,11 +344,11 @@
 
 
 def later_adjoint(
-    steps, place, checkpoints, receivers, near, counts, traces, vel, back_own, mid, intra, inter,
+    steps, place, checkpoints, receivers, near, counts, traces, vel, back_own, mid, inter, intra,
     held, far, pair, image, a, b, w, bands,
 ):
-    assemble(a, 0, mid, intra, inter, place[2])
-    assemble(b, 1, mid, intra, inter, place[2])
+    assemble(a, PAD, 0, mid, inter, intra, place[2])
+    assemble(b, PAD, 1, mid, inter, intra, place[2])
     image[...] = held[...]
     bands[...] = band()
     later, now = adjoint_steps(
@@ -303,7 +356,7 @@
     )
     for f, buf in enumerate((later, now)):
         pair[f, :B] = own(buf)
-        pair[f, B] = merge(mid[f, R], intra[f, R], inter[f, R], far[f])
+        pair[f, B] = merge(mid[f, R], intra[f, PACKED], inter[f, PACKED], far[f])
 
 
 def list_receivers(place, receivers, mine, near, counts):
@@ -356,19 +409,18 @@
     )
 
 
-def exchange(block):
-    low = send(block, UP)
-    high = send(block, DOWN)
-    mid = jnp.concatenate([low, block, high], axis=1)
-    return mid, send(mid, SWAP), send(mid, ACROSS)
-
-
-def exchange_carrying(block, jump):
-    low = send(block, UP)
-    high = send(block, DOWN)
-    known = merge(block[:, B:], low[:, B:], high[:, B:])
-    mid = jnp.concatenate([low[:, :B], block[:, :B], high[:, :B], known], axis=1)
-    return (mid, send(mid, SWAP), send(mid, ACROSS)), send(mid[:, R], jump)
+def exchange(block, place, jump=None):
+    count, planes = block.shape[:2]
+    small = f32(count, planes + PACKED - B, 2, B, 128)
+    mid, swapped, across = pl.pallas_call(
+        functools.partial(pack, count),
+        in_specs=[SM] + [VM] * 3,
+        out_specs=[VM] * 3,
+        out_shape=[f32(count, planes + R - B, 2, B, 128), small, small],
+        compiler_params=pltpu.CompilerParams(vmem_limit_bytes=48 * 1024 * 1024),
+    )(place, send(block, UP), block, send(block, DOWN))
+    parts = (mid, send(across, ACROSS), send(swapped, SWAP))
+    return parts if jump is None else (parts, send(mid[:, R], jump))
 
 
 def pick(two, index):
@@ -402,10 +454,13 @@
 
 def outward_near(got, other, core, odd):
     whole = ordered(got, other, odd, 2)
+    column = jnp.sum(whole[0], axis=(2, 4)) / 256.0
+    spread_out = jnp.broadcast_to(column[None, ..., None], (1, *column.shape, 128))
     front, rear = whole[:, :, :, 0], whole[:, :, :, 1]
     kept = pick((front, rear), core)
-    came = send(pick((rear, front), core), SWAP)
-    return ordered(kept, came, core, 3).reshape(-1, 4, 32, 128)
+    came = send(jnp.concatenate([pick((rear, front), core), spread_out], axis=0), SWAP)
+    column = ordered(column, came[-1, ..., 0], core, 2).reshape(4, 32)
+    return *ordered(kept, came[:-1], core, 3).reshape(-1, 4, 32, 128), column
 
 
 def on_device(velocity_term, model_step, background, receivers, checkpoints):
@@ -435,7 +490,7 @@
         [f32(R, 2, R, 128), f32(4, R, 2, R, 128), f32(2, B, 2, B, 128), f32(NT, 256)],
         [VM] * 4,
         2,
-    )(place, checkpoints, receivers, mine, counts, *exchange(fields))
+    )(place, checkpoints, receivers, mine, counts, *exchange(fields, place))
     for steps in (range(5, 9), range(9, 13), range(13, 16)):
         pair, traces = call(
             functools.partial(later_forward, steps),
@@ -443,7 +498,7 @@
             [f32(2, B, 2, B, 128), f32(NT, 256)],
             [VM] * 2,
             2,
-        )(place, checkpoints, receivers, mine, counts, vel, src, *exchange(pair), traces)
+        )(place, checkpoints, receivers, mine, counts, vel, src, *exchange(pair, place), traces)
     field = pair[1]
     local = merge(traces, send(traces, UP), send(traces, DOWN))
     local = merge(local, send(local, ACROSS), send(local, SWAP))
@@ -455,15 +510,16 @@
     )
     jumps = (around(3), around(-3), shifted(dz=8))
     for steps, jump in zip((range(10, 6, -1), range(6, 2, -1), range(2, -1, -1)), jumps):
-        parts, more = exchange_carrying(pair, jump)
+        parts, more = exchange(pair, place, jump)
         pair, image = call(
             functools.partial(later_adjoint, steps), [SM] * 6 + [VM] * 7, outs, [VM] * 2, 3
         )(*scalars, vel, back_own, *parts, image, more if steps.stop > -1 else carried)
-    image, wavefield = outward_near(*outward_far(jnp.stack([image, field]), odd), core, odd)
-    carried = merge(pair[:, B], more)
+    got, other = outward_far(jnp.stack([image, field]), odd)
+    got, last, more = lax.optimization_barrier((got, pair[:, B], more))
+    image, wavefield, column_image = outward_near(got, other, core, odd)
+    carried = merge(last, more)
     carried = merge(carried, send(carried, shifted(dy=2)))
     traces = carried.transpose(0, 2, 1, 3).reshape(NT, 256)
-    column_image = lax.psum(jnp.sum(image, axis=2), "c") / 256.0
     return (image, traces, column_image, wavefield)
 
 

time: 315 us -> 306 us (0.971)
  the two profiles are of different devices: /device:TPU:137 before, /device:TPU:130 now
where the time goes in v4:
time: 306 us; the launch traced here: 304 us
  starting transfers between devices  163 us (53%)
  waiting for transfers between devices  96.1 us (31%)
  Pallas kernels  38.3 us (13%)
  other arithmetic  3.4 us (1%)
    ppermute x42, starting transfers between devices, send(): return lax.ppermute(value, AXES, pairs)  163 us
    ppermute x42, waiting for transfers between devices, send(): return lax.ppermute(value, AXES, pairs)  96.1 us
    pallas_call x3, Pallas kernels, on_device(): call(functools.partial(later_forward, steps), [SM] * 5 + [VM] * 6, [f32(2...  10.6 us
    pallas_call x3, Pallas kernels, on_device(): call(functools.partial(later_adjoint, steps), [SM] * 6 + [VM] * 7, outs,...  8.71 us
    pallas_call x1, Pallas kernels, on_device(): pl.pallas_call(list_receivers, in_specs=[SM, SM], out_specs=[SM, SM, SM],...  6.57 us
  transfers between devices with their start and end apart: 42, of which 27 were waited for; matrix products, arithmetic and copies ran while one was open for 0% of the time, Pallas kernels for 3%

profile of v4, /device:TPU:130, one launch (start us, length us, event | category | flops | bytes accessed | tf_op | source)
XLA Modules:
  0.0 304.4 jit_solution(7408226562726374880)
XLA Ops:
  2.5 1.9 collective-permute-start
  6.0 9.1 %collective-permute-start.1 = (f32[6,4,2,8,128]{4,3,2,1,0:T(8,128)S(1)}, f32[6,4,2,8,128]{4,3,2,1,0:T(8,128)S(1)}, u32[]{:S(2)}, u32[]{:S(2)}) collective-permute-start(f32[6,4,2,8,128]{4,3,2,1,0:T(8,128)S(1)} %get-tuple-element.104), channel_id=1, source_target_pairs={{0,0},{1,1},{2,32},{3,33},{4,4},{5,5},{6,36},{7,37},{8,8},{9,9},{1... | collective-permute-start | bytes 589832 | tf_op jit(solution)/shard_map/ppermute | solution.py:65
  15.1 1.9 collective-permute-start.2
  17.6 6.6 %shard_map.84 = (s32[256]{0:T(256)}, s32[256]{0:T(256)}, s32[2]{0:T(128)}) custom-call(s32[4]{0:T(128)} %pad_add_fusion.place, s32[3,256]{1,0:T(4,128)} %receivers.17), custom_call_target="tpu_custom_call" | custom-call | tf_op jit(solution)/shard_map/pallas_call | solution.py:473
  24.6 7.6 %collective-permute-done.2 = f32[6,4,2,8,128]{4,3,2,1,0:T(8,128)S(1)} collective-permute-done((f32[6,4,2,8,128]{4,3,2,1,0:T(8,128)S(1)}, f32[6,4,2,8,128]{4,3,2,1,0:T(8,128)S(1)}, u32[]{:S(2)}, u32[]{:S(2)}) %collective-permute-start.2) | collective-permute-done | bytes 196640 | tf_op jit(solution)/shard_map/ppermute | solution.py:65
  32.3 1.9 collective-permute-start.4
  34.3 11.8 %collective-permute-start.3 = (f32[5,8,2,8,128]{4,3,2,1,0:T(8,128)S(1)}, f32[5,8,2,8,128]{4,3,2,1,0:T(8,128)S(1)}, u32[]{:S(2)}, u32[]{:S(2)}) collective-permute-start(f32[5,8,2,8,128]{4,3,2,1,0:T(8,128)S(1)} %pad_maximum_fusion.1.block), channel_id=1, source_target_pairs={{0,64},{1,65},{2,66},{3,67},{4,68},{5,69},{6,70},{7,71},{8,72},{9,... | collective-permute-start | bytes 983048 | tf_op jit(solution)/shard_map/ppermute | solution.py:65
  46.0 11.1 %collective-permute-done.4.high = f32[5,8,2,8,128]{4,3,2,1,0:T(8,128)S(1)} collective-permute-done((f32[5,8,2,8,128]{4,3,2,1,0:T(8,128)S(1)}, f32[5,8,2,8,128]{4,3,2,1,0:T(8,128)S(1)}, u32[]{:S(2)}, u32[]{:S(2)}) %collective-permute-start.4) | collective-permute-done | bytes 327712 | tf_op jit(solution)/shard_map/ppermute | solution.py:65
  57.9 1.9 collective-permute-start.5
  59.8 12.4 %collective-permute-start.6 = (f32[5,14,2,8,128]{4,3,2,1,0:T(8,128)S(1)}, f32[5,14,2,8,128]{4,3,2,1,0:T(8,128)S(1)}, u32[]{:S(2)}, u32[]{:S(2)}) collective-permute-start(f32[5,14,2,8,128]{4,3,2,1,0:T(8,128)S(1)} %get-tuple-element.62), channel_id=1, source_target_pairs={{0,1},{1,0},{2,3},{3,2},{4,5},{5,4},{6,7},{7,6},{8,9},{9,8},{10,11... | collective-permute-start | bytes 1720328 | tf_op jit(solution)/shard_map/ppermute | solution.py:65
  73.8 4.7 %shard_map.86 = (f32[24,2,24,128]{3,2,1,0:T(8,128)S(1)}, f32[4,24,2,24,128]{4,3,2,1,0:T(8,128)S(1)}, f32[2,8,2,8,128]{4,3,2,1,0:T(8,128)S(1)}, f32[16,256]{1,0:T(8,128)S(1)}) custom-call(s32[4]{0:T(128)S(1)} %copy-done.1, s32[16]{0:T(128)S(1)} %copy-done.2, s32[3,256]{1,0:T(4,128)S(1)} %copy-done, s32[256]{0:T(256)S(1)} %copy-done.5, s32[2]{0:T(128)S(1)} %copy-done.3, ...), custom_call_target="tpu_custom_call" | custom-call | tf_op jit(solution)/shard_map/pallas_call | solution.py:487
  78.5 1.9 collective-permute-start.8
  80.4 3.9 %collective-permute-start.7 = (f32[2,8,2,8,128]{4,3,2,1,0:T(8,128)S(1)}, f32[2,8,2,8,128]{4,3,2,1,0:T(8,128)S(1)}, u32[]{:S(2)}, u32[]{:S(2)}) collective-permute-start(f32[2,8,2,8,128]{4,3,2,1,0:T(8,128)S(1)} %get-tuple-element.65.block), channel_id=1, source_target_pairs={{0,64},{1,65},{2,66},{3,67},{4,68},{5,69},{6,70},{7,71},{8,72},{9,... | collective-permute-start | bytes 393224 | tf_op jit(solution)/shard_map/ppermute | solution.py:65
  85.4 3.1 %collective-permute-done.7.low = f32[2,8,2,8,128]{4,3,2,1,0:T(8,128)S(1)} collective-permute-done((f32[2,8,2,8,128]{4,3,2,1,0:T(8,128)S(1)}, f32[2,8,2,8,128]{4,3,2,1,0:T(8,128)S(1)}, u32[]{:S(2)}, u32[]{:S(2)}) %collective-permute-start.7) | collective-permute-done | bytes 131104 | tf_op jit(solution)/shard_map/ppermute | solution.py:65
  89.1 1.9 collective-permute-start.9
  91.1 7.8 %collective-permute-start.10 = (f32[2,14,2,8,128]{4,3,2,1,0:T(8,128)S(1)}, f32[2,14,2,8,128]{4,3,2,1,0:T(8,128)S(1)}, u32[]{:S(2)}, u32[]{:S(2)}) collective-permute-start(f32[2,14,2,8,128]{4,3,2,1,0:T(8,128)S(1)} %get-tuple-element.68), channel_id=1, source_target_pairs={{0,1},{1,0},{2,3},{3,2},{4,5},{5,4},{6,7},{7,6},{8,9},{9,8},{10,11... | collective-permute-start | bytes 688136 | tf_op jit(solution)/shard_map/ppermute | solution.py:65
  100.0 3.8 %shard_map.88 = (f32[2,8,2,8,128]{4,3,2,1,0:T(8,128)S(1)}, f32[16,256]{1,0:T(8,128)S(1)}) custom-call(s32[4]{0:T(128)S(1)} %copy-done.1, s32[16]{0:T(128)S(1)} %copy-done.2, s32[3,256]{1,0:T(4,128)S(1)} %copy-done, s32[256]{0:T(256)S(1)} %copy-done.5, s32[2]{0:T(128)S(1)} %copy-done.3, f32[24,2,24,128]{3,2,1,0:T(8,128)S(1)} %get-tuple-element.63.vel, ...), custom_call_target="tpu_custom_call" | custom-call | tf_op jit(solution)/shard_map/pallas_call | solution.py:495
  103.8 2.5 collective-permute-start.12
  106.4 3.3 %collective-permute-start.11 = (f32[2,8,2,8,128]{4,3,2,1,0:T(8,128)S(1)}, f32[2,8,2,8,128]{4,3,2,1,0:T(8,128)S(1)}, u32[]{:S(2)}, u32[]{:S(2)}) collective-permute-start(f32[2,8,2,8,128]{4,3,2,1,0:T(8,128)S(1)} %get-tuple-element.70.block), channel_id=1, source_target_pairs={{0,64},{1,65},{2,66},{3,67},{4,68},{5,69},{6,70},{7,71},{8,72},{9,... | collective-permute-start | bytes 393224 | tf_op jit(solution)/shard_map/ppermute | solution.py:65
  110.7 4.2 %collective-permute-done.11.low = f32[2,8,2,8,128]{4,3,2,1,0:T(8,128)S(1)} collective-permute-done((f32[2,8,2,8,128]{4,3,2,1,0:T(8,128)S(1)}, f32[2,8,2,8,128]{4,3,2,1,0:T(8,128)S(1)}, u32[]{:S(2)}, u32[]{:S(2)}) %collective-permute-start.11) | collective-permute-done | bytes 131104 | tf_op jit(solution)/shard_map/ppermute | solution.py:65
  115.6 3.0 collective-permute-start.13
  118.6 1.9 collective-permute-start.14
  120.5 2.4 collective-permute-done.13.inter
  122.9 3.8 %shard_map.90 = (f32[2,8,2,8,128]{4,3,2,1,0:T(8,128)S(1)}, f32[16,256]{1,0:T(8,128)S(1)}) custom-call(s32[4]{0:T(128)S(1)} %copy-done.1, s32[16]{0:T(128)S(1)} %copy-done.2, s32[3,256]{1,0:T(4,128)S(1)} %copy-done, s32[256]{0:T(256)S(1)} %copy-done.5, s32[2]{0:T(128)S(1)} %copy-done.3, f32[24,2,24,128]{3,2,1,0:T(8,128)S(1)} %get-tuple-element.63.vel, ...), custom_call_target="tpu_custom_call" | custom-call | tf_op jit(solution)/shard_map/pallas_call | solution.py:495
  126.8 1.9 collective-permute-start.16
  128.7 3.9 %collective-permute-start.15 = (f32[2,8,2,8,128]{4,3,2,1,0:T(8,128)S(1)}, f32[2,8,2,8,128]{4,3,2,1,0:T(8,128)S(1)}, u32[]{:S(2)}, u32[]{:S(2)}) collective-permute-start(f32[2,8,2,8,128]{4,3,2,1,0:T(8,128)S(1)} %get-tuple-element.75.block), channel_id=1, source_target_pairs={{0,64},{1,65},{2,66},{3,67},{4,68},{5,69},{6,70},{7,71},{8,72},{9,... | collective-permute-start | bytes 393224 | tf_op jit(solution)/shard_map/ppermute | solution.py:65
  133.6 3.4 %collective-permute-done.15.low = f32[2,8,2,8,128]{4,3,2,1,0:T(8,128)S(1)} collective-permute-done((f32[2,8,2,8,128]{4,3,2,1,0:T(8,128)S(1)}, f32[2,8,2,8,128]{4,3,2,1,0:T(8,128)S(1)}, u32[]{:S(2)}, u32[]{:S(2)}) %collective-permute-start.15) | collective-permute-done | bytes 131104 | tf_op jit(solution)/shard_map/ppermute | solution.py:65
  137.7 7.2 %collective-permute-start.17 = (f32[2,14,2,8,128]{4,3,2,1,0:T(8,128)S(1)}, f32[2,14,2,8,128]{4,3,2,1,0:T(8,128)S(1)}, u32[]{:S(2)}, u32[]{:S(2)}) collective-permute-start(f32[2,14,2,8,128]{4,3,2,1,0:T(8,128)S(1)} %get-tuple-element.77), channel_id=1, source_target_pairs={{0,61},{1,16},{2,63},{3,18},{4,49},{5,20},{6,51},{7,22},{8,53},{9,... | collective-permute-start | bytes 688136 | tf_op jit(solution)/shard_map/ppermute | solution.py:65
  144.9 2.6 collective-permute-start.18
  148.6 2.9 shard_map.92
  151.5 1.9 collective-permute-start.19
  153.5 5.1 %collective-permute-start.20 = (f32[16,256]{1,0:T(8,128)S(1)}, f32[16,256]{1,0:T(8,128)S(1)}, u32[]{:S(2)}, u32[]{:S(2)}) collective-permute-start(f32[16,256]{1,0:T(8,128)S(1)} %get-tuple-element.80), channel_id=1, source_target_pairs={{0,450},{1,451},{2,448},{3,449},{4,454},{5,455},{6,452},{7,453},{8... | collective-permute-start | bytes 49160 | tf_op jit(solution)/shard_map/ppermute | solution.py:65
  160.0 6.4 %collective-permute-start.21 = (f32[16,256]{1,0:T(8,128)S(1)}, f32[16,256]{1,0:T(8,128)S(1)}, u32[]{:S(2)}, u32[]{:S(2)}) collective-permute-start(f32[16,256]{1,0:T(8,128)S(1)} %compare_select_fusion.4), channel_id=1, source_target_pairs={{0,61},{1,16},{2,63},{3,18},{4,49},{5,20},{6,51},{7,22},{8,53},{9,... | collective-permute-start | bytes 49160 | tf_op jit(solution)/shard_map/ppermute | solution.py:65
  166.4 1.9 collective-permute-start.22
  169.5 3.3 %shard_map.93 = (f32[2,9,2,8,128]{4,3,2,1,0:T(8,128)S(1)}, f32[8,2,8,128]{3,2,1,0:T(8,128)S(1)}) custom-call(s32[4]{0:T(128)S(1)} %copy-done.1, s32[16]{0:T(128)S(1)} %copy-done.2, s32[3,256]{1,0:T(4,128)S(1)} %copy-done, s32[256]{0:T(256)S(1)} %copy-done.4, s32[2]{0:T(128)S(1)} %copy-done.3, f32[16,256]{1,0:T(8,128)S(1)} %compare_select_fusion.2.traces, ...), custom_call_target="tpu_custom_call" | custom-call | tf_op jit(solution)/shard_map/pallas_call | solution.py:508
  172.8 5.0 %collective-permute-start.24 = (f32[2,9,2,8,128]{4,3,2,1,0:T(8,128)S(1)}, f32[2,9,2,8,128]{4,3,2,1,0:T(8,128)S(1)}, u32[]{:S(2)}, u32[]{:S(2)}) collective-permute-start(f32[2,9,2,8,128]{4,3,2,1,0:T(8,128)S(1)} %get-tuple-element.81.block), channel_id=1, source_target_pairs={{0,450},{1,451},{2,448},{3,449},{4,454},{5,455},{6,452},{7,453},{8... | collective-permute-start | bytes 442376 | tf_op jit(solution)/shard_map/ppermute | solution.py:65
  177.8 1.9 collective-permute-start.23
  181.3 5.3 %collective-permute-done.23.low = f32[2,9,2,8,128]{4,3,2,1,0:T(8,128)S(1)} collective-permute-done((f32[2,9,2,8,128]{4,3,2,1,0:T(8,128)S(1)}, f32[2,9,2,8,128]{4,3,2,1,0:T(8,128)S(1)}, u32[]{:S(2)}, u32[]{:S(2)}) %collective-permute-start.23) | collective-permute-done | bytes 147488 | tf_op jit(solution)/shard_map/ppermute | solution.py:65
  187.3 5.7 %collective-permute-start.25 = (f32[2,15,2,8,128]{4,3,2,1,0:T(8,128)S(1)}, f32[2,15,2,8,128]{4,3,2,1,0:T(8,128)S(1)}, u32[]{:S(2)}, u32[]{:S(2)}) collective-permute-start(f32[2,15,2,8,128]{4,3,2,1,0:T(8,128)S(1)} %get-tuple-element.83), channel_id=1, source_target_pairs={{0,61},{1,16},{2,63},{3,18},{4,49},{5,20},{6,51},{7,22},{8,53},{9,... | collective-permute-start | bytes 737288 | tf_op jit(solution)/shard_map/ppermute | solution.py:65
  192.9 1.9 collective-permute-start.26
  194.9 3.6 %collective-permute-start.27 = (f32[2,2,8,128]{3,2,1,0:T(8,128)S(1)}, f32[2,2,8,128]{3,2,1,0:T(8,128)S(1)}, u32[]{:S(2)}, u32[]{:S(2)}) collective-permute-start(f32[2,2,8,128]{3,2,1,0:T(8,128)S(1)} %slice_bitcast_fusion.3), channel_id=1, source_target_pairs={{0,48},{1,49},{2,50},{3,51},{4,52},{5,53},{6,54},{7,55},{8,56},{9,... | collective-permute-start | bytes 49160 | tf_op jit(solution)/shard_map/ppermute | solution.py:65
  198.5 6.8 %collective-permute-done.27.far = f32[2,2,8,128]{3,2,1,0:T(8,128)S(1)} collective-permute-done((f32[2,2,8,128]{3,2,1,0:T(8,128)S(1)}, f32[2,2,8,128]{3,2,1,0:T(8,128)S(1)}, u32[]{:S(2)}, u32[]{:S(2)}) %collective-permute-start.27) | collective-permute-done | bytes 16416 | tf_op jit(solution)/shard_map/ppermute | solution.py:65
  205.3 3.2 %shard_map.95 = (f32[2,9,2,8,128]{4,3,2,1,0:T(8,128)S(1)}, f32[8,2,8,128]{3,2,1,0:T(8,128)S(1)}) custom-call(s32[4]{0:T(128)S(1)} %copy-done.1, s32[16]{0:T(128)S(1)} %copy-done.2, s32[3,256]{1,0:T(4,128)S(1)} %copy-done, s32[256]{0:T(256)S(1)} %copy-done.4, s32[2]{0:T(128)S(1)} %copy-done.3, f32[16,256]{1,0:T(8,128)S(1)} %compare_select_fusion.2.traces, ...), custom_call_target="tpu_custom_call" | custom-call | tf_op jit(solution)/shard_map/pallas_call | solution.py:514
  208.6 1.9 collective-permute-start.29
  210.5 3.9 %collective-permute-start.28 = (f32[2,9,2,8,128]{4,3,2,1,0:T(8,128)S(1)}, f32[2,9,2,8,128]{4,3,2,1,0:T(8,128)S(1)}, u32[]{:S(2)}, u32[]{:S(2)}) collective-permute-start(f32[2,9,2,8,128]{4,3,2,1,0:T(8,128)S(1)} %get-tuple-element.86.block), channel_id=1, source_target_pairs={{0,64},{1,65},{2,66},{3,67},{4,68},{5,69},{6,70},{7,71},{8,72},{9,... | collective-permute-start | bytes 442376 | tf_op jit(solution)/shard_map/ppermute | solution.py:65
  215.6 3.1 %collective-permute-done.28.low = f32[2,9,2,8,128]{4,3,2,1,0:T(8,128)S(1)} collective-permute-done((f32[2,9,2,8,128]{4,3,2,1,0:T(8,128)S(1)}, f32[2,9,2,8,128]{4,3,2,1,0:T(8,128)S(1)}, u32[]{:S(2)}, u32[]{:S(2)}) %collective-permute-start.28) | collective-permute-done | bytes 147488 | tf_op jit(solution)/shard_map/ppermute | solution.py:65
  219.4 3.3 %collective-permute-start.30 = (f32[2,15,2,8,128]{4,3,2,1,0:T(8,128)S(1)}, f32[2,15,2,8,128]{4,3,2,1,0:T(8,128)S(1)}, u32[]{:S(2)}, u32[]{:S(2)}) collective-permute-start(f32[2,15,2,8,128]{4,3,2,1,0:T(8,128)S(1)} %get-tuple-element.88), channel_id=1, source_target_pairs={{0,61},{1,16},{2,63},{3,18},{4,49},{5,20},{6,51},{7,22},{8,53},{9,... | collective-permute-start | bytes 737288 | tf_op jit(solution)/shard_map/ppermute | solution.py:65
  222.7 3.4 %collective-permute-start.31 = (f32[2,15,2,8,128]{4,3,2,1,0:T(8,128)S(1)}, f32[2,15,2,8,128]{4,3,2,1,0:T(8,128)S(1)}, u32[]{:S(2)}, u32[]{:S(2)}) collective-permute-start(f32[2,15,2,8,128]{4,3,2,1,0:T(8,128)S(1)} %get-tuple-element.89), channel_id=1, source_target_pairs={{0,1},{1,0},{2,3},{3,2},{4,5},{5,4},{6,7},{7,6},{8,9},{9,8},{10,11... | collective-permute-start | bytes 737288 | tf_op jit(solution)/shard_map/ppermute | solution.py:65
  226.1 5.1 %collective-permute-start.32 = (f32[2,2,8,128]{3,2,1,0:T(8,128)S(1)}, f32[2,2,8,128]{3,2,1,0:T(8,128)S(1)}, u32[]{:S(2)}, u32[]{:S(2)}) collective-permute-start(f32[2,2,8,128]{3,2,1,0:T(8,128)S(1)} %slice_bitcast_fusion.2), channel_id=1, source_target_pairs={{0,28},{1,29},{2,30},{3,31},{4,16},{5,17},{6,18},{7,19},{8,20},{9,... | collective-permute-start | bytes 49160 | tf_op jit(solution)/shard_map/ppermute | solution.py:65
  232.7 3.1 %shard_map.97 = (f32[2,9,2,8,128]{4,3,2,1,0:T(8,128)S(1)}, f32[8,2,8,128]{3,2,1,0:T(8,128)S(1)}) custom-call(s32[4]{0:T(128)S(1)} %copy-done.1, s32[16]{0:T(128)S(1)} %copy-done.2, s32[3,256]{1,0:T(4,128)S(1)} %copy-done, s32[256]{0:T(256)S(1)} %copy-done.4, s32[2]{0:T(128)S(1)} %copy-done.3, f32[16,256]{1,0:T(8,128)S(1)} %compare_select_fusion.2.traces, ...), custom_call_target="tpu_custom_call" | custom-call | tf_op jit(solution)/shard_map/pallas_call | solution.py:514
  235.8 2.0 collective-permute-start.34
  237.8 3.8 %collective-permute-start.33 = (f32[2,9,2,8,128]{4,3,2,1,0:T(8,128)S(1)}, f32[2,9,2,8,128]{4,3,2,1,0:T(8,128)S(1)}, u32[]{:S(2)}, u32[]{:S(2)}) collective-permute-start(f32[2,9,2,8,128]{4,3,2,1,0:T(8,128)S(1)} %get-tuple-element.91.block), channel_id=1, source_target_pairs={{0,64},{1,65},{2,66},{3,67},{4,68},{5,69},{6,70},{7,71},{8,72},{9,... | collective-permute-start | bytes 442376 | tf_op jit(solution)/shard_map/ppermute | solution.py:65
  242.8 3.3 %collective-permute-done.33.low = f32[2,9,2,8,128]{4,3,2,1,0:T(8,128)S(1)} collective-permute-done((f32[2,9,2,8,128]{4,3,2,1,0:T(8,128)S(1)}, f32[2,9,2,8,128]{4,3,2,1,0:T(8,128)S(1)}, u32[]{:S(2)}, u32[]{:S(2)}) %collective-permute-start.33) | collective-permute-done | bytes 147488 | tf_op jit(solution)/shard_map/ppermute | solution.py:65
  246.7 1.9 collective-permute-start.35
  248.6 4.2 %collective-permute-start.36 = (f32[2,15,2,8,128]{4,3,2,1,0:T(8,128)S(1)}, f32[2,15,2,8,128]{4,3,2,1,0:T(8,128)S(1)}, u32[]{:S(2)}, u32[]{:S(2)}) collective-permute-start(f32[2,15,2,8,128]{4,3,2,1,0:T(8,128)S(1)} %get-tuple-element.94), channel_id=1, source_target_pairs={{0,1},{1,0},{2,3},{3,2},{4,5},{5,4},{6,7},{7,6},{8,9},{9,8},{10,11... | collective-permute-start | bytes 737288 | tf_op jit(solution)/shard_map/ppermute | solution.py:65
  252.9 6.5 %collective-permute-start.38 = (f32[2,2,8,128]{3,2,1,0:T(8,128)S(1)}, f32[2,2,8,128]{3,2,1,0:T(8,128)S(1)}, u32[]{:S(2)}, u32[]{:S(2)}) collective-permute-start(f32[2,2,8,128]{3,2,1,0:T(8,128)S(1)} %slice_bitcast_fusion.1), channel_id=1, source_target_pairs={{0,2},{1,3},{2,0},{3,1},{4,6},{5,7},{6,4},{7,5},{8,10},{9,11},{10,... | collective-permute-start | bytes 49160 | tf_op jit(solution)/shard_map/ppermute | solution.py:65
  259.4 2.4 shard_map.99
  261.8 1.9 collective-permute-start.37
  263.8 4.6 %collective-permute-start.39 = (f32[2,4,2,8,128]{4,3,2,1,0:T(8,128)S(1)}, f32[2,4,2,8,128]{4,3,2,1,0:T(8,128)S(1)}, u32[]{:S(2)}, u32[]{:S(2)}) collective-permute-start(f32[2,4,2,8,128]{4,3,2,1,0:T(8,128)S(1)} %get-tuple-element.111), channel_id=1, source_target_pairs={{0,16},{1,17},{2,272},{3,273},{4,20},{5,21},{6,276},{7,277},{8,24}... | collective-permute-start | bytes 196616 | tf_op jit(solution)/shard_map/ppermute | solution.py:65
  268.4 23.0 %collective-permute-done.37 = f32[2,4,2,8,128]{4,3,2,1,0:T(8,128)S(1)} collective-permute-done((f32[2,4,2,8,128]{4,3,2,1,0:T(8,128)S(1)}, f32[2,4,2,8,128]{4,3,2,1,0:T(8,128)S(1)}, u32[]{:S(2)}, u32[]{:S(2)}) %collective-permute-start.37) | collective-permute-done | bytes 65568 | tf_op jit(solution)/shard_map/ppermute | solution.py:65
  291.4 3.0 collective-permute-done.39
  294.6 1.9 collective-permute-start.41
  296.6 1.9 collective-permute-start.40
  298.5 3.2 %collective-permute-done.41 = f32[2,2,8,128]{3,2,1,0:T(8,128)S(1)} collective-permute-done((f32[2,2,8,128]{3,2,1,0:T(8,128)S(1)}, f32[2,2,8,128]{3,2,1,0:T(8,128)S(1)}, u32[]{:S(2)}, u32[]{:S(2)}) %collective-permute-start.41) | collective-permute-done | bytes 16416 | tf_op jit(solution)/shard_map/ppermute | solution.py:65
  (89 shorter events, 26.6 us)
Async XLA Ops:
  2.5 3.3 %collective-permute-start = (f32[6,4,2,8,128]{4,3,1,0,2:T(8,128)S(1)}, f32[6,4,2,8,128]{4,3,1,0,2:T(8,128)S(1)}, u32[]{:S(2)}, u32[]{:S(2)}) collective-permute-start(f32[6,4,2,8,128]{4,3,1,0,2:T(8,128)S(1)} %select_bitcast_fusion.2), channel_id=1, source_target_pairs={{0,1},{1,0},{2,3},{3,2},{4,5},{5,4},{6,7},{7,6},{8,9},{9,8},{10,11... | collective-permute-start | bytes 589832 | tf_op jit(solution)/shard_map/ppermute | solution.py:65
  5.9 67.9 %copy-start = (s32[3,256]{1,0:T(4,128)S(1)}, s32[3,256]{1,0:T(4,128)}, u32[]{:S(2)}) copy-start(s32[3,256]{1,0:T(4,128)} %receivers.17) | copy-start | bytes 9220
  5.9 67.9 %copy-start.2 = (s32[16]{0:T(128)S(1)}, s32[16]{0:T(128)}, u32[]{:S(2)}) copy-start(s32[16]{0:T(128)} %checkpoints.15) | copy-start | bytes 196
  6.0 18.6 %collective-permute-start.1 = (f32[6,4,2,8,128]{4,3,2,1,0:T(8,128)S(1)}, f32[6,4,2,8,128]{4,3,2,1,0:T(8,128)S(1)}, u32[]{:S(2)}, u32[]{:S(2)}) collective-permute-start(f32[6,4,2,8,128]{4,3,2,1,0:T(8,128)S(1)} %get-tuple-element.104), channel_id=1, source_target_pairs={{0,0},{1,1},{2,32},{3,33},{4,4},{5,5},{6,36},{7,37},{8,8},{9,9},{1... | collective-permute-start | bytes 589832 | tf_op jit(solution)/shard_map/ppermute | solution.py:65
  15.1 17.1 %collective-permute-start.2 = (f32[6,4,2,8,128]{4,3,2,1,0:T(8,128)S(1)}, f32[6,4,2,8,128]{4,3,2,1,0:T(8,128)S(1)}, u32[]{:S(2)}, u32[]{:S(2)}) collective-permute-start(f32[6,4,2,8,128]{4,3,2,1,0:T(8,128)S(1)} %get-tuple-element.105), channel_id=1, source_target_pairs={{0,16},{1,17},{2,48},{3,49},{4,20},{5,21},{6,52},{7,53},{8,24},{9,... | collective-permute-start | bytes 589832 | tf_op jit(solution)/shard_map/ppermute | solution.py:65
  17.6 39.5 %copy-start.1 = (s32[4]{0:T(128)S(1)}, s32[4]{0:T(128)}, u32[]{:S(2)}) copy-start(s32[4]{0:T(128)} %pad_add_fusion.place) | copy-start | bytes 52
  24.2 49.6 %copy-start.3 = (s32[2]{0:T(128)S(1)}, s32[2]{0:T(128)}, u32[]{:S(2)}) copy-start(s32[2]{0:T(128)} %get-tuple-element.57.counts) | copy-start | bytes 28
  24.2 49.6 %copy-start.5 = (s32[256]{0:T(256)S(1)}, s32[256]{0:T(256)}, u32[]{:S(2)}) copy-start(s32[256]{0:T(256)} %get-tuple-element.58.mine) | copy-start | bytes 3076
  32.3 24.8 %collective-permute-start.4 = (f32[5,8,2,8,128]{4,3,2,1,0:T(8,128)S(1)}, f32[5,8,2,8,128]{4,3,2,1,0:T(8,128)S(1)}, u32[]{:S(2)}, u32[]{:S(2)}) collective-permute-start(f32[5,8,2,8,128]{4,3,2,1,0:T(8,128)S(1)} %pad_maximum_fusion.1.block), channel_id=1, source_target_pairs={{0,450},{1,451},{2,448},{3,449},{4,454},{5,455},{6,452},{7,453},{8... | collective-permute-start | bytes 983048 | tf_op jit(solution)/shard_map/ppermute | solution.py:65
  34.3 22.8 %collective-permute-start.3 = (f32[5,8,2,8,128]{4,3,2,1,0:T(8,128)S(1)}, f32[5,8,2,8,128]{4,3,2,1,0:T(8,128)S(1)}, u32[]{:S(2)}, u32[]{:S(2)}) collective-permute-start(f32[5,8,2,8,128]{4,3,2,1,0:T(8,128)S(1)} %pad_maximum_fusion.1.block), channel_id=1, source_target_pairs={{0,64},{1,65},{2,66},{3,67},{4,68},{5,69},{6,70},{7,71},{8,72},{9,... | collective-permute-start | bytes 983048 | tf_op jit(solution)/shard_map/ppermute | solution.py:65
  57.9 14.3 %collective-permute-start.5 = (f32[5,14,2,8,128]{4,3,2,1,0:T(8,128)S(1)}, f32[5,14,2,8,128]{4,3,2,1,0:T(8,128)S(1)}, u32[]{:S(2)}, u32[]{:S(2)}) collective-permute-start(f32[5,14,2,8,128]{4,3,2,1,0:T(8,128)S(1)} %get-tuple-element.61), channel_id=1, source_target_pairs={{0,61},{1,16},{2,63},{3,18},{4,49},{5,20},{6,51},{7,22},{8,53},{9,... | collective-permute-start | bytes 1720328 | tf_op jit(solution)/shard_map/ppermute | solution.py:65
  59.8 14.0 %collective-permute-start.6 = (f32[5,14,2,8,128]{4,3,2,1,0:T(8,128)S(1)}, f32[5,14,2,8,128]{4,3,2,1,0:T(8,128)S(1)}, u32[]{:S(2)}, u32[]{:S(2)}) collective-permute-start(f32[5,14,2,8,128]{4,3,2,1,0:T(8,128)S(1)} %get-tuple-element.62), channel_id=1, source_target_pairs={{0,1},{1,0},{2,3},{3,2},{4,5},{5,4},{6,7},{7,6},{8,9},{9,8},{10,11... | collective-permute-start | bytes 1720328 | tf_op jit(solution)/shard_map/ppermute | solution.py:65
  78.5 6.9 %collective-permute-start.8 = (f32[2,8,2,8,128]{4,3,2,1,0:T(8,128)S(1)}, f32[2,8,2,8,128]{4,3,2,1,0:T(8,128)S(1)}, u32[]{:S(2)}, u32[]{:S(2)}) collective-permute-start(f32[2,8,2,8,128]{4,3,2,1,0:T(8,128)S(1)} %get-tuple-element.65.block), channel_id=1, source_target_pairs={{0,450},{1,451},{2,448},{3,449},{4,454},{5,455},{6,452},{7,453},{8... | collective-permute-start | bytes 393224 | tf_op jit(solution)/shard_map/ppermute | solution.py:65
  80.4 8.1 %collective-permute-start.7 = (f32[2,8,2,8,128]{4,3,2,1,0:T(8,128)S(1)}, f32[2,8,2,8,128]{4,3,2,1,0:T(8,128)S(1)}, u32[]{:S(2)}, u32[]{:S(2)}) collective-permute-start(f32[2,8,2,8,128]{4,3,2,1,0:T(8,128)S(1)} %get-tuple-element.65.block), channel_id=1, source_target_pairs={{0,64},{1,65},{2,66},{3,67},{4,68},{5,69},{6,70},{7,71},{8,72},{9,... | collective-permute-start | bytes 393224 | tf_op jit(solution)/shard_map/ppermute | solution.py:65
  89.1 9.8 %collective-permute-start.9 = (f32[2,14,2,8,128]{4,3,2,1,0:T(8,128)S(1)}, f32[2,14,2,8,128]{4,3,2,1,0:T(8,128)S(1)}, u32[]{:S(2)}, u32[]{:S(2)}) collective-permute-start(f32[2,14,2,8,128]{4,3,2,1,0:T(8,128)S(1)} %get-tuple-element.67), channel_id=1, source_target_pairs={{0,61},{1,16},{2,63},{3,18},{4,49},{5,20},{6,51},{7,22},{8,53},{9,... | collective-permute-start | bytes 688136 | tf_op jit(solution)/shard_map/ppermute | solution.py:65
  91.1 8.9 %collective-permute-start.10 = (f32[2,14,2,8,128]{4,3,2,1,0:T(8,128)S(1)}, f32[2,14,2,8,128]{4,3,2,1,0:T(8,128)S(1)}, u32[]{:S(2)}, u32[]{:S(2)}) collective-permute-start(f32[2,14,2,8,128]{4,3,2,1,0:T(8,128)S(1)} %get-tuple-element.68), channel_id=1, source_target_pairs={{0,1},{1,0},{2,3},{3,2},{4,5},{5,4},{6,7},{7,6},{8,9},{9,8},{10,11... | collective-permute-start | bytes 688136 | tf_op jit(solution)/shard_map/ppermute | solution.py:65
  103.8 6.9 %collective-permute-start.12 = (f32[2,8,2,8,128]{4,3,2,1,0:T(8,128)S(1)}, f32[2,8,2,8,128]{4,3,2,1,0:T(8,128)S(1)}, u32[]{:S(2)}, u32[]{:S(2)}) collective-permute-start(f32[2,8,2,8,128]{4,3,2,1,0:T(8,128)S(1)} %get-tuple-element.70.block), channel_id=1, source_target_pairs={{0,450},{1,451},{2,448},{3,449},{4,454},{5,455},{6,452},{7,453},{8... | collective-permute-start | bytes 393224 | tf_op jit(solution)/shard_map/ppermute | solution.py:65
  106.4 8.6 %collective-permute-start.11 = (f32[2,8,2,8,128]{4,3,2,1,0:T(8,128)S(1)}, f32[2,8,2,8,128]{4,3,2,1,0:T(8,128)S(1)}, u32[]{:S(2)}, u32[]{:S(2)}) collective-permute-start(f32[2,8,2,8,128]{4,3,2,1,0:T(8,128)S(1)} %get-tuple-element.70.block), channel_id=1, source_target_pairs={{0,64},{1,65},{2,66},{3,67},{4,68},{5,69},{6,70},{7,71},{8,72},{9,... | collective-permute-start | bytes 393224 | tf_op jit(solution)/shard_map/ppermute | solution.py:65
  115.6 7.3 %collective-permute-start.13 = (f32[2,14,2,8,128]{4,3,2,1,0:T(8,128)S(1)}, f32[2,14,2,8,128]{4,3,2,1,0:T(8,128)S(1)}, u32[]{:S(2)}, u32[]{:S(2)}) collective-permute-start(f32[2,14,2,8,128]{4,3,2,1,0:T(8,128)S(1)} %get-tuple-element.72), channel_id=1, source_target_pairs={{0,61},{1,16},{2,63},{3,18},{4,49},{5,20},{6,51},{7,22},{8,53},{9,... | collective-permute-start | bytes 688136 | tf_op jit(solution)/shard_map/ppermute | solution.py:65
  118.6 4.3 %collective-permute-start.14 = (f32[2,14,2,8,128]{4,3,2,1,0:T(8,128)S(1)}, f32[2,14,2,8,128]{4,3,2,1,0:T(8,128)S(1)}, u32[]{:S(2)}, u32[]{:S(2)}) collective-permute-start(f32[2,14,2,8,128]{4,3,2,1,0:T(8,128)S(1)} %get-tuple-element.73), channel_id=1, source_target_pairs={{0,1},{1,0},{2,3},{3,2},{4,5},{5,4},{6,7},{7,6},{8,9},{9,8},{10,11... | collective-permute-start | bytes 688136 | tf_op jit(solution)/shard_map/ppermute | solution.py:65
  126.8 42.8 %copy-start.4 = (s32[256]{0:T(256)S(1)}, s32[256]{0:T(256)}, u32[]{:S(2)}) copy-start(s32[256]{0:T(256)} %get-tuple-element.56.near) | copy-start | bytes 3076
  126.8 6.9 %collective-permute-start.16 = (f32[2,8,2,8,128]{4,3,2,1,0:T(8,128)S(1)}, f32[2,8,2,8,128]{4,3,2,1,0:T(8,128)S(1)}, u32[]{:S(2)}, u32[]{:S(2)}) collective-permute-start(f32[2,8,2,8,128]{4,3,2,1,0:T(8,128)S(1)} %get-tuple-element.75.block), channel_id=1, source_target_pairs={{0,450},{1,451},{2,448},{3,449},{4,454},{5,455},{6,452},{7,453},{8... | collective-permute-start | bytes 393224 | tf_op jit(solution)/shard_map/ppermute | solution.py:65
  128.7 8.3 %collective-permute-start.15 = (f32[2,8,2,8,128]{4,3,2,1,0:T(8,128)S(1)}, f32[2,8,2,8,128]{4,3,2,1,0:T(8,128)S(1)}, u32[]{:S(2)}, u32[]{:S(2)}) collective-permute-start(f32[2,8,2,8,128]{4,3,2,1,0:T(8,128)S(1)} %get-tuple-element.75.block), channel_id=1, source_target_pairs={{0,64},{1,65},{2,66},{3,67},{4,68},{5,69},{6,70},{7,71},{8,72},{9,... | collective-permute-start | bytes 393224 | tf_op jit(solution)/shard_map/ppermute | solution.py:65
  137.7 10.9 %collective-permute-start.17 = (f32[2,14,2,8,128]{4,3,2,1,0:T(8,128)S(1)}, f32[2,14,2,8,128]{4,3,2,1,0:T(8,128)S(1)}, u32[]{:S(2)}, u32[]{:S(2)}) collective-permute-start(f32[2,14,2,8,128]{4,3,2,1,0:T(8,128)S(1)} %get-tuple-element.77), channel_id=1, source_target_pairs={{0,61},{1,16},{2,63},{3,18},{4,49},{5,20},{6,51},{7,22},{8,53},{9,... | collective-permute-start | bytes 688136 | tf_op jit(solution)/shard_map/ppermute | solution.py:65
  144.9 3.7 %collective-permute-start.18 = (f32[2,14,2,8,128]{4,3,2,1,0:T(8,128)S(1)}, f32[2,14,2,8,128]{4,3,2,1,0:T(8,128)S(1)}, u32[]{:S(2)}, u32[]{:S(2)}) collective-permute-start(f32[2,14,2,8,128]{4,3,2,1,0:T(8,128)S(1)} %get-tuple-element.78), channel_id=1, source_target_pairs={{0,1},{1,0},{2,3},{3,2},{4,5},{5,4},{6,7},{7,6},{8,9},{9,8},{10,11... | collective-permute-start | bytes 688136 | tf_op jit(solution)/shard_map/ppermute | solution.py:65
  151.5 7.1 %collective-permute-start.19 = (f32[16,256]{1,0:T(8,128)S(1)}, f32[16,256]{1,0:T(8,128)S(1)}, u32[]{:S(2)}, u32[]{:S(2)}) collective-permute-start(f32[16,256]{1,0:T(8,128)S(1)} %get-tuple-element.80), channel_id=1, source_target_pairs={{0,64},{1,65},{2,66},{3,67},{4,68},{5,69},{6,70},{7,71},{8,72},{9,... | collective-permute-start | bytes 49160 | tf_op jit(solution)/shard_map/ppermute | solution.py:65
  153.5 6.6 %collective-permute-start.20 = (f32[16,256]{1,0:T(8,128)S(1)}, f32[16,256]{1,0:T(8,128)S(1)}, u32[]{:S(2)}, u32[]{:S(2)}) collective-permute-start(f32[16,256]{1,0:T(8,128)S(1)} %get-tuple-element.80), channel_id=1, source_target_pairs={{0,450},{1,451},{2,448},{3,449},{4,454},{5,455},{6,452},{7,453},{8... | collective-permute-start | bytes 49160 | tf_op jit(solution)/shard_map/ppermute | solution.py:65
  160.0 8.3 %collective-permute-start.21 = (f32[16,256]{1,0:T(8,128)S(1)}, f32[16,256]{1,0:T(8,128)S(1)}, u32[]{:S(2)}, u32[]{:S(2)}) collective-permute-start(f32[16,256]{1,0:T(8,128)S(1)} %compare_select_fusion.4), channel_id=1, source_target_pairs={{0,61},{1,16},{2,63},{3,18},{4,49},{5,20},{6,51},{7,22},{8,53},{9,... | collective-permute-start | bytes 49160 | tf_op jit(solution)/shard_map/ppermute | solution.py:65
  166.4 3.1 %collective-permute-start.22 = (f32[16,256]{1,0:T(8,128)S(1)}, f32[16,256]{1,0:T(8,128)S(1)}, u32[]{:S(2)}, u32[]{:S(2)}) collective-permute-start(f32[16,256]{1,0:T(8,128)S(1)} %compare_select_fusion.4), channel_id=1, source_target_pairs={{0,1},{1,0},{2,3},{3,2},{4,5},{5,4},{6,7},{7,6},{8,9},{9,8},{10,11... | collective-permute-start | bytes 49160 | tf_op jit(solution)/shard_map/ppermute | solution.py:65
  172.8 8.5 %collective-permute-start.24 = (f32[2,9,2,8,128]{4,3,2,1,0:T(8,128)S(1)}, f32[2,9,2,8,128]{4,3,2,1,0:T(8,128)S(1)}, u32[]{:S(2)}, u32[]{:S(2)}) collective-permute-start(f32[2,9,2,8,128]{4,3,2,1,0:T(8,128)S(1)} %get-tuple-element.81.block), channel_id=1, source_target_pairs={{0,450},{1,451},{2,448},{3,449},{4,454},{5,455},{6,452},{7,453},{8... | collective-permute-start | bytes 442376 | tf_op jit(solution)/shard_map/ppermute | solution.py:65
  177.8 8.8 %collective-permute-start.23 = (f32[2,9,2,8,128]{4,3,2,1,0:T(8,128)S(1)}, f32[2,9,2,8,128]{4,3,2,1,0:T(8,128)S(1)}, u32[]{:S(2)}, u32[]{:S(2)}) collective-permute-start(f32[2,9,2,8,128]{4,3,2,1,0:T(8,128)S(1)} %get-tuple-element.81.block), channel_id=1, source_target_pairs={{0,64},{1,65},{2,66},{3,67},{4,68},{5,69},{6,70},{7,71},{8,72},{9,... | collective-permute-start | bytes 442376 | tf_op jit(solution)/shard_map/ppermute | solution.py:65
  187.3 18.1 %collective-permute-start.25 = (f32[2,15,2,8,128]{4,3,2,1,0:T(8,128)S(1)}, f32[2,15,2,8,128]{4,3,2,1,0:T(8,128)S(1)}, u32[]{:S(2)}, u32[]{:S(2)}) collective-permute-start(f32[2,15,2,8,128]{4,3,2,1,0:T(8,128)S(1)} %get-tuple-element.83), channel_id=1, source_target_pairs={{0,61},{1,16},{2,63},{3,18},{4,49},{5,20},{6,51},{7,22},{8,53},{9,... | collective-permute-start | bytes 737288 | tf_op jit(solution)/shard_map/ppermute | solution.py:65
  192.9 12.4 %collective-permute-start.26 = (f32[2,15,2,8,128]{4,3,2,1,0:T(8,128)S(1)}, f32[2,15,2,8,128]{4,3,2,1,0:T(8,128)S(1)}, u32[]{:S(2)}, u32[]{:S(2)}) collective-permute-start(f32[2,15,2,8,128]{4,3,2,1,0:T(8,128)S(1)} %get-tuple-element.84), channel_id=1, source_target_pairs={{0,1},{1,0},{2,3},{3,2},{4,5},{5,4},{6,7},{7,6},{8,9},{9,8},{10,11... | collective-permute-start | bytes 737288 | tf_op jit(solution)/shard_map/ppermute | solution.py:65
  194.9 10.5 %collective-permute-start.27 = (f32[2,2,8,128]{3,2,1,0:T(8,128)S(1)}, f32[2,2,8,128]{3,2,1,0:T(8,128)S(1)}, u32[]{:S(2)}, u32[]{:S(2)}) collective-permute-start(f32[2,2,8,128]{3,2,1,0:T(8,128)S(1)} %slice_bitcast_fusion.3), channel_id=1, source_target_pairs={{0,48},{1,49},{2,50},{3,51},{4,52},{5,53},{6,54},{7,55},{8,56},{9,... | collective-permute-start | bytes 49160 | tf_op jit(solution)/shard_map/ppermute | solution.py:65
  208.6 7.0 %collective-permute-start.29 = (f32[2,9,2,8,128]{4,3,2,1,0:T(8,128)S(1)}, f32[2,9,2,8,128]{4,3,2,1,0:T(8,128)S(1)}, u32[]{:S(2)}, u32[]{:S(2)}) collective-permute-start(f32[2,9,2,8,128]{4,3,2,1,0:T(8,128)S(1)} %get-tuple-element.86.block), channel_id=1, source_target_pairs={{0,450},{1,451},{2,448},{3,449},{4,454},{5,455},{6,452},{7,453},{8... | collective-permute-start | bytes 442376 | tf_op jit(solution)/shard_map/ppermute | solution.py:65
  210.5 8.2 %collective-permute-start.28 = (f32[2,9,2,8,128]{4,3,2,1,0:T(8,128)S(1)}, f32[2,9,2,8,128]{4,3,2,1,0:T(8,128)S(1)}, u32[]{:S(2)}, u32[]{:S(2)}) collective-permute-start(f32[2,9,2,8,128]{4,3,2,1,0:T(8,128)S(1)} %get-tuple-element.86.block), channel_id=1, source_target_pairs={{0,64},{1,65},{2,66},{3,67},{4,68},{5,69},{6,70},{7,71},{8,72},{9,... | collective-permute-start | bytes 442376 | tf_op jit(solution)/shard_map/ppermute | solution.py:65
  219.4 13.3 %collective-permute-start.30 = (f32[2,15,2,8,128]{4,3,2,1,0:T(8,128)S(1)}, f32[2,15,2,8,128]{4,3,2,1,0:T(8,128)S(1)}, u32[]{:S(2)}, u32[]{:S(2)}) collective-permute-start(f32[2,15,2,8,128]{4,3,2,1,0:T(8,128)S(1)} %get-tuple-element.88), channel_id=1, source_target_pairs={{0,61},{1,16},{2,63},{3,18},{4,49},{5,20},{6,51},{7,22},{8,53},{9,... | collective-permute-start | bytes 737288 | tf_op jit(solution)/shard_map/ppermute | solution.py:65
  222.7 10.0 %collective-permute-start.31 = (f32[2,15,2,8,128]{4,3,2,1,0:T(8,128)S(1)}, f32[2,15,2,8,128]{4,3,2,1,0:T(8,128)S(1)}, u32[]{:S(2)}, u32[]{:S(2)}) collective-permute-start(f32[2,15,2,8,128]{4,3,2,1,0:T(8,128)S(1)} %get-tuple-element.89), channel_id=1, source_target_pairs={{0,1},{1,0},{2,3},{3,2},{4,5},{5,4},{6,7},{7,6},{8,9},{9,8},{10,11... | collective-permute-start | bytes 737288 | tf_op jit(solution)/shard_map/ppermute | solution.py:65
  226.1 6.6 %collective-permute-start.32 = (f32[2,2,8,128]{3,2,1,0:T(8,128)S(1)}, f32[2,2,8,128]{3,2,1,0:T(8,128)S(1)}, u32[]{:S(2)}, u32[]{:S(2)}) collective-permute-start(f32[2,2,8,128]{3,2,1,0:T(8,128)S(1)} %slice_bitcast_fusion.2), channel_id=1, source_target_pairs={{0,28},{1,29},{2,30},{3,31},{4,16},{5,17},{6,18},{7,19},{8,20},{9,... | collective-permute-start | bytes 49160 | tf_op jit(solution)/shard_map/ppermute | solution.py:65
  235.8 7.0 %collective-permute-start.34 = (f32[2,9,2,8,128]{4,3,2,1,0:T(8,128)S(1)}, f32[2,9,2,8,128]{4,3,2,1,0:T(8,128)S(1)}, u32[]{:S(2)}, u32[]{:S(2)}) collective-permute-start(f32[2,9,2,8,128]{4,3,2,1,0:T(8,128)S(1)} %get-tuple-element.91.block), channel_id=1, source_target_pairs={{0,450},{1,451},{2,448},{3,449},{4,454},{5,455},{6,452},{7,453},{8... | collective-permute-start | bytes 442376 | tf_op jit(solution)/shard_map/ppermute | solution.py:65
  237.8 8.2 %collective-permute-start.33 = (f32[2,9,2,8,128]{4,3,2,1,0:T(8,128)S(1)}, f32[2,9,2,8,128]{4,3,2,1,0:T(8,128)S(1)}, u32[]{:S(2)}, u32[]{:S(2)}) collective-permute-start(f32[2,9,2,8,128]{4,3,2,1,0:T(8,128)S(1)} %get-tuple-element.91.block), channel_id=1, source_target_pairs={{0,64},{1,65},{2,66},{3,67},{4,68},{5,69},{6,70},{7,71},{8,72},{9,... | collective-permute-start | bytes 442376 | tf_op jit(solution)/shard_map/ppermute | solution.py:65
  246.7 12.7 %collective-permute-start.35 = (f32[2,15,2,8,128]{4,3,2,1,0:T(8,128)S(1)}, f32[2,15,2,8,128]{4,3,2,1,0:T(8,128)S(1)}, u32[]{:S(2)}, u32[]{:S(2)}) collective-permute-start(f32[2,15,2,8,128]{4,3,2,1,0:T(8,128)S(1)} %get-tuple-element.93), channel_id=1, source_target_pairs={{0,61},{1,16},{2,63},{3,18},{4,49},{5,20},{6,51},{7,22},{8,53},{9,... | collective-permute-start | bytes 737288 | tf_op jit(solution)/shard_map/ppermute | solution.py:65
  248.6 10.8 %collective-permute-start.36 = (f32[2,15,2,8,128]{4,3,2,1,0:T(8,128)S(1)}, f32[2,15,2,8,128]{4,3,2,1,0:T(8,128)S(1)}, u32[]{:S(2)}, u32[]{:S(2)}) collective-permute-start(f32[2,15,2,8,128]{4,3,2,1,0:T(8,128)S(1)} %get-tuple-element.94), channel_id=1, source_target_pairs={{0,1},{1,0},{2,3},{3,2},{4,5},{5,4},{6,7},{7,6},{8,9},{9,8},{10,11... | collective-permute-start | bytes 737288 | tf_op jit(solution)/shard_map/ppermute | solution.py:65
  252.9 15.5 %collective-permute-start.38 = (f32[2,2,8,128]{3,2,1,0:T(8,128)S(1)}, f32[2,2,8,128]{3,2,1,0:T(8,128)S(1)}, u32[]{:S(2)}, u32[]{:S(2)}) collective-permute-start(f32[2,2,8,128]{3,2,1,0:T(8,128)S(1)} %slice_bitcast_fusion.1), channel_id=1, source_target_pairs={{0,2},{1,3},{2,0},{3,1},{4,6},{5,7},{6,4},{7,5},{8,10},{9,11},{10,... | collective-permute-start | bytes 49160 | tf_op jit(solution)/shard_map/ppermute | solution.py:65
  261.8 29.6 %collective-permute-start.37 = (f32[2,4,2,8,128]{4,3,2,1,0:T(8,128)S(1)}, f32[2,4,2,8,128]{4,3,2,1,0:T(8,128)S(1)}, u32[]{:S(2)}, u32[]{:S(2)}) collective-permute-start(f32[2,4,2,8,128]{4,3,2,1,0:T(8,128)S(1)} %get-tuple-element.110), channel_id=1, source_target_pairs={{0,0},{1,1},{2,256},{3,257},{4,4},{5,5},{6,260},{7,261},{8,8},{9,9... | collective-permute-start | bytes 196616 | tf_op jit(solution)/shard_map/ppermute | solution.py:65
  263.8 30.6 %collective-permute-start.39 = (f32[2,4,2,8,128]{4,3,2,1,0:T(8,128)S(1)}, f32[2,4,2,8,128]{4,3,2,1,0:T(8,128)S(1)}, u32[]{:S(2)}, u32[]{:S(2)}) collective-permute-start(f32[2,4,2,8,128]{4,3,2,1,0:T(8,128)S(1)} %get-tuple-element.111), channel_id=1, source_target_pairs={{0,16},{1,17},{2,272},{3,273},{4,20},{5,21},{6,276},{7,277},{8,24}... | collective-permute-start | bytes 196616 | tf_op jit(solution)/shard_map/ppermute | solution.py:65
  294.6 7.1 %collective-permute-start.41 = (f32[2,2,8,128]{3,2,1,0:T(8,128)S(1)}, f32[2,2,8,128]{3,2,1,0:T(8,128)S(1)}, u32[]{:S(2)}, u32[]{:S(2)}) collective-permute-start(f32[2,2,8,128]{3,2,1,0:T(8,128)S(1)} %compare_select_fusion.1), channel_id=1, source_target_pairs={{0,8},{1,9},{2,10},{3,11},{4,12},{5,13},{6,14},{7,15},{8,0},{9,1},... | collective-permute-start | bytes 49160 | tf_op jit(solution)/shard_map/ppermute | solution.py:65
  296.6 5.7 %collective-permute-start.40 = (f32[3,4,2,8,128]{4,3,1,0,2:T(8,128)S(1)}, f32[3,4,2,8,128]{4,3,1,0,2:T(8,128)S(1)}, u32[]{:S(2)}, u32[]{:S(2)}) collective-permute-start(f32[3,4,2,8,128]{4,3,1,0,2:T(8,128)S(1)} %pad_maximum_fusion.2), channel_id=1, source_target_pairs={{0,1},{1,0},{2,3},{3,2},{4,5},{5,4},{6,7},{7,6},{8,9},{9,8},{10,11... | collective-permute-start | bytes 294920 | tf_op jit(solution)/shard_map/ppermute | solution.py:65
